TPU v7x, 32 devices: a whole 2x2x4 slice. The times are simulated.
32 devices in a mesh: depth: 32 (over z, y, x, core), xs: 1.
Axes of the slice: x: 2, y: 2, z: 4, core: 2. Of those that a mesh axis runs over, the one named last changes fastest.
Arguments:
- density: bfloat16 [512, 128, 512], P('depth', None, 'xs'), may hold values from 0.049804688 to 2
- clip_flags: int32 [512, 8, 4], P('depth', None, 'xs'), may hold values 0 or 1
- band_offset: int32 [1], replicated, may hold values from 0 to 3071
- order: int32 [32], replicated, may hold values from 0 to 31, as said below
- ambient: float32 [3], replicated, may hold values from 0.1 to 0.6
- diffuse: float32 [3], replicated, may hold values from 1 to 3
Outputs:
- image: float32 [4, 128, 512], P(None, 'depth', 'xs')
Inputs may be any that keep to these rules, and one draw needn't show every extreme that they name: The front-to-back order of a binary space partition of the slabs: order[k] = k XOR m for one m of 0 to 31.
All inputs are finite; a program needn't handle non-finite values. No bound on the sum of `clip_flags` on one device may be relied on, other than what follows from the above.
Results may differ from a plain program's by a relative error of at most 0.0003.
Values sent between devices are 32-bit elements; how exact they have to be, the bound alone decides.
No kernel may reach another device: no remote copies, remote signals or barrier semaphores. Data moves between devices by JAX's collectives and lax.ppermute only.
A program may use at most 64 MiB of HBM per device.

v0:
```python
import math

import jax
import jax.numpy as jnp
from jax import lax
from jax.sharding import PartitionSpec as P


def prefix(value, axis, join, neutral):
    count, mine = (lax.axis_size(axis), lax.axis_index(axis))
    pieces = lax.all_gather(value, axis)
    so_far = jnp.full_like(value, 0) + jnp.asarray(neutral, value.dtype)

    def lap(position, so_far):
        longer = join(so_far, pieces[position])
        return jnp.where(position < mine, longer, so_far)

    return lax.fori_loop(0, count - 1, lap, so_far)


def swapped(value, axis, distance):
    mask = 2**distance
    pairs = [(source, source ^ mask) for source in range(lax.axis_size(axis))]
    return lax.ppermute(value, axis, pairs)


def on_device(density, clip_flags, band_offset, order, ambient, diffuse):
    slices, rows, cells = density.shape
    depth_n = lax.axis_size("depth")
    xs_n = lax.axis_size("xs")
    kappa = 2.0 / (slices * depth_n)
    extinct = 2.0 / (cells * xs_n)
    blocks_r = clip_flags.shape[1]
    blocks_x = clip_flags.shape[2]
    full_flags = jnp.broadcast_to(
        clip_flags[:, :, None, :, None],
        (slices, blocks_r, rows // blocks_r, blocks_x, cells // blocks_x),
    )
    masked = density * full_flags.reshape(slices, rows, cells).astype(jnp.bfloat16)
    clipped = masked.astype(jnp.float32)
    upper = (
        lax.broadcasted_iota(jnp.int32, (cells, cells), 0)
        < lax.broadcasted_iota(jnp.int32, (cells, cells), 1)
    ).astype(jnp.bfloat16)
    local_prefix = jnp.dot(
        masked.reshape(slices * rows, cells), upper, preferred_element_type=jnp.float32
    ).reshape(slices, rows, cells)
    totals = jnp.sum(clipped, axis=2)
    nearer = prefix(totals, "xs", lambda early, late: early + late, jnp.zeros_like(totals))
    light_depth = extinct * (nearer[:, :, None] + local_prefix)
    row_pos = (band_offset[0] + jnp.arange(rows, dtype=jnp.int32)).astype(jnp.float32)
    source = 0.6 + 0.4 * jnp.cos(2.0 * math.pi * row_pos / 64.0)
    light = source[None, :, None] * jnp.exp(-light_depth)
    before = jnp.cumsum(clipped, axis=0) - clipped
    weight = -jnp.expm1(-kappa * clipped) * jnp.exp(-kappa * before)
    base = jnp.sum(clipped * weight, axis=0)
    lit = jnp.sum(clipped * light * weight, axis=0)
    colors = ambient[:, None, None] * base[None] + diffuse[:, None, None] * lit[None]
    column = jnp.sum(clipped, axis=0)
    slab_ids = jnp.arange(depth_n, dtype=jnp.int32)
    onehot = (order[:, None] == slab_ids[None, :]).astype(jnp.int32)
    ranks = jnp.sum(onehot * slab_ids[:, None], axis=0)
    my_slab = lax.axis_index("depth")
    my_rank = jnp.sum(ranks * (slab_ids == my_slab).astype(jnp.int32))
    block_rows = rows // depth_n
    levels = depth_n.bit_length() - 1
    share_c = colors
    share_d = column
    for level in range(levels):
        groups = (depth_n >> level) // 2
        paired_c = share_c.reshape(3, groups, 2, block_rows, cells)
        paired_d = share_d.reshape(groups, 2, block_rows, cells)
        lower = my_slab >> level & 1 == 0
        keep_c = jnp.where(lower, paired_c[:, :, 0], paired_c[:, :, 1])
        give_c = jnp.where(lower, paired_c[:, :, 1], paired_c[:, :, 0])
        keep_d = jnp.where(lower, paired_d[:, 0], paired_d[:, 1])
        give_d = jnp.where(lower, paired_d[:, 1], paired_d[:, 0])
        recv_c, recv_d = swapped((give_c, give_d), "depth", level)
        partner_front = my_rank >> level & 1 == 1
        front_c = jnp.where(partner_front, recv_c, keep_c)
        back_c = jnp.where(partner_front, keep_c, recv_c)
        front_d = jnp.where(partner_front, recv_d, keep_d)
        merged_c = front_c + back_c * jnp.exp(-kappa * front_d)[None]
        merged_d = keep_d + recv_d
        share_c = merged_c.reshape(3, groups * block_rows, cells)
        share_d = merged_d.reshape(groups * block_rows, cells)
    alpha = -jnp.expm1(-kappa * share_d)
    image = jnp.concatenate([share_c, alpha[None]], axis=0)
    return image


def solution(mesh):
    return jax.shard_map(
        on_device,
        mesh=mesh,
        in_specs=(P("depth", None, "xs"), P("depth", None, "xs"), P(), P(), P(), P()),
        out_specs=P(None, "depth", "xs"),
        check_vma=False,
    )
```

profile of v0, /device:TPU:0, one launch (start us, length us, event | category | flops | bytes accessed | tf_op | source)
XLA Modules:
  0.0 49.1 jit_solution(8118374924605777389)
XLA Ops:
  0.0 0.7 %convert_element_type.20 = bf16[16,8,4]{0,2,1:T(4,128)(2,1)S(1)} convert(s32[16,8,4]{0,2,1:T(4,128)} %param.7) | non-fusion elementwise | flops 512 | bytes 3072 | tf_op jit(solution)/shard_map/convert_element_type | solution.py:39
  0.7 0.1 copy.41
  0.9 0.6 %broadcast_in_dim.2 = bf16[16,8,16,4,128]{4,3,2,1,0:T(4,128)(2,1)S(1)} broadcast(bf16[16,8,4]{2,1,0:T(8,128)(2,1)S(1)} %copy.41), dimensions={0,1,3} | broadcast | bytes 2098176 | tf_op jit(solution)/shard_map/broadcast_in_dim | solution.py:35
  1.5 2.2 %convert_element_type.21 = bf16[16,128,512]{2,1,0:T(8,128)(2,1)} reshape(bf16[16,8,16,4,128]{4,3,2,1,0:T(4,128)(2,1)S(1)} %broadcast_in_dim.2) | data formatting | bytes 4194304 | tf_op jit(solution)/shard_map/convert_element_type | solution.py:39
  3.7 2.9 %mul.172 = bf16[16,128,512]{2,1,0:T(8,128)(2,1)S(1)} multiply(bf16[16,128,512]{2,1,0:T(8,128)(2,1)} %param.6, bf16[16,128,512]{2,1,0:T(8,128)(2,1)} %convert_element_type.21) | non-fusion elementwise | flops 1048576 | bytes 6291456 | tf_op jit(solution)/shard_map/mul | solution.py:39
  6.6 4.6 %fusion.7 = (f32[128,512]{1,0:T(8,128)S(1)}, f32[128,512]{1,0:T(8,128)S(1)}, f32[16,128,512]{2,1,0:T(8,128)}) fusion(bf16[16,128,512]{2,1,0:T(8,128)(2,1)S(1)} %mul.172), kind=kOutput, calls=%fused_computation.12 | output fusion | flops 26083328 | bytes 6815744 | tf_op jit(solution)/shard_map/jit(cumsum)/reduce_window_sum | solution.py:54
  11.4 0.5 %collective-permute-start.1 = (f32[16,4,512]{2,1,0:T(4,128)S(1)}, f32[16,4,512]{2,1,0:T(4,128)S(1)}, u32[]{:S(2)}, u32[]{:S(2)}) collective-permute-start(f32[16,4,512]{2,1,0:T(4,128)S(1)} %fusion.19), channel_id=1, source_target_pairs={{0,1},{1,0},{2,3},{3,2},{4,5},{5,4},{6,7},{7,6},{8,9},{9,8},{10,11... | collective-permute-start | bytes 393224 | tf_op jit(solution)/shard_map/ppermute | solution.py:24
  12.6 0.1 select_reduce_fusion
  12.7 0.6 %fusion.49 = s32[]{:T(128)} fusion(s32[32]{0:T(128)S(1)} %select_reduce_fusion, s32[]{:T(128)S(6)} %axis_index.12), kind=kLoop, calls=%fused_computation.93 | loop fusion | flops 95 | bytes 136 | tf_op jit(solution)/shard_map/reduce_sum | solution.py:64
  14.0 4.1 %fusion.9 = f32[128,512]{1,0:T(8,128)S(1)} fusion(f32[16,128,512]{2,1,0:T(8,128)} %get-tuple-element.17, bf16[16,128,512]{2,1,0:T(8,128)(2,1)S(1)} %mul.172, f32[128]{0:T(128)S(1)} %multiply_add_fusion.1), kind=kOutput, calls=%fused_computation.14 | convolution fusion | flops 1081278464 | bytes 6554112 | tf_op jit(solution)/shard_map/dot_general | solution.py:45
  18.1 0.1 mul.189
  18.2 0.1 mul.177
  18.3 0.2 multiply_add_fusion
  18.6 0.1 fusion.21
  18.7 2.6 %collective-permute-start.3 = (f32[8,4,512]{2,1,0:T(4,128)S(1)}, f32[8,4,512]{2,1,0:T(4,128)S(1)}, u32[]{:S(2)}, u32[]{:S(2)}) collective-permute-start(f32[8,4,512]{2,1,0:T(4,128)S(1)} %fusion.25), channel_id=1, source_target_pairs={{0,2},{1,3},{2,0},{3,1},{4,6},{5,7},{6,4},{7,5},{8,10},{9,11},{10,... | collective-permute-start | bytes 196616 | tf_op jit(solution)/shard_map/ppermute | solution.py:24
  21.3 0.1 select_bitcast_fusion
  21.4 0.3 collective-permute-start
  22.3 1.7 %collective-permute-done.3 = f32[8,4,512]{2,1,0:T(4,128)S(1)} collective-permute-done((f32[8,4,512]{2,1,0:T(4,128)S(1)}, f32[8,4,512]{2,1,0:T(4,128)S(1)}, u32[]{:S(2)}, u32[]{:S(2)}) %collective-permute-start.3) | collective-permute-done | bytes 65568 | tf_op jit(solution)/shard_map/ppermute | solution.py:24
  24.1 1.8 %collective-permute-start.5 = (f32[4,4,512]{2,1,0:T(4,128)S(1)}, f32[4,4,512]{2,1,0:T(4,128)S(1)}, u32[]{:S(2)}, u32[]{:S(2)}) collective-permute-start(f32[4,4,512]{2,1,0:T(4,128)S(1)} %fusion.32), channel_id=1, source_target_pairs={{0,4},{1,5},{2,6},{3,7},{4,0},{5,1},{6,2},{7,3},{8,12},{9,13},{10,... | collective-permute-start | bytes 98312 | tf_op jit(solution)/shard_map/ppermute | solution.py:24
  27.9 0.2 collective-permute-done.5
  28.1 0.2 fusion.14
  28.4 1.8 %collective-permute-start.2 = (f32[3,8,4,512]{3,2,1,0:T(4,128)S(1)}, f32[3,8,4,512]{3,2,1,0:T(4,128)S(1)}, u32[]{:S(2)}, u32[]{:S(2)}) collective-permute-start(f32[3,8,4,512]{3,2,1,0:T(4,128)S(1)} %fusion.16), channel_id=1, source_target_pairs={{0,2},{1,3},{2,0},{3,1},{4,6},{5,7},{6,4},{7,5},{8,10},{9,11},{10,... | collective-permute-start | bytes 589832 | tf_op jit(solution)/shard_map/ppermute | solution.py:24
  30.2 1.6 %collective-permute-start.7 = (f32[2,4,512]{2,1,0:T(4,128)S(1)}, f32[2,4,512]{2,1,0:T(4,128)S(1)}, u32[]{:S(2)}, u32[]{:S(2)}) collective-permute-start(f32[2,4,512]{2,1,0:T(4,128)S(1)} %select_bitcast_fusion.1), channel_id=1, source_target_pairs={{0,8},{1,9},{2,10},{3,11},{4,12},{5,13},{6,14},{7,15},{8,0},{9,1},... | collective-permute-start | bytes 49160 | tf_op jit(solution)/shard_map/ppermute | solution.py:24
  31.8 2.7 %collective-permute-done.2 = f32[3,8,4,512]{3,2,1,0:T(4,128)S(1)} collective-permute-done((f32[3,8,4,512]{3,2,1,0:T(4,128)S(1)}, f32[3,8,4,512]{3,2,1,0:T(4,128)S(1)}, u32[]{:S(2)}, u32[]{:S(2)}) %collective-permute-start.2) | collective-permute-done | bytes 196640 | tf_op jit(solution)/shard_map/ppermute | solution.py:24
  34.5 0.1 fusion.17
  34.6 1.4 %collective-permute-start.4 = (f32[3,4,4,512]{3,2,1,0:T(4,128)S(1)}, f32[3,4,4,512]{3,2,1,0:T(4,128)S(1)}, u32[]{:S(2)}, u32[]{:S(2)}) collective-permute-start(f32[3,4,4,512]{3,2,1,0:T(4,128)S(1)} %fusion.22), channel_id=1, source_target_pairs={{0,4},{1,5},{2,6},{3,7},{4,0},{5,1},{6,2},{7,3},{8,12},{9,13},{10,... | collective-permute-start | bytes 294920 | tf_op jit(solution)/shard_map/ppermute | solution.py:24
  36.1 3.2 %collective-permute-done.4 = f32[3,4,4,512]{3,2,1,0:T(4,128)S(1)} collective-permute-done((f32[3,4,4,512]{3,2,1,0:T(4,128)S(1)}, f32[3,4,4,512]{3,2,1,0:T(4,128)S(1)}, u32[]{:S(2)}, u32[]{:S(2)}) %collective-permute-start.4) | collective-permute-done | bytes 98336 | tf_op jit(solution)/shard_map/ppermute | solution.py:24
  39.4 1.6 %collective-permute-start.6 = (f32[3,2,4,512]{3,2,1,0:T(4,128)S(1)}, f32[3,2,4,512]{3,2,1,0:T(4,128)S(1)}, u32[]{:S(2)}, u32[]{:S(2)}) collective-permute-start(f32[3,2,4,512]{3,2,1,0:T(4,128)S(1)} %fusion.28), channel_id=1, source_target_pairs={{0,8},{1,9},{2,10},{3,11},{4,12},{5,13},{6,14},{7,15},{8,0},{9,1},... | collective-permute-start | bytes 147464 | tf_op jit(solution)/shard_map/ppermute | solution.py:24
  41.0 2.6 %collective-permute-start.9 = (f32[1,4,512]{2,1,0:T(4,128)S(1)}, f32[1,4,512]{2,1,0:T(4,128)S(1)}, u32[]{:S(2)}, u32[]{:S(2)}) collective-permute-start(f32[1,4,512]{2,1,0:T(4,128)S(1)} %select_bitcast_fusion.2), channel_id=1, source_target_pairs={{0,16},{1,17},{2,18},{3,19},{4,20},{5,21},{6,22},{7,23},{8,24},{9,... | collective-permute-start | bytes 24584 | tf_op jit(solution)/shard_map/ppermute | solution.py:24
  43.6 2.6 %collective-permute-start.8 = (f32[3,1,4,512]{3,2,0,1:T(4,128)S(1)}, f32[3,1,4,512]{3,2,0,1:T(4,128)S(1)}, u32[]{:S(2)}, u32[]{:S(2)}) collective-permute-start(f32[3,1,4,512]{3,2,0,1:T(4,128)S(1)} %fusion.35), channel_id=1, source_target_pairs={{0,16},{1,17},{2,18},{3,19},{4,20},{5,21},{6,22},{7,23},{8,24},{9,... | collective-permute-start | bytes 73736 | tf_op jit(solution)/shard_map/ppermute | solution.py:24
  46.2 2.2 %collective-permute-done.8 = f32[3,1,4,512]{3,2,0,1:T(4,128)S(1)} collective-permute-done((f32[3,1,4,512]{3,2,0,1:T(4,128)S(1)}, f32[3,1,4,512]{3,2,0,1:T(4,128)S(1)}, u32[]{:S(2)}, u32[]{:S(2)}) %collective-permute-start.8) | collective-permute-done | bytes 24608 | tf_op jit(solution)/shard_map/ppermute | solution.py:24
  48.5 0.6 %pad_maximum_fusion = f32[4,4,512]{2,1,0:T(4,128)} fusion(f32[1,4,512]{2,1,0:T(4,128)S(1)} %get-tuple-element.16, f32[3,4,512]{2,1,0:T(4,128)S(1)} %fusion.37), kind=kLoop, calls=%fused_computation.56 | loop fusion | flops 8192 | bytes 65536 | tf_op jit(solution)/shard_map/concatenate | solution.py:88
  (29 shorter events, 0.5 us)
Async XLA Ops:
  6.6 6.0 %copy-start.2 = (s32[32]{0:T(128)S(1)}, s32[32]{0:T(128)}, u32[]{:S(2)}) copy-start(s32[32]{0:T(128)} %param.9) | copy-start | bytes 388
  11.4 7.2 %collective-permute-start.1 = (f32[16,4,512]{2,1,0:T(4,128)S(1)}, f32[16,4,512]{2,1,0:T(4,128)S(1)}, u32[]{:S(2)}, u32[]{:S(2)}) collective-permute-start(f32[16,4,512]{2,1,0:T(4,128)S(1)} %fusion.19), channel_id=1, source_target_pairs={{0,1},{1,0},{2,3},{3,2},{4,5},{5,4},{6,7},{7,6},{8,9},{9,8},{10,11... | collective-permute-start | bytes 393224 | tf_op jit(solution)/shard_map/ppermute | solution.py:24
  14.0 4.3 %copy-start = (f32[3]{0:T(128)S(1)}, f32[3]{0:T(128)}, u32[]{:S(2)}) copy-start(f32[3]{0:T(128)} %param.11) | copy-start | bytes 40
  14.0 4.3 %copy-start.1 = (f32[3]{0:T(128)S(1)}, f32[3]{0:T(128)}, u32[]{:S(2)}) copy-start(f32[3]{0:T(128)} %param.10) | copy-start | bytes 40
  18.7 5.3 %collective-permute-start.3 = (f32[8,4,512]{2,1,0:T(4,128)S(1)}, f32[8,4,512]{2,1,0:T(4,128)S(1)}, u32[]{:S(2)}, u32[]{:S(2)}) collective-permute-start(f32[8,4,512]{2,1,0:T(4,128)S(1)} %fusion.25), channel_id=1, source_target_pairs={{0,2},{1,3},{2,0},{3,1},{4,6},{5,7},{6,4},{7,5},{8,10},{9,11},{10,... | collective-permute-start | bytes 196616 | tf_op jit(solution)/shard_map/ppermute | solution.py:24
  21.4 6.7 %collective-permute-start = (f32[3,16,4,512]{3,2,1,0:T(4,128)S(1)}, f32[3,16,4,512]{3,2,1,0:T(4,128)S(1)}, u32[]{:S(2)}, u32[]{:S(2)}) collective-permute-start(f32[3,16,4,512]{3,2,1,0:T(4,128)S(1)} %select_bitcast_fusion), channel_id=1, source_target_pairs={{0,1},{1,0},{2,3},{3,2},{4,5},{5,4},{6,7},{7,6},{8,9},{9,8},{10,11... | collective-permute-start | bytes 1179656 | tf_op jit(solution)/shard_map/ppermute | solution.py:24
  24.1 4.0 %collective-permute-start.5 = (f32[4,4,512]{2,1,0:T(4,128)S(1)}, f32[4,4,512]{2,1,0:T(4,128)S(1)}, u32[]{:S(2)}, u32[]{:S(2)}) collective-permute-start(f32[4,4,512]{2,1,0:T(4,128)S(1)} %fusion.32), channel_id=1, source_target_pairs={{0,4},{1,5},{2,6},{3,7},{4,0},{5,1},{6,2},{7,3},{8,12},{9,13},{10,... | collective-permute-start | bytes 98312 | tf_op jit(solution)/shard_map/ppermute | solution.py:24
  28.4 6.1 %collective-permute-start.2 = (f32[3,8,4,512]{3,2,1,0:T(4,128)S(1)}, f32[3,8,4,512]{3,2,1,0:T(4,128)S(1)}, u32[]{:S(2)}, u32[]{:S(2)}) collective-permute-start(f32[3,8,4,512]{3,2,1,0:T(4,128)S(1)} %fusion.16), channel_id=1, source_target_pairs={{0,2},{1,3},{2,0},{3,1},{4,6},{5,7},{6,4},{7,5},{8,10},{9,11},{10,... | collective-permute-start | bytes 589832 | tf_op jit(solution)/shard_map/ppermute | solution.py:24
  30.2 5.9 %collective-permute-start.7 = (f32[2,4,512]{2,1,0:T(4,128)S(1)}, f32[2,4,512]{2,1,0:T(4,128)S(1)}, u32[]{:S(2)}, u32[]{:S(2)}) collective-permute-start(f32[2,4,512]{2,1,0:T(4,128)S(1)} %select_bitcast_fusion.1), channel_id=1, source_target_pairs={{0,8},{1,9},{2,10},{3,11},{4,12},{5,13},{6,14},{7,15},{8,0},{9,1},... | collective-permute-start | bytes 49160 | tf_op jit(solution)/shard_map/ppermute | solution.py:24
  34.6 4.7 %collective-permute-start.4 = (f32[3,4,4,512]{3,2,1,0:T(4,128)S(1)}, f32[3,4,4,512]{3,2,1,0:T(4,128)S(1)}, u32[]{:S(2)}, u32[]{:S(2)}) collective-permute-start(f32[3,4,4,512]{3,2,1,0:T(4,128)S(1)} %fusion.22), channel_id=1, source_target_pairs={{0,4},{1,5},{2,6},{3,7},{4,0},{5,1},{6,2},{7,3},{8,12},{9,13},{10,... | collective-permute-start | bytes 294920 | tf_op jit(solution)/shard_map/ppermute | solution.py:24
  39.4 4.2 %collective-permute-start.6 = (f32[3,2,4,512]{3,2,1,0:T(4,128)S(1)}, f32[3,2,4,512]{3,2,1,0:T(4,128)S(1)}, u32[]{:S(2)}, u32[]{:S(2)}) collective-permute-start(f32[3,2,4,512]{3,2,1,0:T(4,128)S(1)} %fusion.28), channel_id=1, source_target_pairs={{0,8},{1,9},{2,10},{3,11},{4,12},{5,13},{6,14},{7,15},{8,0},{9,1},... | collective-permute-start | bytes 147464 | tf_op jit(solution)/shard_map/ppermute | solution.py:24
  41.0 5.2 %collective-permute-start.9 = (f32[1,4,512]{2,1,0:T(4,128)S(1)}, f32[1,4,512]{2,1,0:T(4,128)S(1)}, u32[]{:S(2)}, u32[]{:S(2)}) collective-permute-start(f32[1,4,512]{2,1,0:T(4,128)S(1)} %select_bitcast_fusion.2), channel_id=1, source_target_pairs={{0,16},{1,17},{2,18},{3,19},{4,20},{5,21},{6,22},{7,23},{8,24},{9,... | collective-permute-start | bytes 24584 | tf_op jit(solution)/shard_map/ppermute | solution.py:24
  43.6 4.8 %collective-permute-start.8 = (f32[3,1,4,512]{3,2,0,1:T(4,128)S(1)}, f32[3,1,4,512]{3,2,0,1:T(4,128)S(1)}, u32[]{:S(2)}, u32[]{:S(2)}) collective-permute-start(f32[3,1,4,512]{3,2,0,1:T(4,128)S(1)} %fusion.35), channel_id=1, source_target_pairs={{0,16},{1,17},{2,18},{3,19},{4,20},{5,21},{6,22},{7,23},{8,24},{9,... | collective-permute-start | bytes 73736 | tf_op jit(solution)/shard_map/ppermute | solution.py:24
where the time goes:
time: 49.3 us; the launch traced here: 49.1 us
  starting transfers between devices  16.8 us (34%)
  other arithmetic  10.7 us (22%)
  waiting for transfers between devices  10.1 us (20%)
  between operations  4.14 us (8%)
  matrix products  4.11 us (8%)
  local copies, waits for them, and re-layouts  3.22 us (7%)
    ppermute x10, starting transfers between devices, swapped(): return lax.ppermute(value, axis, pairs)  16.8 us
    ppermute x10, waiting for transfers between devices, swapped(): return lax.ppermute(value, axis, pairs)  10.1 us
    another operation x1, other arithmetic, on_device(): before = jnp.cumsum(clipped, axis=0) - clipped  4.64 us
    dot_general x1, matrix products, on_device(): jnp.dot(masked.reshape(slices * rows, cells), upper, preferred_element_ty...  4.11 us
    mul x1, other arithmetic, on_device(): density * full_flags.reshape(slices, rows, cells).astype(jnp.bfloat16)  2.92 us
    convert_element_type x2, local copies, waits for them, and re-layouts, on_device(): full_flags.reshape(slices, rows, cells).astype(jnp.bfloat16)  2.37 us
  transfers between devices with their start and end apart: 10, of which 5 were waited for; matrix products, arithmetic and copies ran while one was open for 11% of the time, Pallas kernels for 0%

commit v1 on v0

v1 whole, which is shorter than its diff:
```python
import functools
import math

import jax
import jax.numpy as jnp
from jax import lax
from jax.experimental import pallas as pl
from jax.experimental.pallas import tpu as pltpu
from jax.sharding import PartitionSpec as P

LANES = 128


def prefix(value, axis, join, neutral):
    count, mine = (lax.axis_size(axis), lax.axis_index(axis))
    pieces = lax.all_gather(value, axis)
    so_far = jnp.full_like(value, 0) + jnp.asarray(neutral, value.dtype)

    def lap(position, so_far):
        longer = join(so_far, pieces[position])
        return jnp.where(position < mine, longer, so_far)

    return lax.fori_loop(0, count - 1, lap, so_far)


def slab_kernel(depth_scale, light_scale, share_rows, has_nearer, bit_ref, flags_ref, dens_ref, *rest):
    if has_nearer:
        nearer_ref, keep_ref, give_ref, dens, masked, upper, sems = rest
    else:
        keep_ref, give_ref, dens, masked, upper, sems = rest
    slices, rows, cells = dens.shape
    blocks_r, blocks_x = flags_ref.shape[1:]
    band = rows // blocks_r
    width = cells // blocks_x
    shares = band // share_rows

    def copy(block):
        at = pl.ds(pl.multiple_of(block * band, band), band)
        return pltpu.make_async_copy(dens_ref.at[:, at, :], dens.at[:, at, :], sems.at[block])

    for block in range(blocks_r):
        copy(block).start()
    upper[...] = (
        lax.broadcasted_iota(jnp.int32, (cells, cells), 0)
        < lax.broadcasted_iota(jnp.int32, (cells, cells), 1)
    ).astype(jnp.float32).astype(jnp.bfloat16)
    odd = bit_ref[0] == 1

    def step(block, carry):
        copy(block).wait()
        at = pl.ds(pl.multiple_of(block * band, band), band)
        for z in range(slices):
            for j in range(blocks_x):
                cols = pl.ds(j * width, width)
                flag = flags_ref[z, block, j].astype(jnp.float32)
                flag = jnp.full((band, width), flag, jnp.float32).astype(jnp.bfloat16)
                masked[z, :, cols] = dens[z, at, cols] * flag
        lhs = masked[...].reshape(slices * band, cells)
        inside = jnp.dot(lhs, upper[...], preferred_element_type=jnp.float32)
        inside = inside.reshape(slices, band, cells)
        before = jnp.zeros((band, cells), jnp.float32)
        through = jnp.ones((band, cells), jnp.float32)
        base = jnp.zeros((band, cells), jnp.float32)
        lit = jnp.zeros((band, cells), jnp.float32)
        for z in range(slices):
            clipped = masked[z].astype(jnp.float32)
            before = before + clipped
            behind = jnp.exp2(before * depth_scale)
            emitted = clipped * (through - behind)
            through = behind
            shade = inside[z]
            if has_nearer:
                shade = shade + nearer_ref[z, at, :]
            base = base + emitted
            lit = lit + emitted * jnp.exp2(shade * light_scale)
        for channel, value in enumerate((base, lit, before)):
            for pair in range(shares // 2):
                halves = []
                for side in range(2):
                    first = (2 * pair + side) * share_rows
                    halves.append(
                        jnp.concatenate(
                            [
                                value[first : first + share_rows, j * LANES : (j + 1) * LANES]
                                for j in range(cells // LANES)
                            ],
                            axis=0,
                        )
                    )
                to = block * (shares // 2) + pair
                keep_ref[channel, to] = jnp.where(odd, halves[1], halves[0])
                give_ref[channel, to] = jnp.where(odd, halves[0], halves[1])
        return carry

    lax.fori_loop(0, blocks_r, step, 0)


def composite_slab(bit, clip_flags, density, nearer, kappa, extinct, depth_n):
    slices, rows, cells = density.shape
    share_rows = rows // depth_n
    half = (3, depth_n // 2, share_rows * cells // LANES, LANES)
    log2e = math.log2(math.e)
    has_nearer = nearer is not None
    smem = pl.BlockSpec(memory_space=pltpu.SMEM)
    vmem = pl.BlockSpec(memory_space=pltpu.VMEM)
    return pl.pallas_call(
        functools.partial(slab_kernel, -kappa * log2e, -extinct * log2e, share_rows, has_nearer),
        out_shape=[jax.ShapeDtypeStruct(half, jnp.float32)] * 2,
        in_specs=[smem, smem, pl.BlockSpec(memory_space=pltpu.HBM)] + [vmem] * has_nearer,
        out_specs=[vmem, vmem],
        scratch_shapes=[
            pltpu.VMEM((slices, rows, cells), jnp.bfloat16),
            pltpu.VMEM((slices, rows // clip_flags.shape[1], cells), jnp.bfloat16),
            pltpu.VMEM((cells, cells), jnp.bfloat16),
            pltpu.SemaphoreType.DMA((clip_flags.shape[1],)),
        ],
        compiler_params=pltpu.CompilerParams(vmem_limit_bytes=32 * 2**20),
        cost_estimate=pl.CostEstimate(
            flops=2 * slices * rows * cells * cells,
            bytes_accessed=2 * slices * rows * cells,
            transcendentals=2 * slices * rows * cells,
        ),
        name="slab",
    )(bit, clip_flags, density, *([nearer] if has_nearer else []))


def on_device(density, clip_flags, band_offset, order, ambient, diffuse):
    slices, rows, cells = density.shape
    depth_n = lax.axis_size("depth")
    xs_n = lax.axis_size("xs")
    kappa = 2.0 / (slices * depth_n)
    extinct = 2.0 / (cells * xs_n)
    share_rows = rows // depth_n
    levels = depth_n.bit_length() - 1
    my_slab = lax.axis_index("depth")
    my_rank = my_slab ^ order[0]
    nearer = None
    if xs_n > 1:
        blocks_r, blocks_x = clip_flags.shape[1:]
        kept = density.astype(jnp.float32).reshape(
            slices, blocks_r, rows // blocks_r, blocks_x, cells // blocks_x
        )
        totals = jnp.sum(kept, axis=4) * clip_flags[:, :, None, :].astype(jnp.float32)
        totals = jnp.sum(totals, axis=3).reshape(slices, rows)
        nearer = prefix(totals, "xs", lambda early, late: early + late, jnp.zeros_like(totals))
        nearer = nearer[:, :, None]
    bit = (my_slab & 1).astype(jnp.int32).reshape(1)
    keep, give = composite_slab(bit, clip_flags, density, nearer, kappa, extinct, depth_n)
    for level in range(levels):
        mask = 2**level
        pairs = [(source, source ^ mask) for source in range(depth_n)]
        recv = lax.ppermute(give, "depth", pairs)
        partner_front = (my_rank >> level & 1).astype(jnp.float32)
        keep_fade = jnp.exp(-kappa * partner_front * recv[2])
        recv_fade = jnp.exp(-kappa * (1.0 - partner_front) * keep[2])
        colors = keep[:2] * keep_fade[None] + recv[:2] * recv_fade[None]
        column = keep[2:] + recv[2:]
        share = jnp.concatenate([colors, column], axis=0)
        if level + 1 < levels:
            side = my_slab >> (level + 1) & 1
            split = share.reshape(3, share.shape[1] // 2, 2, *share.shape[2:])
            keep = lax.dynamic_index_in_dim(split, side, axis=2, keepdims=False)
            give = lax.dynamic_index_in_dim(split, 1 - side, axis=2, keepdims=False)
    share = share.reshape(3, cells // LANES, share_rows, LANES)
    share = share.transpose(0, 2, 1, 3).reshape(3, share_rows, cells)
    row_pos = band_offset[0] + my_slab * share_rows + jnp.arange(share_rows, dtype=jnp.int32)
    source = 0.6 + 0.4 * jnp.cos(2.0 * math.pi * row_pos.astype(jnp.float32) / 64.0)
    lit = source[:, None] * share[1]
    colors = ambient[:, None, None] * share[0][None] + diffuse[:, None, None] * lit[None]
    alpha = -jnp.expm1(-kappa * share[2])
    return jnp.concatenate([colors, alpha[None]], axis=0)


def solution(mesh):
    return jax.shard_map(
        on_device,
        mesh=mesh,
        in_specs=(P("depth", None, "xs"), P("depth", None, "xs"), P(), P(), P(), P()),
        out_specs=P(None, "depth", "xs"),
        check_vma=False,
    )
```

time: 49.3 us -> 32.7 us (0.66)
  other arithmetic: 10.7 us -> 1.17 us
  starting transfers between devices: 16.8 us -> 10.3 us
  Pallas kernels: 0 us -> 4.9 us
  matrix products: 4.11 us -> 0 us
  between operations: 4.14 us -> 0.88 us
  waiting for transfers between devices: 10.1 us -> 12.7 us
  local copies, waits for them, and re-layouts: 3.22 us -> 2.52 us
    ppermute x10 -> x5, starting transfers between devices: 16.8 us -> 10.3 us  [on_device(): recv = lax.ppermute(give, 'depth', pairs)]
    pallas_call x0 -> x1, Pallas kernels: none -> 4.9 us  [composite_slab(): pl.pallas_call(functools.partial(slab_kernel, -kappa * log2e, -extinct *...]
    another operation x2 -> x0, other arithmetic: 4.66 us -> none  [the longest x1 4.64 us: on_device(): before = jnp.cumsum(clipped, axis=0) - clipped]
    dot_general x1 -> x0, matrix products: 4.11 us -> none  [on_device(): jnp.dot(masked.reshape(slices * rows, cells), upper, preferred_element_ty...]
    mul x2 -> x6, other arithmetic: 2.94 us -> 0.17 us  [the longest x4 0.08 us: on_device(): colors = keep[:2] * keep_fade[None] + recv[:2] * recv_fade[None]]
    ppermute x10 -> x5, waiting for transfers between devices: 10.1 us -> 12.7 us  [on_device(): recv = lax.ppermute(give, 'depth', pairs)]
    unnamed x6 -> x9, local copies, waits for them, and re-layouts: 0.02 us -> 2.46 us
    convert_element_type x2 -> x0, local copies, waits for them, and re-layouts: 2.37 us -> none  [on_device(): full_flags.reshape(slices, rows, cells).astype(jnp.bfloat16)]
  transfers between devices with their start and end apart: 10 -> 5, of which waited for: 5 -> 5; matrix products, arithmetic and copies ran while one was open for 11% -> 0% of each run, Pallas kernels for 0% -> 0%
where the time goes in v1:
time: 32.7 us; the launch traced here: 32.5 us
  waiting for transfers between devices  12.7 us (39%)
  starting transfers between devices  10.3 us (31%)
  Pallas kernels  4.9 us (15%)
  local copies, waits for them, and re-layouts  2.52 us (8%)
  other arithmetic  1.17 us (4%)
  between operations  0.88 us (3%)
    ppermute x5, waiting for transfers between devices, on_device(): recv = lax.ppermute(give, 'depth', pairs)  12.7 us
    ppermute x5, starting transfers between devices, on_device(): recv = lax.ppermute(give, 'depth', pairs)  10.3 us
    pallas_call x1, Pallas kernels, composite_slab(): pl.pallas_call(functools.partial(slab_kernel, -kappa * log2e, -extinct *...  4.9 us
    unnamed x9, local copies, waits for them, and re-layouts  2.46 us
  transfers between devices with their start and end apart: 5, of which 5 were waited for; matrix products, arithmetic and copies ran while one was open for 0% of the time, Pallas kernels for 0%

profile of v1, /device:TPU:0, one launch (start us, length us, event | category | flops | bytes accessed | tf_op | source)
XLA Modules:
  0.0 32.5 jit_solution(12120504440095008922)
XLA Ops:
  0.0 0.0 copy-start.3
  0.0 0.9 %copy.18.flags_ref = s32[16,8,4]{2,1,0:T(8,128)S(1)} copy(s32[16,8,4]{0,2,1:T(4,128)} %param.7) | data formatting | bytes 4096 | tf_op args[1]
  0.9 0.0 copy-start
  0.9 1.6 %copy-done = bf16[16,128,512]{2,1,0:T(8,128)(2,1)S(1)} copy-done((bf16[16,128,512]{2,1,0:T(8,128)(2,1)S(1)}, bf16[16,128,512]{2,1,0:T(8,128)(2,1)}, u32[]{:S(2)}) %copy-start) | copy-done | bytes 2097176
  2.4 4.9 %slab.1 = (f32[3,16,16,128]{3,2,1,0:T(8,128)S(1)}, f32[3,16,16,128]{3,2,1,0:T(8,128)S(1)}) custom-call(s32[1]{0:T(128)} %bitcast.bit_ref, s32[16,8,4]{2,1,0:T(8,128)S(1)} %copy.18.flags_ref, bf16[16,128,512]{2,1,0:T(8,128)(2,1)S(1)} %copy-done), custom_call_target="tpu_custom_call" | custom-call | flops 1073741824 | bytes 2097152 | tf_op jit(solution)/shard_map/slab/pallas_call | solution.py:106
  7.4 0.5 %collective-permute-start = (f32[3,16,16,128]{3,2,1,0:T(8,128)S(1)}, f32[3,16,16,128]{3,2,1,0:T(8,128)S(1)}, u32[]{:S(2)}, u32[]{:S(2)}) collective-permute-start(f32[3,16,16,128]{3,2,1,0:T(8,128)S(1)} %get-tuple-element.8), channel_id=1, source_target_pairs={{0,1},{1,0},{2,3},{3,2},{4,5},{5,4},{6,7},{7,6},{8,9},{9,8},{10,11... | collective-permute-start | bytes 1179656 | tf_op jit(solution)/shard_map/ppermute | solution.py:152
  7.9 0.0 copy-done.3
  7.9 1.3 %collective-permute-done = f32[3,16,16,128]{3,2,1,0:T(8,128)S(1)} collective-permute-done((f32[3,16,16,128]{3,2,1,0:T(8,128)S(1)}, f32[3,16,16,128]{3,2,1,0:T(8,128)S(1)}, u32[]{:S(2)}, u32[]{:S(2)}) %collective-permute-start) | collective-permute-done | bytes 393248 | tf_op jit(solution)/shard_map/ppermute | solution.py:152
  9.3 0.1 fusion
  9.3 0.0 copy-start.1
  9.4 0.0 copy-start.2
  9.4 2.9 %collective-permute-start.1 = (f32[3,8,16,128]{3,2,1,0:T(8,128)S(1)}, f32[3,8,16,128]{3,2,1,0:T(8,128)S(1)}, u32[]{:S(2)}, u32[]{:S(2)}) collective-permute-start(f32[3,8,16,128]{3,2,1,0:T(8,128)S(1)} %dynamic-slice_bitcast_fusion), channel_id=1, source_target_pairs={{0,2},{1,3},{2,0},{3,1},{4,6},{5,7},{6,4},{7,5},{8,10},{9,11},{10,... | collective-permute-start | bytes 589832 | tf_op jit(solution)/shard_map/ppermute | solution.py:152
  13.0 4.5 %collective-permute-done.1 = f32[3,8,16,128]{3,2,1,0:T(8,128)S(1)} collective-permute-done((f32[3,8,16,128]{3,2,1,0:T(8,128)S(1)}, f32[3,8,16,128]{3,2,1,0:T(8,128)S(1)}, u32[]{:S(2)}, u32[]{:S(2)}) %collective-permute-start.1) | collective-permute-done | bytes 196640 | tf_op jit(solution)/shard_map/ppermute | solution.py:152
  17.7 1.8 %collective-permute-start.2 = (f32[3,4,16,128]{3,2,1,0:T(8,128)S(1)}, f32[3,4,16,128]{3,2,1,0:T(8,128)S(1)}, u32[]{:S(2)}, u32[]{:S(2)}) collective-permute-start(f32[3,4,16,128]{3,2,1,0:T(8,128)S(1)} %get-tuple-element.13), channel_id=1, source_target_pairs={{0,4},{1,5},{2,6},{3,7},{4,0},{5,1},{6,2},{7,3},{8,12},{9,13},{10,... | collective-permute-start | bytes 294920 | tf_op jit(solution)/shard_map/ppermute | solution.py:152
  19.5 2.8 %collective-permute-done.2 = f32[3,4,16,128]{3,2,1,0:T(8,128)S(1)} collective-permute-done((f32[3,4,16,128]{3,2,1,0:T(8,128)S(1)}, f32[3,4,16,128]{3,2,1,0:T(8,128)S(1)}, u32[]{:S(2)}, u32[]{:S(2)}) %collective-permute-start.2) | collective-permute-done | bytes 98336 | tf_op jit(solution)/shard_map/ppermute | solution.py:152
  22.4 1.9 %collective-permute-start.3 = (f32[3,2,16,128]{3,2,1,0:T(8,128)S(1)}, f32[3,2,16,128]{3,2,1,0:T(8,128)S(1)}, u32[]{:S(2)}, u32[]{:S(2)}) collective-permute-start(f32[3,2,16,128]{3,2,1,0:T(8,128)S(1)} %get-tuple-element.17), channel_id=1, source_target_pairs={{0,8},{1,9},{2,10},{3,11},{4,12},{5,13},{6,14},{7,15},{8,0},{9,1},... | collective-permute-start | bytes 147464 | tf_op jit(solution)/shard_map/ppermute | solution.py:152
  24.3 2.3 %collective-permute-done.3 = f32[3,2,16,128]{3,2,1,0:T(8,128)S(1)} collective-permute-done((f32[3,2,16,128]{3,2,1,0:T(8,128)S(1)}, f32[3,2,16,128]{3,2,1,0:T(8,128)S(1)}, u32[]{:S(2)}, u32[]{:S(2)}) %collective-permute-start.3) | collective-permute-done | bytes 49184 | tf_op jit(solution)/shard_map/ppermute | solution.py:152
  26.6 3.2 %collective-permute-start.4 = (f32[3,1,16,128]{3,2,1,0:T(8,128)S(1)}, f32[3,1,16,128]{3,2,1,0:T(8,128)S(1)}, u32[]{:S(2)}, u32[]{:S(2)}) collective-permute-start(f32[3,1,16,128]{3,2,1,0:T(8,128)S(1)} %get-tuple-element.20), channel_id=1, source_target_pairs={{0,16},{1,17},{2,18},{3,19},{4,20},{5,21},{6,22},{7,23},{8,24},{9,... | collective-permute-start | bytes 73736 | tf_op jit(solution)/shard_map/ppermute | solution.py:152
  29.9 1.8 %collective-permute-done.4 = f32[3,1,16,128]{3,2,1,0:T(8,128)S(1)} collective-permute-done((f32[3,1,16,128]{3,2,1,0:T(8,128)S(1)}, f32[3,1,16,128]{3,2,1,0:T(8,128)S(1)}, u32[]{:S(2)}, u32[]{:S(2)}) %collective-permute-start.4) | collective-permute-done | bytes 24608 | tf_op jit(solution)/shard_map/ppermute | solution.py:152
  31.7 0.1 fusion.15
  31.8 0.0 copy-done.1
  31.8 0.0 copy-done.2
  31.8 0.1 multiply_add_fusion
  31.8 0.6 %pad_maximum_fusion.3 = f32[4,4,512]{2,1,0:T(4,128)} fusion(f32[1,4,512]{2,1,0:T(4,128)S(1)} %get-tuple-element.25, f32[3,4,512]{2,1,0:T(4,128)S(1)} %multiply_add_fusion), kind=kLoop, calls=%fused_computation.34 | loop fusion | flops 8192 | bytes 65536 | tf_op jit(solution)/shard_map/concatenate | solution.py:171
  (22 shorter events, 0.4 us)
Async XLA Ops:
  0.0 7.9 %copy-start.3 = (s32[32]{0:T(128)S(1)}, s32[32]{0:T(128)}, u32[]{:S(2)}) copy-start(s32[32]{0:T(128)} %param.9) | copy-start | bytes 388
  0.9 1.6 %copy-start = (bf16[16,128,512]{2,1,0:T(8,128)(2,1)S(1)}, bf16[16,128,512]{2,1,0:T(8,128)(2,1)}, u32[]{:S(2)}) copy-start(bf16[16,128,512]{2,1,0:T(8,128)(2,1)} %dens_ref.1) | copy-start | bytes 6291460
  7.4 1.9 %collective-permute-start = (f32[3,16,16,128]{3,2,1,0:T(8,128)S(1)}, f32[3,16,16,128]{3,2,1,0:T(8,128)S(1)}, u32[]{:S(2)}, u32[]{:S(2)}) collective-permute-start(f32[3,16,16,128]{3,2,1,0:T(8,128)S(1)} %get-tuple-element.8), channel_id=1, source_target_pairs={{0,1},{1,0},{2,3},{3,2},{4,5},{5,4},{6,7},{7,6},{8,9},{9,8},{10,11... | collective-permute-start | bytes 1179656 | tf_op jit(solution)/shard_map/ppermute | solution.py:152
  9.3 22.4 %copy-start.1 = (f32[3]{0:T(128)S(1)}, f32[3]{0:T(128)}, u32[]{:S(2)}) copy-start(f32[3]{0:T(128)} %param.11) | copy-start | bytes 40
  9.4 22.4 %copy-start.2 = (f32[3]{0:T(128)S(1)}, f32[3]{0:T(128)}, u32[]{:S(2)}) copy-start(f32[3]{0:T(128)} %param.10) | copy-start | bytes 40
  9.4 8.1 %collective-permute-start.1 = (f32[3,8,16,128]{3,2,1,0:T(8,128)S(1)}, f32[3,8,16,128]{3,2,1,0:T(8,128)S(1)}, u32[]{:S(2)}, u32[]{:S(2)}) collective-permute-start(f32[3,8,16,128]{3,2,1,0:T(8,128)S(1)} %dynamic-slice_bitcast_fusion), channel_id=1, source_target_pairs={{0,2},{1,3},{2,0},{3,1},{4,6},{5,7},{6,4},{7,5},{8,10},{9,11},{10,... | collective-permute-start | bytes 589832 | tf_op jit(solution)/shard_map/ppermute | solution.py:152
  17.7 4.7 %collective-permute-start.2 = (f32[3,4,16,128]{3,2,1,0:T(8,128)S(1)}, f32[3,4,16,128]{3,2,1,0:T(8,128)S(1)}, u32[]{:S(2)}, u32[]{:S(2)}) collective-permute-start(f32[3,4,16,128]{3,2,1,0:T(8,128)S(1)} %get-tuple-element.13), channel_id=1, source_target_pairs={{0,4},{1,5},{2,6},{3,7},{4,0},{5,1},{6,2},{7,3},{8,12},{9,13},{10,... | collective-permute-start | bytes 294920 | tf_op jit(solution)/shard_map/ppermute | solution.py:152
  22.4 4.2 %collective-permute-start.3 = (f32[3,2,16,128]{3,2,1,0:T(8,128)S(1)}, f32[3,2,16,128]{3,2,1,0:T(8,128)S(1)}, u32[]{:S(2)}, u32[]{:S(2)}) collective-permute-start(f32[3,2,16,128]{3,2,1,0:T(8,128)S(1)} %get-tuple-element.17), channel_id=1, source_target_pairs={{0,8},{1,9},{2,10},{3,11},{4,12},{5,13},{6,14},{7,15},{8,0},{9,1},... | collective-permute-start | bytes 147464 | tf_op jit(solution)/shard_map/ppermute | solution.py:152
  26.6 5.0 %collective-permute-start.4 = (f32[3,1,16,128]{3,2,1,0:T(8,128)S(1)}, f32[3,1,16,128]{3,2,1,0:T(8,128)S(1)}, u32[]{:S(2)}, u32[]{:S(2)}) collective-permute-start(f32[3,1,16,128]{3,2,1,0:T(8,128)S(1)} %get-tuple-element.20), channel_id=1, source_target_pairs={{0,16},{1,17},{2,18},{3,19},{4,20},{5,21},{6,22},{7,23},{8,24},{9,... | collective-permute-start | bytes 73736 | tf_op jit(solution)/shard_map/ppermute | solution.py:152

commit v2 on v1

v2 whole, which is shorter than its diff:
```python
import functools
import math

import jax
import jax.numpy as jnp
from jax import lax
from jax.experimental import pallas as pl
from jax.experimental.pallas import tpu as pltpu

from jax.sharding import PartitionSpec as P

LANES = 128

def prefix(value, axis, join, neutral):
    count, mine = (lax.axis_size(axis), lax.axis_index(axis))
    pieces = lax.all_gather(value, axis)
    so_far = jnp.full_like(value, 0) + jnp.asarray(neutral, value.dtype)

    def lap(position, so_far):
        longer = join(so_far, pieces[position])
        return jnp.where(position < mine, longer, so_far)

    return lax.fori_loop(0, count - 1, lap, so_far)


def slab_kernel(depth_scale, light_scale, share_rows, has_nearer, flags_hbm, dens_ref, *rest):
    if has_nearer:
        nearer_ref, *rest = rest
    keep_ref, give_ref, dens, masked, inside, upper, flags, sems, flag_sem = rest
    slices, rows, cells = dens.shape
    blocks_r, blocks_x = flags.shape[:2]
    band = rows // blocks_r
    width = cells // blocks_x
    span = upper.shape[0]
    group = masked.shape[2] // band
    tall = group * band
    shares = band // share_rows

    def copy(step):
        at = pl.ds(pl.multiple_of(step * tall, tall), tall)
        return pltpu.make_async_copy(dens_ref.at[:, at, :], dens.at[:, at, :], sems.at[step])

    flag_copy = pltpu.make_async_copy(flags_hbm, flags, flag_sem)
    flag_copy.start()
    for step in range(rows // tall):
        copy(step).start()
    upper[...] = (
        lax.broadcasted_iota(jnp.int32, (span, span), 0) < lax.broadcasted_iota(jnp.int32, (span, span), 1)
    ).astype(jnp.float32).astype(jnp.bfloat16)
    odd = lax.axis_index("depth") & 1 == 1
    flag_copy.wait()

    def work(step, carry):
        copy(step).wait()
        for g in range(group):
            block = step * group + g
            at = pl.ds(pl.multiple_of(block * band, band), band)
            for j in range(blocks_x):
                for z in range(slices):
                    flag = flags[block, j, z].astype(jnp.float32)
                    flag = jnp.full((band, width), flag, jnp.float32).astype(jnp.bfloat16)
                    masked[j * width // span, z, g * band : (g + 1) * band, j * width % span : j * width % span + width] = (
                        dens[z, at, j * width : (j + 1) * width] * flag
                    )
        lhs = masked[...].reshape(cells // span * slices * tall, span)
        inside[...] = jnp.dot(lhs, upper[...], preferred_element_type=jnp.float32).reshape(inside.shape)
        for g in range(group):
            sub = slice(g * band, (g + 1) * band)
            at = pl.ds(pl.multiple_of((step * group + g) * band, band), band)
            outs = []
            for j in range(cells // LANES):
                h, first = j * LANES // span, j * LANES % span
                cols = slice(first, first + LANES)
                before = jnp.zeros((band, LANES), jnp.float32)
                through = jnp.ones((band, LANES), jnp.float32)
                base = jnp.zeros((band, LANES), jnp.float32)
                lit = jnp.zeros((band, LANES), jnp.float32)
                for z in range(slices):
                    clipped = masked[h, z, sub, cols].astype(jnp.float32)
                    before = before + clipped
                    behind = jnp.exp2(before * depth_scale)
                    emitted = clipped * (through - behind)
                    through = behind
                    shade = inside[h, z, sub, cols]
                    for left in range(h):
                        shade = shade + inside[left, z, sub, span - 1 : span] + masked[left, z, sub, span - 1 : span].astype(jnp.float32)
                    if has_nearer:
                        shade = shade + nearer_ref[z, at, :]
                    base = base + emitted
                    lit = lit + emitted * jnp.exp2(shade * light_scale)
                outs.append((base, lit, before))
            for channel in range(3):
                for pair in range(shares // 2):
                    halves = []
                    for side in range(2):
                        first = (2 * pair + side) * share_rows
                        halves.append(jnp.concatenate([o[channel][first : first + share_rows] for o in outs], axis=0))
                    to = (step * group + g) * (shares // 2) + pair
                    keep_ref[channel, to] = jnp.where(odd, halves[1], halves[0])
                    give_ref[channel, to] = jnp.where(odd, halves[0], halves[1])
        return carry

    lax.fori_loop(0, rows // tall, work, 0)


def composite_slab(clip_flags, density, nearer, kappa, extinct, depth_n):
    slices, rows, cells = density.shape
    share_rows = rows // depth_n
    blocks_r, blocks_x = clip_flags.shape[1:]
    half = (3, depth_n // 2, share_rows * cells // LANES, LANES)
    log2e = math.log2(math.e)
    has_nearer = nearer is not None
    span = math.gcd(cells, 2 * LANES)
    tall = math.gcd(blocks_r, 2) * rows // blocks_r
    vmem = pl.BlockSpec(memory_space=pltpu.VMEM)
    return pl.pallas_call(
        functools.partial(slab_kernel, -kappa * log2e, -extinct * log2e, share_rows, has_nearer),
        out_shape=[jax.ShapeDtypeStruct(half, jnp.float32)] * 2,
        in_specs=[pl.BlockSpec(memory_space=pltpu.HBM)] * 2 + [vmem] * has_nearer,
        out_specs=[vmem, vmem],
        scratch_shapes=[
            pltpu.VMEM((slices, rows, cells), jnp.bfloat16),
            pltpu.VMEM((cells // span, slices, tall, span), jnp.bfloat16),
            pltpu.VMEM((cells // span, slices, tall, span), jnp.float32),
            pltpu.VMEM((span, span), jnp.bfloat16),
            pltpu.SMEM((blocks_r, blocks_x, slices), jnp.int32),
            pltpu.SemaphoreType.DMA((rows // tall,)),
            pltpu.SemaphoreType.DMA,
        ],
        compiler_params=pltpu.CompilerParams(vmem_limit_bytes=60 * 2**20),
        cost_estimate=pl.CostEstimate(
            flops=2 * slices * rows * cells * cells,
            bytes_accessed=2 * slices * rows * cells,
            transcendentals=2 * slices * rows * cells,
        ),
        name="slab",
    )(clip_flags.transpose(1, 2, 0), density, *([nearer] if has_nearer else []))


def exchange(pieces, my_slab, my_rank, low, kappa):
    depth_n = lax.axis_size("depth")
    held = [pieces[0]]
    for m in range(1, len(pieces)):
        pairs = [(source, source ^ (m << low)) for source in range(depth_n)]
        held.append(lax.ppermute(pieces[m], "depth", pairs))
    place = my_rank >> low & (len(pieces) - 1)
    colors = 0.0
    for m, piece in enumerate(held):
        ahead = 0.0
        for other, front in enumerate(held):
            if other != m:
                ahead = ahead + front[2] * ((place ^ other) < (place ^ m)).astype(jnp.float32)
        colors = colors + piece[:2] * jnp.exp(-kappa * ahead)[None]
    return jnp.concatenate([colors, sum(piece[2:] for piece in held)], axis=0)


def on_device(density, clip_flags, band_offset, order, ambient, diffuse):
    slices, rows, cells = density.shape
    depth_n = lax.axis_size("depth")
    xs_n = lax.axis_size("xs")
    kappa = 2.0 / (slices * depth_n)
    extinct = 2.0 / (cells * xs_n)
    share_rows = rows // depth_n
    levels = depth_n.bit_length() - 1
    my_slab = lax.axis_index("depth")
    my_rank = my_slab ^ order[0]
    nearer = None
    if xs_n > 1:
        blocks_r, blocks_x = clip_flags.shape[1:]
        kept = density.astype(jnp.float32).reshape(
            slices, blocks_r, rows // blocks_r, blocks_x, cells // blocks_x
        )
        totals = jnp.sum(kept, axis=4) * clip_flags[:, :, None, :].astype(jnp.float32)
        totals = jnp.sum(totals, axis=3).reshape(slices, rows)
        nearer = prefix(totals, "xs", lambda early, late: early + late, jnp.zeros_like(totals))
        nearer = nearer[:, :, None]
    pieces = composite_slab(clip_flags, density, nearer, kappa, extinct, depth_n)
    share = exchange(pieces, my_slab, my_rank, 0, kappa)
    low = 1
    while low < levels:
        count = 4 if low + 1 < levels else 2
        split = share.reshape(3, share.shape[1] // count, count, *share.shape[2:])
        mine = my_slab >> low & (count - 1)
        pieces = [
            lax.dynamic_index_in_dim(split, mine ^ m, axis=2, keepdims=False) for m in range(count)
        ]
        share = exchange(pieces, my_slab, my_rank, low, kappa)
        low += count.bit_length() - 1
    share = share.reshape(3, cells // LANES, share_rows, LANES)
    share = share.transpose(0, 2, 1, 3).reshape(3, share_rows, cells)
    row_pos = band_offset[0] + my_slab * share_rows + jnp.arange(share_rows, dtype=jnp.int32)
    source = 0.6 + 0.4 * jnp.cos(2.0 * math.pi * row_pos.astype(jnp.float32) / 64.0)
    lit = source[:, None] * share[1]
    colors = ambient[:, None, None] * share[0][None] + diffuse[:, None, None] * lit[None]
    alpha = -jnp.expm1(-kappa * share[2])
    return jnp.concatenate([colors, alpha[None]], axis=0)


def solution(mesh):
    return jax.shard_map(
        on_device,
        mesh=mesh,
        in_specs=(P("depth", None, "xs"), P("depth", None, "xs"), P(), P(), P(), P()),
        out_specs=P(None, "depth", "xs"),
        check_vma=False,
    )
```

time: 32.7 us -> 29.7 us (0.908)
  local copies, waits for them, and re-layouts: 2.52 us -> 0.08 us
  other arithmetic: 1.17 us -> 2.99 us
  waiting for transfers between devices: 12.7 us -> 11.6 us
  starting transfers between devices: 10.3 us -> 9.43 us
  Pallas kernels: 4.9 us -> 4.46 us
    unnamed x9 -> x7, local copies, waits for them, and re-layouts: 2.46 us -> 0.02 us
    ppermute x5 -> x7, waiting for transfers between devices: 12.7 us -> 11.6 us  [exchange(): held.append(lax.ppermute(pieces[m], 'depth', pairs))]
    add x6 -> x4, other arithmetic: 0.14 us -> 1.1 us  [the longest x3 1.06 us: exchange(): colors = colors + piece[:2] * jnp.exp(-kappa * ahead)[None]]
    mul x5 -> x4, other arithmetic: 0.1 us -> 1.01 us  [exchange(): colors = colors + piece[:2] * jnp.exp(-kappa * ahead)[None]]
    ppermute x5 -> x7, starting transfers between devices: 10.3 us -> 9.43 us  [exchange(): held.append(lax.ppermute(pieces[m], 'depth', pairs))]
    pallas_call x1, Pallas kernels: 4.9 us -> 4.46 us  [composite_slab(): pl.pallas_call(functools.partial(slab_kernel, -kappa * log2e, -extinct *...]
  transfers between devices with their start and end apart: 5 -> 7, of which waited for: 5 -> 6; matrix products, arithmetic and copies ran while one was open for 0% -> 0% of each run, Pallas kernels for 0% -> 0%
where the time goes in v2:
time: 29.7 us; the launch traced here: 29.5 us
  waiting for transfers between devices  11.6 us (39%)
  starting transfers between devices  9.43 us (32%)
  Pallas kernels  4.46 us (15%)
  other arithmetic  2.99 us (10%)
  between operations  0.9 us (3%)
    ppermute x7, waiting for transfers between devices, exchange(): held.append(lax.ppermute(pieces[m], 'depth', pairs))  11.6 us
    ppermute x7, starting transfers between devices, exchange(): held.append(lax.ppermute(pieces[m], 'depth', pairs))  9.43 us
    pallas_call x1, Pallas kernels, composite_slab(): pl.pallas_call(functools.partial(slab_kernel, -kappa * log2e, -extinct *...  4.46 us
    add x3, other arithmetic, exchange(): colors = colors + piece[:2] * jnp.exp(-kappa * ahead)[None]  1.06 us
    mul x4, other arithmetic, exchange(): colors = colors + piece[:2] * jnp.exp(-kappa * ahead)[None]  1.01 us
    concatenate x1, other arithmetic, on_device(): return jnp.concatenate([colors, alpha[None]], axis=0)  0.63 us
  transfers between devices with their start and end apart: 7, of which 6 were waited for; matrix products, arithmetic and copies ran while one was open for 0% of the time, Pallas kernels for 0%

profile of v2, /device:TPU:0, one launch (start us, length us, event | category | flops | bytes accessed | tf_op | source)
XLA Modules:
  0.0 29.5 jit_solution(15566668166739109016)
XLA Ops:
  0.0 0.0 copy-start.2
  0.0 4.5 %slab.1 = (f32[3,16,16,128]{3,2,1,0:T(8,128)}, f32[3,16,16,128]{3,2,1,0:T(8,128)}) custom-call(s32[8,4,16]{2,1,0:T(4,128)} %bitcast.71, bf16[16,128,512]{2,1,0:T(8,128)(2,1)} %dens_ref.1), custom_call_target="tpu_custom_call" | custom-call | flops 1073741824 | bytes 2097152 | tf_op jit(solution)/shard_map/slab/pallas_call | solution.py:116
  4.5 0.5 %collective-permute-start = (f32[3,16,16,128]{3,2,1,0:T(8,128)}, f32[3,16,16,128]{3,2,1,0:T(8,128)S(1)}, u32[]{:S(2)}, u32[]{:S(2)}) collective-permute-start(f32[3,16,16,128]{3,2,1,0:T(8,128)} %get-tuple-element.8), channel_id=1, source_target_pairs={{0,1},{1,0},{2,3},{3,2},{4,5},{5,4},{6,7},{7,6},{8,9},{9,8},{10,11... | collective-permute-start | bytes 1179656 | tf_op jit(solution)/shard_map/ppermute | solution.py:145
  5.0 0.0 copy-done.2
  5.1 1.5 %collective-permute-done = f32[3,16,16,128]{3,2,1,0:T(8,128)S(1)} collective-permute-done((f32[3,16,16,128]{3,2,1,0:T(8,128)}, f32[3,16,16,128]{3,2,1,0:T(8,128)S(1)}, u32[]{:S(2)}, u32[]{:S(2)}) %collective-permute-start) | collective-permute-done | bytes 393248 | tf_op jit(solution)/shard_map/ppermute | solution.py:145
  6.6 1.0 %exponential_bitcast_fusion.1 = (f32[16,16,128]{2,1,0:T(8,128)S(1)}, f32[1,16,16,128]{3,2,1,0:T(8,128)S(1)}, f32[16,16,128]{2,1,0:T(8,128)S(1)}) fusion(f32[3,16,16,128]{3,2,1,0:T(8,128)S(1)} %collective-permute-done, f32[]{:T(128)S(6)} %convert_element_type.85, f32[3,16,16,128]{3,2,1,0:T(8,128)} %get-tuple-element.7, f32[]{:T(128)S(6)} %convert_element_type.86), kind=kLoop, calls=%fused_computation.8 | loop fusion | flops 163840 | bytes 655368 | tf_op jit(solution)/shard_map/mul | solution.py:153
  7.5 0.0 copy-start
  7.5 0.0 copy-start.1
  7.5 1.0 %fusion = f32[2,16,16,128]{3,2,1,0:T(8,128)S(1)} fusion(f32[3,16,16,128]{3,2,1,0:T(8,128)S(1)} %collective-permute-done, f32[3,16,16,128]{3,2,1,0:T(8,128)} %get-tuple-element.7, f32[16,16,128]{2,1,0:T(8,128)S(1)} %get-tuple-element.18, f32[16,16,128]{2,1,0:T(8,128)S(1)} %get-tuple-element.16), kind=kLoop, calls=%fused_computation.2 | loop fusion | flops 196608 | bytes 1048576 | tf_op jit(solution)/shard_map/add | solution.py:153
  8.6 2.9 %collective-permute-start.1 = (f32[3,4,16,128]{3,2,1,0:T(8,128)S(1)}, f32[3,4,16,128]{3,2,1,0:T(8,128)S(1)}, u32[]{:S(2)}, u32[]{:S(2)}) collective-permute-start(f32[3,4,16,128]{3,2,1,0:T(8,128)S(1)} %get-tuple-element.15), channel_id=1, source_target_pairs={{0,2},{1,3},{2,0},{3,1},{4,6},{5,7},{6,4},{7,5},{8,10},{9,11},{10,... | collective-permute-start | bytes 294920 | tf_op jit(solution)/shard_map/ppermute | solution.py:145
  11.6 1.5 %collective-permute-start.2 = (f32[3,4,16,128]{3,2,1,0:T(8,128)S(1)}, f32[3,4,16,128]{3,2,1,0:T(8,128)S(1)}, u32[]{:S(2)}, u32[]{:S(2)}) collective-permute-start(f32[3,4,16,128]{3,2,1,0:T(8,128)S(1)} %get-tuple-element.14), channel_id=1, source_target_pairs={{0,4},{1,5},{2,6},{3,7},{4,0},{5,1},{6,2},{7,3},{8,12},{9,13},{10,... | collective-permute-start | bytes 294920 | tf_op jit(solution)/shard_map/ppermute | solution.py:145
  13.1 0.0 collective-permute-start.3
  13.8 1.0 %collective-permute-done.1 = f32[3,4,16,128]{3,2,1,0:T(8,128)S(1)} collective-permute-done((f32[3,4,16,128]{3,2,1,0:T(8,128)S(1)}, f32[3,4,16,128]{3,2,1,0:T(8,128)S(1)}, u32[]{:S(2)}, u32[]{:S(2)}) %collective-permute-start.1) | collective-permute-done | bytes 98336 | tf_op jit(solution)/shard_map/ppermute | solution.py:145
  14.7 2.6 %collective-permute-done.2 = f32[3,4,16,128]{3,2,1,0:T(8,128)S(1)} collective-permute-done((f32[3,4,16,128]{3,2,1,0:T(8,128)S(1)}, f32[3,4,16,128]{3,2,1,0:T(8,128)S(1)}, u32[]{:S(2)}, u32[]{:S(2)}) %collective-permute-start.2) | collective-permute-done | bytes 98336 | tf_op jit(solution)/shard_map/ppermute | solution.py:145
  17.3 1.3 %collective-permute-done.3 = f32[3,4,16,128]{3,2,1,0:T(8,128)S(1)} collective-permute-done((f32[3,4,16,128]{3,2,1,0:T(8,128)S(1)}, f32[3,4,16,128]{3,2,1,0:T(8,128)S(1)}, u32[]{:S(2)}, u32[]{:S(2)}) %collective-permute-start.3) | collective-permute-done | bytes 98336 | tf_op jit(solution)/shard_map/ppermute | solution.py:145
  18.7 1.6 %collective-permute-start.4 = (f32[3,1,16,128]{3,2,1,0:T(8,128)S(1)}, f32[3,1,16,128]{3,2,1,0:T(8,128)S(1)}, u32[]{:S(2)}, u32[]{:S(2)}) collective-permute-start(f32[3,1,16,128]{3,2,1,0:T(8,128)S(1)} %get-tuple-element.21), channel_id=1, source_target_pairs={{0,8},{1,9},{2,10},{3,11},{4,12},{5,13},{6,14},{7,15},{8,0},{9,1},... | collective-permute-start | bytes 73736 | tf_op jit(solution)/shard_map/ppermute | solution.py:145
  20.4 2.6 %collective-permute-start.5 = (f32[3,1,16,128]{3,2,1,0:T(8,128)S(1)}, f32[3,1,16,128]{3,2,1,0:T(8,128)S(1)}, u32[]{:S(2)}, u32[]{:S(2)}) collective-permute-start(f32[3,1,16,128]{3,2,1,0:T(8,128)S(1)} %get-tuple-element.23), channel_id=1, source_target_pairs={{0,16},{1,17},{2,18},{3,19},{4,20},{5,21},{6,22},{7,23},{8,24},{9,... | collective-permute-start | bytes 73736 | tf_op jit(solution)/shard_map/ppermute | solution.py:145
  23.0 0.2 collective-permute-start.6
  23.3 0.0 collective-permute-done.4
  23.3 2.0 %collective-permute-done.5 = f32[3,1,16,128]{3,2,1,0:T(8,128)S(1)} collective-permute-done((f32[3,1,16,128]{3,2,1,0:T(8,128)S(1)}, f32[3,1,16,128]{3,2,1,0:T(8,128)S(1)}, u32[]{:S(2)}, u32[]{:S(2)}) %collective-permute-start.5) | collective-permute-done | bytes 24608 | tf_op jit(solution)/shard_map/ppermute | solution.py:145
  25.2 3.3 %collective-permute-done.6 = f32[3,1,16,128]{3,2,1,0:T(8,128)S(1)} collective-permute-done((f32[3,1,16,128]{3,2,1,0:T(8,128)S(1)}, f32[3,1,16,128]{3,2,1,0:T(8,128)S(1)}, u32[]{:S(2)}, u32[]{:S(2)}) %collective-permute-start.6) | collective-permute-done | bytes 24608 | tf_op jit(solution)/shard_map/ppermute | solution.py:145
  28.7 0.1 bitcast_multiply_fusion
  28.8 0.0 copy-done
  28.8 0.0 copy-done.1
  28.8 0.1 multiply_add_fusion
  28.9 0.6 %pad_maximum_fusion.1 = f32[4,4,512]{2,1,0:T(4,128)} fusion(f32[1,4,512]{2,1,0:T(4,128)S(1)} %neg.14, f32[3,4,512]{2,1,0:T(4,128)S(1)} %multiply_add_fusion), kind=kLoop, calls=%fused_computation.27 | loop fusion | flops 8192 | bytes 65536 | tf_op jit(solution)/shard_map/concatenate | solution.py:196
  (15 shorter events, 0.3 us)
Async XLA Ops:
  0.0 5.0 %copy-start.2 = (s32[32]{0:T(128)S(1)}, s32[32]{0:T(128)}, u32[]{:S(2)}) copy-start(s32[32]{0:T(128)} %param.9) | copy-start | bytes 388
  4.5 2.1 %collective-permute-start = (f32[3,16,16,128]{3,2,1,0:T(8,128)}, f32[3,16,16,128]{3,2,1,0:T(8,128)S(1)}, u32[]{:S(2)}, u32[]{:S(2)}) collective-permute-start(f32[3,16,16,128]{3,2,1,0:T(8,128)} %get-tuple-element.8), channel_id=1, source_target_pairs={{0,1},{1,0},{2,3},{3,2},{4,5},{5,4},{6,7},{7,6},{8,9},{9,8},{10,11... | collective-permute-start | bytes 1179656 | tf_op jit(solution)/shard_map/ppermute | solution.py:145
  7.5 21.3 %copy-start = (f32[3]{0:T(128)S(1)}, f32[3]{0:T(128)}, u32[]{:S(2)}) copy-start(f32[3]{0:T(128)} %param.11) | copy-start | bytes 40
  7.5 21.3 %copy-start.1 = (f32[3]{0:T(128)S(1)}, f32[3]{0:T(128)}, u32[]{:S(2)}) copy-start(f32[3]{0:T(128)} %param.10) | copy-start | bytes 40
  8.6 6.1 %collective-permute-start.1 = (f32[3,4,16,128]{3,2,1,0:T(8,128)S(1)}, f32[3,4,16,128]{3,2,1,0:T(8,128)S(1)}, u32[]{:S(2)}, u32[]{:S(2)}) collective-permute-start(f32[3,4,16,128]{3,2,1,0:T(8,128)S(1)} %get-tuple-element.15), channel_id=1, source_target_pairs={{0,2},{1,3},{2,0},{3,1},{4,6},{5,7},{6,4},{7,5},{8,10},{9,11},{10,... | collective-permute-start | bytes 294920 | tf_op jit(solution)/shard_map/ppermute | solution.py:145
  11.6 5.8 %collective-permute-start.2 = (f32[3,4,16,128]{3,2,1,0:T(8,128)S(1)}, f32[3,4,16,128]{3,2,1,0:T(8,128)S(1)}, u32[]{:S(2)}, u32[]{:S(2)}) collective-permute-start(f32[3,4,16,128]{3,2,1,0:T(8,128)S(1)} %get-tuple-element.14), channel_id=1, source_target_pairs={{0,4},{1,5},{2,6},{3,7},{4,0},{5,1},{6,2},{7,3},{8,12},{9,13},{10,... | collective-permute-start | bytes 294920 | tf_op jit(solution)/shard_map/ppermute | solution.py:145
  13.1 5.5 %collective-permute-start.3 = (f32[3,4,16,128]{3,2,1,0:T(8,128)S(1)}, f32[3,4,16,128]{3,2,1,0:T(8,128)S(1)}, u32[]{:S(2)}, u32[]{:S(2)}) collective-permute-start(f32[3,4,16,128]{3,2,1,0:T(8,128)S(1)} %get-tuple-element.13), channel_id=1, source_target_pairs={{0,6},{1,7},{2,4},{3,5},{4,2},{5,3},{6,0},{7,1},{8,14},{9,15},{10,... | collective-permute-start | bytes 294920 | tf_op jit(solution)/shard_map/ppermute | solution.py:145
  18.7 4.5 %collective-permute-start.4 = (f32[3,1,16,128]{3,2,1,0:T(8,128)S(1)}, f32[3,1,16,128]{3,2,1,0:T(8,128)S(1)}, u32[]{:S(2)}, u32[]{:S(2)}) collective-permute-start(f32[3,1,16,128]{3,2,1,0:T(8,128)S(1)} %get-tuple-element.21), channel_id=1, source_target_pairs={{0,8},{1,9},{2,10},{3,11},{4,12},{5,13},{6,14},{7,15},{8,0},{9,1},... | collective-permute-start | bytes 73736 | tf_op jit(solution)/shard_map/ppermute | solution.py:145
  20.4 4.9 %collective-permute-start.5 = (f32[3,1,16,128]{3,2,1,0:T(8,128)S(1)}, f32[3,1,16,128]{3,2,1,0:T(8,128)S(1)}, u32[]{:S(2)}, u32[]{:S(2)}) collective-permute-start(f32[3,1,16,128]{3,2,1,0:T(8,128)S(1)} %get-tuple-element.23), channel_id=1, source_target_pairs={{0,16},{1,17},{2,18},{3,19},{4,20},{5,21},{6,22},{7,23},{8,24},{9,... | collective-permute-start | bytes 73736 | tf_op jit(solution)/shard_map/ppermute | solution.py:145
  23.0 5.6 %collective-permute-start.6 = (f32[3,1,16,128]{3,2,1,0:T(8,128)S(1)}, f32[3,1,16,128]{3,2,1,0:T(8,128)S(1)}, u32[]{:S(2)}, u32[]{:S(2)}) collective-permute-start(f32[3,1,16,128]{3,2,1,0:T(8,128)S(1)} %get-tuple-element.24), channel_id=1, source_target_pairs={{0,24},{1,25},{2,26},{3,27},{4,28},{5,29},{6,30},{7,31},{8,16},{9,... | collective-permute-start | bytes 73736 | tf_op jit(solution)/shard_map/ppermute | solution.py:145

commit v3 on v2

--- a/solution.py
+++ b/solution.py
@@ -115,7 +115,7 @@
     vmem = pl.BlockSpec(memory_space=pltpu.VMEM)
     return pl.pallas_call(
         functools.partial(slab_kernel, -kappa * log2e, -extinct * log2e, share_rows, has_nearer),
-        out_shape=[jax.ShapeDtypeStruct(half, jnp.float32)] * 2,
+        out_shape=[pltpu.VMEM(half, jnp.float32)] * 2,
         in_specs=[pl.BlockSpec(memory_space=pltpu.HBM)] * 2 + [vmem] * has_nearer,
         out_specs=[vmem, vmem],
         scratch_shapes=[
@@ -127,14 +127,14 @@
             pltpu.SemaphoreType.DMA((rows // tall,)),
             pltpu.SemaphoreType.DMA,
         ],
-        compiler_params=pltpu.CompilerParams(vmem_limit_bytes=60 * 2**20),
+        compiler_params=pltpu.CompilerParams(vmem_limit_bytes=24 * 2**20),
         cost_estimate=pl.CostEstimate(
             flops=2 * slices * rows * cells * cells,
             bytes_accessed=2 * slices * rows * cells,
             transcendentals=2 * slices * rows * cells,
         ),
         name="slab",
-    )(clip_flags.transpose(1, 2, 0), density, *([nearer] if has_nearer else []))
+    )(clip_flags.transpose(1, 2, 0), pltpu.with_memory_space_constraint(density, pltpu.HBM), *([nearer] if has_nearer else []))
 
 
 def exchange(pieces, my_slab, my_rank, low, kappa):

time: 29.7 us -> 27.5 us (0.926)
  other arithmetic: 2.99 us -> 1.13 us
  Pallas kernels: 4.46 us -> 3.56 us
  local copies, waits for them, and re-layouts: 0.08 us -> 0.81 us
    add x3, other arithmetic: 1.06 us -> 0.1 us  [exchange(): colors = colors + piece[:2] * jnp.exp(-kappa * ahead)[None]]
    pallas_call x1, Pallas kernels: 4.46 us -> 3.56 us  [composite_slab(): pl.pallas_call(functools.partial(slab_kernel, -kappa * log2e, -extinct *...]
    mul x4, other arithmetic: 1.01 us -> 0.1 us  [exchange(): colors = colors + piece[:2] * jnp.exp(-kappa * ahead)[None]]
    unnamed x7 -> x9, local copies, waits for them, and re-layouts: 0.02 us -> 0.75 us
where the time goes in v3:
time: 27.5 us; the launch traced here: 27.3 us
  waiting for transfers between devices  11.4 us (41%)
  starting transfers between devices  9.44 us (34%)
  Pallas kernels  3.56 us (13%)
  other arithmetic  1.13 us (4%)
  between operations  0.91 us (3%)
  local copies, waits for them, and re-layouts  0.81 us (3%)
    ppermute x7, waiting for transfers between devices, exchange(): held.append(lax.ppermute(pieces[m], 'depth', pairs))  11.4 us
    ppermute x7, starting transfers between devices, exchange(): held.append(lax.ppermute(pieces[m], 'depth', pairs))  9.44 us
    pallas_call x1, Pallas kernels, composite_slab(): pl.pallas_call(functools.partial(slab_kernel, -kappa * log2e, -extinct *...  3.56 us
    unnamed x9, local copies, waits for them, and re-layouts  0.75 us
    concatenate x1, other arithmetic, on_device(): return jnp.concatenate([colors, alpha[None]], axis=0)  0.63 us
  transfers between devices with their start and end apart: 7, of which 6 were waited for; matrix products, arithmetic and copies ran while one was open for 0% of the time, Pallas kernels for 0%

profile of v3, /device:TPU:0, one launch (start us, length us, event | category | flops | bytes accessed | tf_op | source)
XLA Modules:
  0.0 27.3 jit_solution(805381608212761696)
XLA Ops:
  0.0 0.0 copy-start.3
  0.0 0.0 copy-start
  0.0 0.7 %copy-done = s32[16,8,4]{0,2,1:T(4,128)S(1)} copy-done((s32[16,8,4]{0,2,1:T(4,128)S(1)}, s32[16,8,4]{0,2,1:T(4,128)}, u32[]{:S(2)}) %copy-start) | copy-done | bytes 2072
  0.7 3.6 %slab.1 = (f32[3,16,16,128]{3,2,1,0:T(8,128)S(1)}, f32[3,16,16,128]{3,2,1,0:T(8,128)S(1)}) custom-call(s32[8,4,16]{2,1,0:T(4,128)S(1)} %bitcast.65, bf16[16,128,512]{2,1,0:T(8,128)(2,1)} %dens_ref.1), custom_call_target="tpu_custom_call" | custom-call | flops 1073741824 | bytes 2097152 | tf_op jit(solution)/shard_map/slab/pallas_call | solution.py:116
  4.3 0.5 %collective-permute-start = (f32[3,16,16,128]{3,2,1,0:T(8,128)S(1)}, f32[3,16,16,128]{3,2,1,0:T(8,128)S(1)}, u32[]{:S(2)}, u32[]{:S(2)}) collective-permute-start(f32[3,16,16,128]{3,2,1,0:T(8,128)S(1)} %get-tuple-element.8), channel_id=1, source_target_pairs={{0,1},{1,0},{2,3},{3,2},{4,5},{5,4},{6,7},{7,6},{8,9},{9,8},{10,11... | collective-permute-start | bytes 1179656 | tf_op jit(solution)/shard_map/ppermute | solution.py:145
  4.8 0.0 copy-done.3
  4.9 1.3 %collective-permute-done = f32[3,16,16,128]{3,2,1,0:T(8,128)S(1)} collective-permute-done((f32[3,16,16,128]{3,2,1,0:T(8,128)S(1)}, f32[3,16,16,128]{3,2,1,0:T(8,128)S(1)}, u32[]{:S(2)}, u32[]{:S(2)}) %collective-permute-start) | collective-permute-done | bytes 393248 | tf_op jit(solution)/shard_map/ppermute | solution.py:145
  6.2 0.0 copy-start.1
  6.2 0.0 copy-start.2
  6.2 0.1 fusion
  6.4 2.9 %collective-permute-start.1 = (f32[3,4,16,128]{3,2,1,0:T(8,128)S(1)}, f32[3,4,16,128]{3,2,1,0:T(8,128)S(1)}, u32[]{:S(2)}, u32[]{:S(2)}) collective-permute-start(f32[3,4,16,128]{3,2,1,0:T(8,128)S(1)} %get-tuple-element.15), channel_id=1, source_target_pairs={{0,2},{1,3},{2,0},{3,1},{4,6},{5,7},{6,4},{7,5},{8,10},{9,11},{10,... | collective-permute-start | bytes 294920 | tf_op jit(solution)/shard_map/ppermute | solution.py:145
  9.3 1.5 %collective-permute-start.2 = (f32[3,4,16,128]{3,2,1,0:T(8,128)S(1)}, f32[3,4,16,128]{3,2,1,0:T(8,128)S(1)}, u32[]{:S(2)}, u32[]{:S(2)}) collective-permute-start(f32[3,4,16,128]{3,2,1,0:T(8,128)S(1)} %get-tuple-element.14), channel_id=1, source_target_pairs={{0,4},{1,5},{2,6},{3,7},{4,0},{5,1},{6,2},{7,3},{8,12},{9,13},{10,... | collective-permute-start | bytes 294920 | tf_op jit(solution)/shard_map/ppermute | solution.py:145
  10.8 0.0 collective-permute-start.3
  11.5 1.0 %collective-permute-done.1 = f32[3,4,16,128]{3,2,1,0:T(8,128)S(1)} collective-permute-done((f32[3,4,16,128]{3,2,1,0:T(8,128)S(1)}, f32[3,4,16,128]{3,2,1,0:T(8,128)S(1)}, u32[]{:S(2)}, u32[]{:S(2)}) %collective-permute-start.1) | collective-permute-done | bytes 98336 | tf_op jit(solution)/shard_map/ppermute | solution.py:145
  12.5 2.6 %collective-permute-done.2 = f32[3,4,16,128]{3,2,1,0:T(8,128)S(1)} collective-permute-done((f32[3,4,16,128]{3,2,1,0:T(8,128)S(1)}, f32[3,4,16,128]{3,2,1,0:T(8,128)S(1)}, u32[]{:S(2)}, u32[]{:S(2)}) %collective-permute-start.2) | collective-permute-done | bytes 98336 | tf_op jit(solution)/shard_map/ppermute | solution.py:145
  15.1 1.3 %collective-permute-done.3 = f32[3,4,16,128]{3,2,1,0:T(8,128)S(1)} collective-permute-done((f32[3,4,16,128]{3,2,1,0:T(8,128)S(1)}, f32[3,4,16,128]{3,2,1,0:T(8,128)S(1)}, u32[]{:S(2)}, u32[]{:S(2)}) %collective-permute-start.3) | collective-permute-done | bytes 98336 | tf_op jit(solution)/shard_map/ppermute | solution.py:145
  16.5 1.6 %collective-permute-start.4 = (f32[3,1,16,128]{3,2,1,0:T(8,128)S(1)}, f32[3,1,16,128]{3,2,1,0:T(8,128)S(1)}, u32[]{:S(2)}, u32[]{:S(2)}) collective-permute-start(f32[3,1,16,128]{3,2,1,0:T(8,128)S(1)} %get-tuple-element.21), channel_id=1, source_target_pairs={{0,8},{1,9},{2,10},{3,11},{4,12},{5,13},{6,14},{7,15},{8,0},{9,1},... | collective-permute-start | bytes 73736 | tf_op jit(solution)/shard_map/ppermute | solution.py:145
  18.1 2.6 %collective-permute-start.5 = (f32[3,1,16,128]{3,2,1,0:T(8,128)S(1)}, f32[3,1,16,128]{3,2,1,0:T(8,128)S(1)}, u32[]{:S(2)}, u32[]{:S(2)}) collective-permute-start(f32[3,1,16,128]{3,2,1,0:T(8,128)S(1)} %get-tuple-element.23), channel_id=1, source_target_pairs={{0,16},{1,17},{2,18},{3,19},{4,20},{5,21},{6,22},{7,23},{8,24},{9,... | collective-permute-start | bytes 73736 | tf_op jit(solution)/shard_map/ppermute | solution.py:145
  20.7 0.2 collective-permute-start.6
  21.0 0.0 collective-permute-done.4
  21.0 2.0 %collective-permute-done.5 = f32[3,1,16,128]{3,2,1,0:T(8,128)S(1)} collective-permute-done((f32[3,1,16,128]{3,2,1,0:T(8,128)S(1)}, f32[3,1,16,128]{3,2,1,0:T(8,128)S(1)}, u32[]{:S(2)}, u32[]{:S(2)}) %collective-permute-start.5) | collective-permute-done | bytes 24608 | tf_op jit(solution)/shard_map/ppermute | solution.py:145
  23.0 3.3 %collective-permute-done.6 = f32[3,1,16,128]{3,2,1,0:T(8,128)S(1)} collective-permute-done((f32[3,1,16,128]{3,2,1,0:T(8,128)S(1)}, f32[3,1,16,128]{3,2,1,0:T(8,128)S(1)}, u32[]{:S(2)}, u32[]{:S(2)}) %collective-permute-start.6) | collective-permute-done | bytes 24608 | tf_op jit(solution)/shard_map/ppermute | solution.py:145
  26.5 0.1 bitcast_multiply_fusion
  26.6 0.0 copy-done.1
  26.6 0.0 copy-done.2
  26.6 0.1 multiply_add_fusion
  26.6 0.6 %pad_maximum_fusion.1 = f32[4,4,512]{2,1,0:T(4,128)} fusion(f32[1,4,512]{2,1,0:T(4,128)S(1)} %neg.14, f32[3,4,512]{2,1,0:T(4,128)S(1)} %multiply_add_fusion), kind=kLoop, calls=%fused_computation.27 | loop fusion | flops 8192 | bytes 65536 | tf_op jit(solution)/shard_map/concatenate | solution.py:196
  (16 shorter events, 0.4 us)
Async XLA Ops:
  0.0 4.8 %copy-start.3 = (s32[32]{0:T(128)S(1)}, s32[32]{0:T(128)}, u32[]{:S(2)}) copy-start(s32[32]{0:T(128)} %param.9) | copy-start | bytes 388
  0.0 0.7 %copy-start = (s32[16,8,4]{0,2,1:T(4,128)S(1)}, s32[16,8,4]{0,2,1:T(4,128)}, u32[]{:S(2)}) copy-start(s32[16,8,4]{0,2,1:T(4,128)} %param.7) | copy-start | bytes 6148
  4.3 1.9 %collective-permute-start = (f32[3,16,16,128]{3,2,1,0:T(8,128)S(1)}, f32[3,16,16,128]{3,2,1,0:T(8,128)S(1)}, u32[]{:S(2)}, u32[]{:S(2)}) collective-permute-start(f32[3,16,16,128]{3,2,1,0:T(8,128)S(1)} %get-tuple-element.8), channel_id=1, source_target_pairs={{0,1},{1,0},{2,3},{3,2},{4,5},{5,4},{6,7},{7,6},{8,9},{9,8},{10,11... | collective-permute-start | bytes 1179656 | tf_op jit(solution)/shard_map/ppermute | solution.py:145
  6.2 20.3 %copy-start.1 = (f32[3]{0:T(128)S(1)}, f32[3]{0:T(128)}, u32[]{:S(2)}) copy-start(f32[3]{0:T(128)} %param.11) | copy-start | bytes 40
  6.2 20.3 %copy-start.2 = (f32[3]{0:T(128)S(1)}, f32[3]{0:T(128)}, u32[]{:S(2)}) copy-start(f32[3]{0:T(128)} %param.10) | copy-start | bytes 40
  6.4 6.1 %collective-permute-start.1 = (f32[3,4,16,128]{3,2,1,0:T(8,128)S(1)}, f32[3,4,16,128]{3,2,1,0:T(8,128)S(1)}, u32[]{:S(2)}, u32[]{:S(2)}) collective-permute-start(f32[3,4,16,128]{3,2,1,0:T(8,128)S(1)} %get-tuple-element.15), channel_id=1, source_target_pairs={{0,2},{1,3},{2,0},{3,1},{4,6},{5,7},{6,4},{7,5},{8,10},{9,11},{10,... | collective-permute-start | bytes 294920 | tf_op jit(solution)/shard_map/ppermute | solution.py:145
  9.3 5.8 %collective-permute-start.2 = (f32[3,4,16,128]{3,2,1,0:T(8,128)S(1)}, f32[3,4,16,128]{3,2,1,0:T(8,128)S(1)}, u32[]{:S(2)}, u32[]{:S(2)}) collective-permute-start(f32[3,4,16,128]{3,2,1,0:T(8,128)S(1)} %get-tuple-element.14), channel_id=1, source_target_pairs={{0,4},{1,5},{2,6},{3,7},{4,0},{5,1},{6,2},{7,3},{8,12},{9,13},{10,... | collective-permute-start | bytes 294920 | tf_op jit(solution)/shard_map/ppermute | solution.py:145
  10.8 5.5 %collective-permute-start.3 = (f32[3,4,16,128]{3,2,1,0:T(8,128)S(1)}, f32[3,4,16,128]{3,2,1,0:T(8,128)S(1)}, u32[]{:S(2)}, u32[]{:S(2)}) collective-permute-start(f32[3,4,16,128]{3,2,1,0:T(8,128)S(1)} %get-tuple-element.13), channel_id=1, source_target_pairs={{0,6},{1,7},{2,4},{3,5},{4,2},{5,3},{6,0},{7,1},{8,14},{9,15},{10,... | collective-permute-start | bytes 294920 | tf_op jit(solution)/shard_map/ppermute | solution.py:145
  16.5 4.5 %collective-permute-start.4 = (f32[3,1,16,128]{3,2,1,0:T(8,128)S(1)}, f32[3,1,16,128]{3,2,1,0:T(8,128)S(1)}, u32[]{:S(2)}, u32[]{:S(2)}) collective-permute-start(f32[3,1,16,128]{3,2,1,0:T(8,128)S(1)} %get-tuple-element.21), channel_id=1, source_target_pairs={{0,8},{1,9},{2,10},{3,11},{4,12},{5,13},{6,14},{7,15},{8,0},{9,1},... | collective-permute-start | bytes 73736 | tf_op jit(solution)/shard_map/ppermute | solution.py:145
  18.1 4.9 %collective-permute-start.5 = (f32[3,1,16,128]{3,2,1,0:T(8,128)S(1)}, f32[3,1,16,128]{3,2,1,0:T(8,128)S(1)}, u32[]{:S(2)}, u32[]{:S(2)}) collective-permute-start(f32[3,1,16,128]{3,2,1,0:T(8,128)S(1)} %get-tuple-element.23), channel_id=1, source_target_pairs={{0,16},{1,17},{2,18},{3,19},{4,20},{5,21},{6,22},{7,23},{8,24},{9,... | collective-permute-start | bytes 73736 | tf_op jit(solution)/shard_map/ppermute | solution.py:145
  20.7 5.6 %collective-permute-start.6 = (f32[3,1,16,128]{3,2,1,0:T(8,128)S(1)}, f32[3,1,16,128]{3,2,1,0:T(8,128)S(1)}, u32[]{:S(2)}, u32[]{:S(2)}) collective-permute-start(f32[3,1,16,128]{3,2,1,0:T(8,128)S(1)} %get-tuple-element.24), channel_id=1, source_target_pairs={{0,24},{1,25},{2,26},{3,27},{4,28},{5,29},{6,30},{7,31},{8,16},{9,... | collective-permute-start | bytes 73736 | tf_op jit(solution)/shard_map/ppermute | solution.py:145

commit v4 on v3

--- a/solution.py
+++ b/solution.py
@@ -139,19 +139,19 @@
 
 def exchange(pieces, my_slab, my_rank, low, kappa):
     depth_n = lax.axis_size("depth")
-    held = [pieces[0]]
-    for m in range(1, len(pieces)):
+    held = {0: pieces[0]}
+    for m in range(len(pieces) - 1, 0, -1):
         pairs = [(source, source ^ (m << low)) for source in range(depth_n)]
-        held.append(lax.ppermute(pieces[m], "depth", pairs))
+        held[m] = lax.ppermute(pieces[m], "depth", pairs)
     place = my_rank >> low & (len(pieces) - 1)
     colors = 0.0
-    for m, piece in enumerate(held):
+    for m, piece in held.items():
         ahead = 0.0
-        for other, front in enumerate(held):
+        for other, front in held.items():
             if other != m:
                 ahead = ahead + front[2] * ((place ^ other) < (place ^ m)).astype(jnp.float32)
         colors = colors + piece[:2] * jnp.exp(-kappa * ahead)[None]
-    return jnp.concatenate([colors, sum(piece[2:] for piece in held)], axis=0)
+    return jnp.concatenate([colors, sum(piece[2:] for piece in held.values())], axis=0)
 
 
 def on_device(density, clip_flags, band_offset, order, ambient, diffuse):

time: 27.5 us -> 25.4 us (0.924)
  waiting for transfers between devices: 11.4 us -> 9.28 us
    ppermute x7, waiting for transfers between devices: 11.4 us -> 9.28 us  [exchange(): held[m] = lax.ppermute(pieces[m], 'depth', pairs)]
where the time goes in v4:
time: 25.4 us; the launch traced here: 25.2 us
  starting transfers between devices  9.49 us (37%)
  waiting for transfers between devices  9.28 us (37%)
  Pallas kernels  3.56 us (14%)
  other arithmetic  1.13 us (4%)
  between operations  0.9 us (4%)
  local copies, waits for them, and re-layouts  0.81 us (3%)
    ppermute x7, starting transfers between devices, exchange(): held[m] = lax.ppermute(pieces[m], 'depth', pairs)  9.49 us
    ppermute x7, waiting for transfers between devices, exchange(): held[m] = lax.ppermute(pieces[m], 'depth', pairs)  9.28 us
    pallas_call x1, Pallas kernels, composite_slab(): pl.pallas_call(functools.partial(slab_kernel, -kappa * log2e, -extinct *...  3.56 us
    unnamed x9, local copies, waits for them, and re-layouts  0.75 us
    concatenate x1, other arithmetic, on_device(): return jnp.concatenate([colors, alpha[None]], axis=0)  0.63 us
  transfers between devices with their start and end apart: 7, of which 6 were waited for; matrix products, arithmetic and copies ran while one was open for 0% of the time, Pallas kernels for 0%

profile of v4, /device:TPU:0, one launch (start us, length us, event | category | flops | bytes accessed | tf_op | source)
XLA Modules:
  0.0 25.2 jit_solution(14398645838604297739)
XLA Ops:
  0.0 0.0 copy-start.3
  0.0 0.0 copy-start
  0.0 0.7 %copy-done = s32[16,8,4]{0,2,1:T(4,128)S(1)} copy-done((s32[16,8,4]{0,2,1:T(4,128)S(1)}, s32[16,8,4]{0,2,1:T(4,128)}, u32[]{:S(2)}) %copy-start) | copy-done | bytes 2072
  0.7 3.6 %slab.1 = (f32[3,16,16,128]{3,2,1,0:T(8,128)S(1)}, f32[3,16,16,128]{3,2,1,0:T(8,128)S(1)}) custom-call(s32[8,4,16]{2,1,0:T(4,128)S(1)} %bitcast.65, bf16[16,128,512]{2,1,0:T(8,128)(2,1)} %dens_ref.1), custom_call_target="tpu_custom_call" | custom-call | flops 1073741824 | bytes 2097152 | tf_op jit(solution)/shard_map/slab/pallas_call | solution.py:116
  4.3 0.5 %collective-permute-start = (f32[3,16,16,128]{3,2,1,0:T(8,128)S(1)}, f32[3,16,16,128]{3,2,1,0:T(8,128)S(1)}, u32[]{:S(2)}, u32[]{:S(2)}) collective-permute-start(f32[3,16,16,128]{3,2,1,0:T(8,128)S(1)} %get-tuple-element.8), channel_id=1, source_target_pairs={{0,1},{1,0},{2,3},{3,2},{4,5},{5,4},{6,7},{7,6},{8,9},{9,8},{10,11... | collective-permute-start | bytes 1179656 | tf_op jit(solution)/shard_map/ppermute | solution.py:145
  4.8 0.0 copy-done.3
  4.9 1.3 %collective-permute-done = f32[3,16,16,128]{3,2,1,0:T(8,128)S(1)} collective-permute-done((f32[3,16,16,128]{3,2,1,0:T(8,128)S(1)}, f32[3,16,16,128]{3,2,1,0:T(8,128)S(1)}, u32[]{:S(2)}, u32[]{:S(2)}) %collective-permute-start) | collective-permute-done | bytes 393248 | tf_op jit(solution)/shard_map/ppermute | solution.py:145
  6.2 0.0 copy-start.1
  6.2 0.0 copy-start.2
  6.2 0.1 fusion
  6.4 3.9 %collective-permute-start.1 = (f32[3,4,16,128]{3,2,1,0:T(8,128)S(1)}, f32[3,4,16,128]{3,2,1,0:T(8,128)S(1)}, u32[]{:S(2)}, u32[]{:S(2)}) collective-permute-start(f32[3,4,16,128]{3,2,1,0:T(8,128)S(1)} %get-tuple-element.15), channel_id=1, source_target_pairs={{0,6},{1,7},{2,4},{3,5},{4,2},{5,3},{6,0},{7,1},{8,14},{9,15},{10,... | collective-permute-start | bytes 294920 | tf_op jit(solution)/shard_map/ppermute | solution.py:145
  10.3 0.5 %collective-permute-start.2 = (f32[3,4,16,128]{3,2,1,0:T(8,128)S(1)}, f32[3,4,16,128]{3,2,1,0:T(8,128)S(1)}, u32[]{:S(2)}, u32[]{:S(2)}) collective-permute-start(f32[3,4,16,128]{3,2,1,0:T(8,128)S(1)} %get-tuple-element.14), channel_id=1, source_target_pairs={{0,4},{1,5},{2,6},{3,7},{4,0},{5,1},{6,2},{7,3},{8,12},{9,13},{10,... | collective-permute-start | bytes 294920 | tf_op jit(solution)/shard_map/ppermute | solution.py:145
  10.8 0.1 collective-permute-start.3
  11.6 1.9 %collective-permute-done.1 = f32[3,4,16,128]{3,2,1,0:T(8,128)S(1)} collective-permute-done((f32[3,4,16,128]{3,2,1,0:T(8,128)S(1)}, f32[3,4,16,128]{3,2,1,0:T(8,128)S(1)}, u32[]{:S(2)}, u32[]{:S(2)}) %collective-permute-start.1) | collective-permute-done | bytes 98336 | tf_op jit(solution)/shard_map/ppermute | solution.py:145
  13.5 2.0 %collective-permute-done.2 = f32[3,4,16,128]{3,2,1,0:T(8,128)S(1)} collective-permute-done((f32[3,4,16,128]{3,2,1,0:T(8,128)S(1)}, f32[3,4,16,128]{3,2,1,0:T(8,128)S(1)}, u32[]{:S(2)}, u32[]{:S(2)}) %collective-permute-start.2) | collective-permute-done | bytes 98336 | tf_op jit(solution)/shard_map/ppermute | solution.py:145
  15.5 0.2 collective-permute-done.3
  15.9 3.7 %collective-permute-start.4 = (f32[3,1,16,128]{3,2,1,0:T(8,128)S(1)}, f32[3,1,16,128]{3,2,1,0:T(8,128)S(1)}, u32[]{:S(2)}, u32[]{:S(2)}) collective-permute-start(f32[3,1,16,128]{3,2,1,0:T(8,128)S(1)} %get-tuple-element.21), channel_id=1, source_target_pairs={{0,24},{1,25},{2,26},{3,27},{4,28},{5,29},{6,30},{7,31},{8,16},{9,... | collective-permute-start | bytes 73736 | tf_op jit(solution)/shard_map/ppermute | solution.py:145
  19.5 0.0 collective-permute-start.5
  19.5 0.8 %collective-permute-start.6 = (f32[3,1,16,128]{3,2,1,0:T(8,128)S(1)}, f32[3,1,16,128]{3,2,1,0:T(8,128)S(1)}, u32[]{:S(2)}, u32[]{:S(2)}) collective-permute-start(f32[3,1,16,128]{3,2,1,0:T(8,128)S(1)} %get-tuple-element.24), channel_id=1, source_target_pairs={{0,8},{1,9},{2,10},{3,11},{4,12},{5,13},{6,14},{7,15},{8,0},{9,1},... | collective-permute-start | bytes 73736 | tf_op jit(solution)/shard_map/ppermute | solution.py:145
  20.4 1.2 %collective-permute-done.4 = f32[3,1,16,128]{3,2,1,0:T(8,128)S(1)} collective-permute-done((f32[3,1,16,128]{3,2,1,0:T(8,128)S(1)}, f32[3,1,16,128]{3,2,1,0:T(8,128)S(1)}, u32[]{:S(2)}, u32[]{:S(2)}) %collective-permute-start.4) | collective-permute-done | bytes 24608 | tf_op jit(solution)/shard_map/ppermute | solution.py:145
  21.6 2.7 %collective-permute-done.5 = f32[3,1,16,128]{3,2,1,0:T(8,128)S(1)} collective-permute-done((f32[3,1,16,128]{3,2,1,0:T(8,128)S(1)}, f32[3,1,16,128]{3,2,1,0:T(8,128)S(1)}, u32[]{:S(2)}, u32[]{:S(2)}) %collective-permute-start.5) | collective-permute-done | bytes 24608 | tf_op jit(solution)/shard_map/ppermute | solution.py:145
  24.3 0.0 collective-permute-done.6
  24.4 0.1 bitcast_multiply_fusion
  24.5 0.0 copy-done.1
  24.5 0.0 copy-done.2
  24.5 0.1 multiply_add_fusion
  24.6 0.6 %pad_maximum_fusion.1 = f32[4,4,512]{2,1,0:T(4,128)} fusion(f32[1,4,512]{2,1,0:T(4,128)S(1)} %neg.14, f32[3,4,512]{2,1,0:T(4,128)S(1)} %multiply_add_fusion), kind=kLoop, calls=%fused_computation.27 | loop fusion | flops 8192 | bytes 65536 | tf_op jit(solution)/shard_map/concatenate | solution.py:196
  (16 shorter events, 0.4 us)
Async XLA Ops:
  0.0 4.8 %copy-start.3 = (s32[32]{0:T(128)S(1)}, s32[32]{0:T(128)}, u32[]{:S(2)}) copy-start(s32[32]{0:T(128)} %param.9) | copy-start | bytes 388
  0.0 0.7 %copy-start = (s32[16,8,4]{0,2,1:T(4,128)S(1)}, s32[16,8,4]{0,2,1:T(4,128)}, u32[]{:S(2)}) copy-start(s32[16,8,4]{0,2,1:T(4,128)} %param.7) | copy-start | bytes 6148
  4.3 1.9 %collective-permute-start = (f32[3,16,16,128]{3,2,1,0:T(8,128)S(1)}, f32[3,16,16,128]{3,2,1,0:T(8,128)S(1)}, u32[]{:S(2)}, u32[]{:S(2)}) collective-permute-start(f32[3,16,16,128]{3,2,1,0:T(8,128)S(1)} %get-tuple-element.8), channel_id=1, source_target_pairs={{0,1},{1,0},{2,3},{3,2},{4,5},{5,4},{6,7},{7,6},{8,9},{9,8},{10,11... | collective-permute-start | bytes 1179656 | tf_op jit(solution)/shard_map/ppermute | solution.py:145
  6.2 18.3 %copy-start.1 = (f32[3]{0:T(128)S(1)}, f32[3]{0:T(128)}, u32[]{:S(2)}) copy-start(f32[3]{0:T(128)} %param.11) | copy-start | bytes 40
  6.2 18.2 %copy-start.2 = (f32[3]{0:T(128)S(1)}, f32[3]{0:T(128)}, u32[]{:S(2)}) copy-start(f32[3]{0:T(128)} %param.10) | copy-start | bytes 40
  6.4 7.1 %collective-permute-start.1 = (f32[3,4,16,128]{3,2,1,0:T(8,128)S(1)}, f32[3,4,16,128]{3,2,1,0:T(8,128)S(1)}, u32[]{:S(2)}, u32[]{:S(2)}) collective-permute-start(f32[3,4,16,128]{3,2,1,0:T(8,128)S(1)} %get-tuple-element.15), channel_id=1, source_target_pairs={{0,6},{1,7},{2,4},{3,5},{4,2},{5,3},{6,0},{7,1},{8,14},{9,15},{10,... | collective-permute-start | bytes 294920 | tf_op jit(solution)/shard_map/ppermute | solution.py:145
  10.3 5.2 %collective-permute-start.2 = (f32[3,4,16,128]{3,2,1,0:T(8,128)S(1)}, f32[3,4,16,128]{3,2,1,0:T(8,128)S(1)}, u32[]{:S(2)}, u32[]{:S(2)}) collective-permute-start(f32[3,4,16,128]{3,2,1,0:T(8,128)S(1)} %get-tuple-element.14), channel_id=1, source_target_pairs={{0,4},{1,5},{2,6},{3,7},{4,0},{5,1},{6,2},{7,3},{8,12},{9,13},{10,... | collective-permute-start | bytes 294920 | tf_op jit(solution)/shard_map/ppermute | solution.py:145
  10.8 4.9 %collective-permute-start.3 = (f32[3,4,16,128]{3,2,1,0:T(8,128)S(1)}, f32[3,4,16,128]{3,2,1,0:T(8,128)S(1)}, u32[]{:S(2)}, u32[]{:S(2)}) collective-permute-start(f32[3,4,16,128]{3,2,1,0:T(8,128)S(1)} %get-tuple-element.13), channel_id=1, source_target_pairs={{0,2},{1,3},{2,0},{3,1},{4,6},{5,7},{6,4},{7,5},{8,10},{9,11},{10,... | collective-permute-start | bytes 294920 | tf_op jit(solution)/shard_map/ppermute | solution.py:145
  15.9 5.7 %collective-permute-start.4 = (f32[3,1,16,128]{3,2,1,0:T(8,128)S(1)}, f32[3,1,16,128]{3,2,1,0:T(8,128)S(1)}, u32[]{:S(2)}, u32[]{:S(2)}) collective-permute-start(f32[3,1,16,128]{3,2,1,0:T(8,128)S(1)} %get-tuple-element.21), channel_id=1, source_target_pairs={{0,24},{1,25},{2,26},{3,27},{4,28},{5,29},{6,30},{7,31},{8,16},{9,... | collective-permute-start | bytes 73736 | tf_op jit(solution)/shard_map/ppermute | solution.py:145
  19.5 4.7 %collective-permute-start.5 = (f32[3,1,16,128]{3,2,1,0:T(8,128)S(1)}, f32[3,1,16,128]{3,2,1,0:T(8,128)S(1)}, u32[]{:S(2)}, u32[]{:S(2)}) collective-permute-start(f32[3,1,16,128]{3,2,1,0:T(8,128)S(1)} %get-tuple-element.23), channel_id=1, source_target_pairs={{0,16},{1,17},{2,18},{3,19},{4,20},{5,21},{6,22},{7,23},{8,24},{9,... | collective-permute-start | bytes 73736 | tf_op jit(solution)/shard_map/ppermute | solution.py:145
  19.5 4.7 %collective-permute-start.6 = (f32[3,1,16,128]{3,2,1,0:T(8,128)S(1)}, f32[3,1,16,128]{3,2,1,0:T(8,128)S(1)}, u32[]{:S(2)}, u32[]{:S(2)}) collective-permute-start(f32[3,1,16,128]{3,2,1,0:T(8,128)S(1)} %get-tuple-element.24), channel_id=1, source_target_pairs={{0,8},{1,9},{2,10},{3,11},{4,12},{5,13},{6,14},{7,15},{8,0},{9,1},... | collective-permute-start | bytes 73736 | tf_op jit(solution)/shard_map/ppermute | solution.py:145

commit v5 on v4

--- a/solution.py
+++ b/solution.py
@@ -31,8 +31,8 @@
     blocks_r, blocks_x = flags.shape[:2]
     band = rows // blocks_r
     width = cells // blocks_x
-    span = upper.shape[0]
-    group = masked.shape[2] // band
+    span = math.gcd(cells, 2 * LANES)
+    group = masked.shape[1] // band
     tall = group * band
     shares = band // share_rows
 
@@ -45,7 +45,7 @@
     for step in range(rows // tall):
         copy(step).start()
     upper[...] = (
-        lax.broadcasted_iota(jnp.int32, (span, span), 0) < lax.broadcasted_iota(jnp.int32, (span, span), 1)
+        lax.broadcasted_iota(jnp.int32, (cells, cells), 0) < lax.broadcasted_iota(jnp.int32, (cells, cells), 1)
     ).astype(jnp.float32).astype(jnp.bfloat16)
     odd = lax.axis_index("depth") & 1 == 1
     flag_copy.wait()
@@ -59,31 +59,31 @@
                 for z in range(slices):
                     flag = flags[block, j, z].astype(jnp.float32)
                     flag = jnp.full((band, width), flag, jnp.float32).astype(jnp.bfloat16)
-                    masked[j * width // span, z, g * band : (g + 1) * band, j * width % span : j * width % span + width] = (
-                        dens[z, at, j * width : (j + 1) * width] * flag
-                    )
-        lhs = masked[...].reshape(cells // span * slices * tall, span)
-        inside[...] = jnp.dot(lhs, upper[...], preferred_element_type=jnp.float32).reshape(inside.shape)
+                    cols = slice(j * width, (j + 1) * width)
+                    masked[z, g * band : (g + 1) * band, cols] = dens[z, at, cols] * flag
+        for h in range(cells // span):
+            lhs = masked[:, :, : (h + 1) * span].reshape(slices * tall, (h + 1) * span)
+            cols = slice(h * span, (h + 1) * span)
+            inside[:, :, cols] = jnp.dot(
+                lhs, upper[: (h + 1) * span, cols], preferred_element_type=jnp.float32
+            ).reshape(slices, tall, span)
         for g in range(group):
             sub = slice(g * band, (g + 1) * band)
             at = pl.ds(pl.multiple_of((step * group + g) * band, band), band)
             outs = []
             for j in range(cells // LANES):
-                h, first = j * LANES // span, j * LANES % span
-                cols = slice(first, first + LANES)
+                cols = slice(j * LANES, (j + 1) * LANES)
                 before = jnp.zeros((band, LANES), jnp.float32)
                 through = jnp.ones((band, LANES), jnp.float32)
                 base = jnp.zeros((band, LANES), jnp.float32)
                 lit = jnp.zeros((band, LANES), jnp.float32)
                 for z in range(slices):
-                    clipped = masked[h, z, sub, cols].astype(jnp.float32)
+                    clipped = masked[z, sub, cols].astype(jnp.float32)
                     before = before + clipped
                     behind = jnp.exp2(before * depth_scale)
                     emitted = clipped * (through - behind)
                     through = behind
-                    shade = inside[h, z, sub, cols]
-                    for left in range(h):
-                        shade = shade + inside[left, z, sub, span - 1 : span] + masked[left, z, sub, span - 1 : span].astype(jnp.float32)
+                    shade = inside[z, sub, cols]
                     if has_nearer:
                         shade = shade + nearer_ref[z, at, :]
                     base = base + emitted
@@ -110,7 +110,6 @@
     half = (3, depth_n // 2, share_rows * cells // LANES, LANES)
     log2e = math.log2(math.e)
     has_nearer = nearer is not None
-    span = math.gcd(cells, 2 * LANES)
     tall = math.gcd(blocks_r, 2) * rows // blocks_r
     vmem = pl.BlockSpec(memory_space=pltpu.VMEM)
     return pl.pallas_call(
@@ -120,9 +119,9 @@
         out_specs=[vmem, vmem],
         scratch_shapes=[
             pltpu.VMEM((slices, rows, cells), jnp.bfloat16),
-            pltpu.VMEM((cells // span, slices, tall, span), jnp.bfloat16),
-            pltpu.VMEM((cells // span, slices, tall, span), jnp.float32),
-            pltpu.VMEM((span, span), jnp.bfloat16),
+            pltpu.VMEM((slices, tall, cells), jnp.bfloat16),
+            pltpu.VMEM((slices, tall, cells), jnp.float32),
+            pltpu.VMEM((cells, cells), jnp.bfloat16),
             pltpu.SMEM((blocks_r, blocks_x, slices), jnp.int32),
             pltpu.SemaphoreType.DMA((rows // tall,)),
             pltpu.SemaphoreType.DMA,
@@ -134,7 +133,7 @@
             transcendentals=2 * slices * rows * cells,
         ),
         name="slab",
-    )(clip_flags.transpose(1, 2, 0), pltpu.with_memory_space_constraint(density, pltpu.HBM), *([nearer] if has_nearer else []))
+    )(pltpu.with_memory_space_constraint(clip_flags.transpose(1, 2, 0), pltpu.HBM), pltpu.with_memory_space_constraint(density, pltpu.HBM), *([nearer] if has_nearer else []))
 
 
 def exchange(pieces, my_slab, my_rank, low, kappa):

time: 25.4 us -> 24.5 us (0.965)
  local copies, waits for them, and re-layouts: 0.81 us -> 0.08 us
    unnamed x9 -> x7, local copies, waits for them, and re-layouts: 0.75 us -> 0.02 us
where the time goes in v5:
time: 24.5 us; the launch traced here: 24.4 us
  starting transfers between devices  9.5 us (39%)
  waiting for transfers between devices  9.29 us (38%)
  Pallas kernels  3.47 us (14%)
  other arithmetic  1.13 us (5%)
  between operations  0.9 us (4%)
    ppermute x7, starting transfers between devices, exchange(): held[m] = lax.ppermute(pieces[m], 'depth', pairs)  9.5 us
    ppermute x7, waiting for transfers between devices, exchange(): held[m] = lax.ppermute(pieces[m], 'depth', pairs)  9.29 us
    pallas_call x1, Pallas kernels, composite_slab(): pl.pallas_call(functools.partial(slab_kernel, -kappa * log2e, -extinct *...  3.47 us
    concatenate x1, other arithmetic, on_device(): return jnp.concatenate([colors, alpha[None]], axis=0)  0.63 us
  transfers between devices with their start and end apart: 7, of which 6 were waited for; matrix products, arithmetic and copies ran while one was open for 0% of the time, Pallas kernels for 0%

profile of v5, /device:TPU:0, one launch (start us, length us, event | category | flops | bytes accessed | tf_op | source)
XLA Modules:
  0.0 24.4 jit_solution(8100183758289754615)
XLA Ops:
  0.0 0.0 copy-start.2
  0.0 3.5 %slab.1 = (f32[3,16,16,128]{3,2,1,0:T(8,128)S(1)}, f32[3,16,16,128]{3,2,1,0:T(8,128)S(1)}) custom-call(s32[8,4,16]{2,1,0:T(4,128)} %bitcast.71, bf16[16,128,512]{2,1,0:T(8,128)(2,1)} %dens_ref.1), custom_call_target="tpu_custom_call" | custom-call | flops 1073741824 | bytes 2097152 | tf_op jit(solution)/shard_map/slab/pallas_call | solution.py:115
  3.5 0.5 %collective-permute-start = (f32[3,16,16,128]{3,2,1,0:T(8,128)S(1)}, f32[3,16,16,128]{3,2,1,0:T(8,128)S(1)}, u32[]{:S(2)}, u32[]{:S(2)}) collective-permute-start(f32[3,16,16,128]{3,2,1,0:T(8,128)S(1)} %get-tuple-element.8), channel_id=1, source_target_pairs={{0,1},{1,0},{2,3},{3,2},{4,5},{5,4},{6,7},{7,6},{8,9},{9,8},{10,11... | collective-permute-start | bytes 1179656 | tf_op jit(solution)/shard_map/ppermute | solution.py:144
  4.0 0.0 copy-done.2
  4.1 1.3 %collective-permute-done = f32[3,16,16,128]{3,2,1,0:T(8,128)S(1)} collective-permute-done((f32[3,16,16,128]{3,2,1,0:T(8,128)S(1)}, f32[3,16,16,128]{3,2,1,0:T(8,128)S(1)}, u32[]{:S(2)}, u32[]{:S(2)}) %collective-permute-start) | collective-permute-done | bytes 393248 | tf_op jit(solution)/shard_map/ppermute | solution.py:144
  5.4 0.0 copy-start
  5.4 0.0 copy-start.1
  5.4 0.1 fusion
  5.6 3.9 %collective-permute-start.1 = (f32[3,4,16,128]{3,2,1,0:T(8,128)S(1)}, f32[3,4,16,128]{3,2,1,0:T(8,128)S(1)}, u32[]{:S(2)}, u32[]{:S(2)}) collective-permute-start(f32[3,4,16,128]{3,2,1,0:T(8,128)S(1)} %get-tuple-element.15), channel_id=1, source_target_pairs={{0,6},{1,7},{2,4},{3,5},{4,2},{5,3},{6,0},{7,1},{8,14},{9,15},{10,... | collective-permute-start | bytes 294920 | tf_op jit(solution)/shard_map/ppermute | solution.py:144
  9.4 0.5 %collective-permute-start.2 = (f32[3,4,16,128]{3,2,1,0:T(8,128)S(1)}, f32[3,4,16,128]{3,2,1,0:T(8,128)S(1)}, u32[]{:S(2)}, u32[]{:S(2)}) collective-permute-start(f32[3,4,16,128]{3,2,1,0:T(8,128)S(1)} %get-tuple-element.14), channel_id=1, source_target_pairs={{0,4},{1,5},{2,6},{3,7},{4,0},{5,1},{6,2},{7,3},{8,12},{9,13},{10,... | collective-permute-start | bytes 294920 | tf_op jit(solution)/shard_map/ppermute | solution.py:144
  10.0 0.1 collective-permute-start.3
  10.8 1.9 %collective-permute-done.1 = f32[3,4,16,128]{3,2,1,0:T(8,128)S(1)} collective-permute-done((f32[3,4,16,128]{3,2,1,0:T(8,128)S(1)}, f32[3,4,16,128]{3,2,1,0:T(8,128)S(1)}, u32[]{:S(2)}, u32[]{:S(2)}) %collective-permute-start.1) | collective-permute-done | bytes 98336 | tf_op jit(solution)/shard_map/ppermute | solution.py:144
  12.6 2.0 %collective-permute-done.2 = f32[3,4,16,128]{3,2,1,0:T(8,128)S(1)} collective-permute-done((f32[3,4,16,128]{3,2,1,0:T(8,128)S(1)}, f32[3,4,16,128]{3,2,1,0:T(8,128)S(1)}, u32[]{:S(2)}, u32[]{:S(2)}) %collective-permute-start.2) | collective-permute-done | bytes 98336 | tf_op jit(solution)/shard_map/ppermute | solution.py:144
  14.7 0.2 collective-permute-done.3
  15.0 3.7 %collective-permute-start.4 = (f32[3,1,16,128]{3,2,1,0:T(8,128)S(1)}, f32[3,1,16,128]{3,2,1,0:T(8,128)S(1)}, u32[]{:S(2)}, u32[]{:S(2)}) collective-permute-start(f32[3,1,16,128]{3,2,1,0:T(8,128)S(1)} %get-tuple-element.21), channel_id=1, source_target_pairs={{0,24},{1,25},{2,26},{3,27},{4,28},{5,29},{6,30},{7,31},{8,16},{9,... | collective-permute-start | bytes 73736 | tf_op jit(solution)/shard_map/ppermute | solution.py:144
  18.7 0.0 collective-permute-start.5
  18.7 0.8 %collective-permute-start.6 = (f32[3,1,16,128]{3,2,1,0:T(8,128)S(1)}, f32[3,1,16,128]{3,2,1,0:T(8,128)S(1)}, u32[]{:S(2)}, u32[]{:S(2)}) collective-permute-start(f32[3,1,16,128]{3,2,1,0:T(8,128)S(1)} %get-tuple-element.24), channel_id=1, source_target_pairs={{0,8},{1,9},{2,10},{3,11},{4,12},{5,13},{6,14},{7,15},{8,0},{9,1},... | collective-permute-start | bytes 73736 | tf_op jit(solution)/shard_map/ppermute | solution.py:144
  19.6 1.2 %collective-permute-done.4 = f32[3,1,16,128]{3,2,1,0:T(8,128)S(1)} collective-permute-done((f32[3,1,16,128]{3,2,1,0:T(8,128)S(1)}, f32[3,1,16,128]{3,2,1,0:T(8,128)S(1)}, u32[]{:S(2)}, u32[]{:S(2)}) %collective-permute-start.4) | collective-permute-done | bytes 24608 | tf_op jit(solution)/shard_map/ppermute | solution.py:144
  20.7 2.7 %collective-permute-done.5 = f32[3,1,16,128]{3,2,1,0:T(8,128)S(1)} collective-permute-done((f32[3,1,16,128]{3,2,1,0:T(8,128)S(1)}, f32[3,1,16,128]{3,2,1,0:T(8,128)S(1)}, u32[]{:S(2)}, u32[]{:S(2)}) %collective-permute-start.5) | collective-permute-done | bytes 24608 | tf_op jit(solution)/shard_map/ppermute | solution.py:144
  23.4 0.0 collective-permute-done.6
  23.6 0.1 bitcast_multiply_fusion
  23.7 0.0 copy-done
  23.7 0.0 copy-done.1
  23.7 0.1 multiply_add_fusion
  23.7 0.6 %pad_maximum_fusion.1 = f32[4,4,512]{2,1,0:T(4,128)} fusion(f32[1,4,512]{2,1,0:T(4,128)S(1)} %neg.14, f32[3,4,512]{2,1,0:T(4,128)S(1)} %multiply_add_fusion), kind=kLoop, calls=%fused_computation.27 | loop fusion | flops 8192 | bytes 65536 | tf_op jit(solution)/shard_map/concatenate | solution.py:195
  (16 shorter events, 0.4 us)
Async XLA Ops:
  0.0 4.0 %copy-start.2 = (s32[32]{0:T(128)S(1)}, s32[32]{0:T(128)}, u32[]{:S(2)}) copy-start(s32[32]{0:T(128)} %param.9) | copy-start | bytes 388
  3.5 1.9 %collective-permute-start = (f32[3,16,16,128]{3,2,1,0:T(8,128)S(1)}, f32[3,16,16,128]{3,2,1,0:T(8,128)S(1)}, u32[]{:S(2)}, u32[]{:S(2)}) collective-permute-start(f32[3,16,16,128]{3,2,1,0:T(8,128)S(1)} %get-tuple-element.8), channel_id=1, source_target_pairs={{0,1},{1,0},{2,3},{3,2},{4,5},{5,4},{6,7},{7,6},{8,9},{9,8},{10,11... | collective-permute-start | bytes 1179656 | tf_op jit(solution)/shard_map/ppermute | solution.py:144
  5.4 18.3 %copy-start = (f32[3]{0:T(128)S(1)}, f32[3]{0:T(128)}, u32[]{:S(2)}) copy-start(f32[3]{0:T(128)} %param.11) | copy-start | bytes 40
  5.4 18.2 %copy-start.1 = (f32[3]{0:T(128)S(1)}, f32[3]{0:T(128)}, u32[]{:S(2)}) copy-start(f32[3]{0:T(128)} %param.10) | copy-start | bytes 40
  5.6 7.1 %collective-permute-start.1 = (f32[3,4,16,128]{3,2,1,0:T(8,128)S(1)}, f32[3,4,16,128]{3,2,1,0:T(8,128)S(1)}, u32[]{:S(2)}, u32[]{:S(2)}) collective-permute-start(f32[3,4,16,128]{3,2,1,0:T(8,128)S(1)} %get-tuple-element.15), channel_id=1, source_target_pairs={{0,6},{1,7},{2,4},{3,5},{4,2},{5,3},{6,0},{7,1},{8,14},{9,15},{10,... | collective-permute-start | bytes 294920 | tf_op jit(solution)/shard_map/ppermute | solution.py:144
  9.4 5.2 %collective-permute-start.2 = (f32[3,4,16,128]{3,2,1,0:T(8,128)S(1)}, f32[3,4,16,128]{3,2,1,0:T(8,128)S(1)}, u32[]{:S(2)}, u32[]{:S(2)}) collective-permute-start(f32[3,4,16,128]{3,2,1,0:T(8,128)S(1)} %get-tuple-element.14), channel_id=1, source_target_pairs={{0,4},{1,5},{2,6},{3,7},{4,0},{5,1},{6,2},{7,3},{8,12},{9,13},{10,... | collective-permute-start | bytes 294920 | tf_op jit(solution)/shard_map/ppermute | solution.py:144
  10.0 4.9 %collective-permute-start.3 = (f32[3,4,16,128]{3,2,1,0:T(8,128)S(1)}, f32[3,4,16,128]{3,2,1,0:T(8,128)S(1)}, u32[]{:S(2)}, u32[]{:S(2)}) collective-permute-start(f32[3,4,16,128]{3,2,1,0:T(8,128)S(1)} %get-tuple-element.13), channel_id=1, source_target_pairs={{0,2},{1,3},{2,0},{3,1},{4,6},{5,7},{6,4},{7,5},{8,10},{9,11},{10,... | collective-permute-start | bytes 294920 | tf_op jit(solution)/shard_map/ppermute | solution.py:144
  15.0 5.7 %collective-permute-start.4 = (f32[3,1,16,128]{3,2,1,0:T(8,128)S(1)}, f32[3,1,16,128]{3,2,1,0:T(8,128)S(1)}, u32[]{:S(2)}, u32[]{:S(2)}) collective-permute-start(f32[3,1,16,128]{3,2,1,0:T(8,128)S(1)} %get-tuple-element.21), channel_id=1, source_target_pairs={{0,24},{1,25},{2,26},{3,27},{4,28},{5,29},{6,30},{7,31},{8,16},{9,... | collective-permute-start | bytes 73736 | tf_op jit(solution)/shard_map/ppermute | solution.py:144
  18.7 4.7 %collective-permute-start.5 = (f32[3,1,16,128]{3,2,1,0:T(8,128)S(1)}, f32[3,1,16,128]{3,2,1,0:T(8,128)S(1)}, u32[]{:S(2)}, u32[]{:S(2)}) collective-permute-start(f32[3,1,16,128]{3,2,1,0:T(8,128)S(1)} %get-tuple-element.23), channel_id=1, source_target_pairs={{0,16},{1,17},{2,18},{3,19},{4,20},{5,21},{6,22},{7,23},{8,24},{9,... | collective-permute-start | bytes 73736 | tf_op jit(solution)/shard_map/ppermute | solution.py:144
  18.7 4.7 %collective-permute-start.6 = (f32[3,1,16,128]{3,2,1,0:T(8,128)S(1)}, f32[3,1,16,128]{3,2,1,0:T(8,128)S(1)}, u32[]{:S(2)}, u32[]{:S(2)}) collective-permute-start(f32[3,1,16,128]{3,2,1,0:T(8,128)S(1)} %get-tuple-element.24), channel_id=1, source_target_pairs={{0,8},{1,9},{2,10},{3,11},{4,12},{5,13},{6,14},{7,15},{8,0},{9,1},... | collective-permute-start | bytes 73736 | tf_op jit(solution)/shard_map/ppermute | solution.py:144

commit v6 on v5

--- a/solution.py
+++ b/solution.py
@@ -133,24 +133,91 @@
             transcendentals=2 * slices * rows * cells,
         ),
         name="slab",
-    )(pltpu.with_memory_space_constraint(clip_flags.transpose(1, 2, 0), pltpu.HBM), pltpu.with_memory_space_constraint(density, pltpu.HBM), *([nearer] if has_nearer else []))
-
-
-def exchange(pieces, my_slab, my_rank, low, kappa):
+    )(
+        pltpu.with_memory_space_constraint(clip_flags.transpose(1, 2, 0), pltpu.HBM),
+        pltpu.with_memory_space_constraint(density, pltpu.HBM),
+        *([nearer] if has_nearer else []),
+    )
+
+
+def step_of(position, hop, count, ring):
+    if ring:
+        turn = ((position & 1) << 1 | position >> 1) + hop & 3
+        return (turn & 1) << 1 | turn >> 1
+    return position ^ hop
+
+
+def sending_order(count, ring):
+    if count < 4:
+        return (1,)
+    return (1, 3, 2) if ring else (3, 2, 1)
+
+
+def sent_and_held(pieces, low, ring):
     depth_n = lax.axis_size("depth")
-    held = {0: pieces[0]}
-    for m in range(len(pieces) - 1, 0, -1):
-        pairs = [(source, source ^ (m << low)) for source in range(depth_n)]
-        held[m] = lax.ppermute(pieces[m], "depth", pairs)
-    place = my_rank >> low & (len(pieces) - 1)
-    colors = 0.0
-    for m, piece in held.items():
+    count = len(pieces)
+    held = []
+    for hop in sending_order(count, ring):
+        pairs = []
+        for source in range(depth_n):
+            position = source >> low & (count - 1)
+            pairs.append((source, source + ((step_of(position, hop, count, ring) - position) << low)))
+        held.append(lax.ppermute(pieces[hop], "depth", pairs))
+    return [*held, pieces[0]]
+
+
+def over(kappa, places, held):
+    base, lit, column = 0.0, 0.0, 0.0
+    for place, piece in zip(places, held):
         ahead = 0.0
-        for other, front in held.items():
-            if other != m:
-                ahead = ahead + front[2] * ((place ^ other) < (place ^ m)).astype(jnp.float32)
-        colors = colors + piece[:2] * jnp.exp(-kappa * ahead)[None]
-    return jnp.concatenate([colors, sum(piece[2:] for piece in held.values())], axis=0)
+        for other, front in zip(places, held):
+            if front is not piece:
+                ahead = ahead + jnp.where(other < place, front[2], 0.0)
+        passed = jnp.exp(-kappa * ahead)
+        base = base + piece[0] * passed
+        lit = lit + piece[1] * passed
+        column = column + piece[2]
+    return base, lit, column
+
+
+def places_of(order_ref, low, count, ring):
+    mine = lax.axis_index("depth") >> low & (count - 1)
+    flips = order_ref[0:1, 0:1] >> low & (count - 1)
+    return [flips ^ step_of(mine, -hop if ring else hop, count, ring) for hop in (*sending_order(count, ring), 0)]
+
+
+def merge_kernel(kappa, low, count, ring, next_ring, order_ref, *refs):
+    held, out = refs[:count], refs[count:]
+    places = places_of(order_ref, low, count, ring)
+    fan = len(out)
+    mine = lax.axis_index("depth") >> (low + count.bit_length() - 1) & (fan - 1)
+    for hop in range(fan):
+        for row in range(out[hop].shape[1]):
+            at = row * fan + step_of(mine, hop, fan, next_ring)
+            merged = over(kappa, places, [[piece[channel, at] for channel in range(3)] for piece in held])
+            for channel in range(3):
+                out[hop][channel, row] = merged[channel]
+
+
+def opacity(depth):
+    series = 1.0 - depth * (1.0 / 6.0)
+    for term in (5.0, 4.0, 3.0, 2.0):
+        series = 1.0 - depth * (1.0 / term) * series
+    return jnp.where(depth < 0.125, depth * series, 1.0 - jnp.exp(-depth))
+
+
+def finish_kernel(kappa, low, count, ring, order_ref, glow_ref, *refs):
+    held, image = refs[:count], refs[count]
+    places = places_of(order_ref, low, count, ring)
+    base, lit, column = over(kappa, places, [[piece[channel, 0] for channel in range(3)] for piece in held])
+    share_rows = image.shape[1]
+    for channel in range(4):
+        if channel < 3:
+            value = glow_ref[0, channel] * base + glow_ref[1, channel] * lit
+        else:
+            value = opacity(kappa * column)
+        for j in range(image.shape[2] // LANES):
+            image[channel, :, j * LANES : (j + 1) * LANES] = value[j * share_rows : (j + 1) * share_rows]
 
 
 def on_device(density, clip_flags, band_offset, order, ambient, diffuse):
@@ -162,7 +229,6 @@
     share_rows = rows // depth_n
     levels = depth_n.bit_length() - 1
     my_slab = lax.axis_index("depth")
-    my_rank = my_slab ^ order[0]
     nearer = None
     if xs_n > 1:
         blocks_r, blocks_x = clip_flags.shape[1:]
@@ -173,26 +239,40 @@
         totals = jnp.sum(totals, axis=3).reshape(slices, rows)
         nearer = prefix(totals, "xs", lambda early, late: early + late, jnp.zeros_like(totals))
         nearer = nearer[:, :, None]
-    pieces = composite_slab(clip_flags, density, nearer, kappa, extinct, depth_n)
-    share = exchange(pieces, my_slab, my_rank, 0, kappa)
-    low = 1
-    while low < levels:
-        count = 4 if low + 1 < levels else 2
-        split = share.reshape(3, share.shape[1] // count, count, *share.shape[2:])
-        mine = my_slab >> low & (count - 1)
-        pieces = [
-            lax.dynamic_index_in_dim(split, mine ^ m, axis=2, keepdims=False) for m in range(count)
-        ]
-        share = exchange(pieces, my_slab, my_rank, low, kappa)
-        low += count.bit_length() - 1
-    share = share.reshape(3, cells // LANES, share_rows, LANES)
-    share = share.transpose(0, 2, 1, 3).reshape(3, share_rows, cells)
+    held = sent_and_held(composite_slab(clip_flags, density, nearer, kappa, extinct, depth_n), 0, False)
+    first = order[None]
+    vmem = pl.BlockSpec(memory_space=pltpu.VMEM)
+    low, ring = 0, False
+    while True:
+        count = len(held)
+        through = low + count.bit_length() - 1
+        if through == levels:
+            break
+        fan = 4 if through + 1 < levels else 2
+        next_ring = low > 0 and fan == 4
+        shape = (3, held[0].shape[1] // fan, *held[0].shape[2:])
+        pieces = pl.pallas_call(
+            functools.partial(merge_kernel, kappa, low, count, ring, next_ring),
+            out_shape=[pltpu.VMEM(shape, jnp.float32)] * fan,
+            in_specs=[vmem] * (1 + count),
+            out_specs=[vmem] * fan,
+            compiler_params=pltpu.CompilerParams(vmem_limit_bytes=4 * 2**20),
+            name="merge",
+        )(first, *held)
+        low, ring = through, next_ring
+        held = sent_and_held(pieces, low, ring)
     row_pos = band_offset[0] + my_slab * share_rows + jnp.arange(share_rows, dtype=jnp.int32)
     source = 0.6 + 0.4 * jnp.cos(2.0 * math.pi * row_pos.astype(jnp.float32) / 64.0)
-    lit = source[:, None] * share[1]
-    colors = ambient[:, None, None] * share[0][None] + diffuse[:, None, None] * lit[None]
-    alpha = -jnp.expm1(-kappa * share[2])
-    return jnp.concatenate([colors, alpha[None]], axis=0)
+    source = jnp.tile(source, cells // LANES)
+    glow = jnp.stack([jnp.broadcast_to(ambient[:, None], (3, source.shape[0])), diffuse[:, None] * source[None]])
+    glow = jnp.broadcast_to(glow[..., None], (*glow.shape, LANES))
+    return pl.pallas_call(
+        functools.partial(finish_kernel, kappa, low, len(held), ring),
+        out_shape=jax.ShapeDtypeStruct((4, share_rows, cells), jnp.float32),
+        in_specs=[vmem] * (2 + len(held)),
+        compiler_params=pltpu.CompilerParams(vmem_limit_bytes=4 * 2**20),
+        name="finish",
+    )(first, glow, *held)
 
 
 def solution(mesh):

time: 24.5 us -> 23.7 us (0.967)
  Pallas kernels: 3.47 us -> 4.5 us
  other arithmetic: 1.13 us -> 0.12 us
  waiting for transfers between devices: 9.29 us -> 8.7 us
  starting transfers between devices: 9.5 us -> 9.25 us
    pallas_call x0 -> x3, Pallas kernels: none -> 1.01 us  [the longest x1 0.73 us: on_device(): pl.pallas_call(functools.partial(finish_kernel, kappa, low, len(held), ri...]
    concatenate x4 -> x0, other arithmetic: 0.68 us -> none  [the longest x1 0.63 us: on_device(): return jnp.concatenate([colors, alpha[None]], axis=0)]
    ppermute x7, waiting for transfers between devices: 9.29 us -> 8.7 us  [sent_and_held(): held.append(lax.ppermute(pieces[hop], 'depth', pairs))]
    ppermute x7, starting transfers between devices: 9.5 us -> 9.25 us  [sent_and_held(): held.append(lax.ppermute(pieces[hop], 'depth', pairs))]
  transfers between devices with their start and end apart: 7 -> 7, of which waited for: 6 -> 7; matrix products, arithmetic and copies ran while one was open for 0% -> 1% of each run, Pallas kernels for 0% -> 0%
where the time goes in v6:
time: 23.7 us; the launch traced here: 23.5 us
  starting transfers between devices  9.25 us (39%)
  waiting for transfers between devices  8.7 us (37%)
  Pallas kernels  4.5 us (19%)
  between operations  0.69 us (3%)
  local copies, waits for them, and re-layouts  0.24 us (1%)
    ppermute x7, starting transfers between devices, sent_and_held(): held.append(lax.ppermute(pieces[hop], 'depth', pairs))  9.25 us
    ppermute x7, waiting for transfers between devices, sent_and_held(): held.append(lax.ppermute(pieces[hop], 'depth', pairs))  8.7 us
    pallas_call x1, Pallas kernels, composite_slab(): pl.pallas_call(functools.partial(slab_kernel, -kappa * log2e, -extinct *...  3.49 us
    pallas_call x1, Pallas kernels, on_device(): pl.pallas_call(functools.partial(finish_kernel, kappa, low, len(held), ri...  0.73 us
  transfers between devices with their start and end apart: 7, of which 7 were waited for; matrix products, arithmetic and copies ran while one was open for 1% of the time, Pallas kernels for 0%

profile of v6, /device:TPU:0, one launch (start us, length us, event | category | flops | bytes accessed | tf_op | source)
XLA Modules:
  0.0 23.5 jit_solution(2737401281352992488)
XLA Ops:
  0.0 0.0 copy-start
  0.0 0.0 copy-start.2
  0.0 0.0 copy-start.1
  0.0 3.5 %slab.1 = (f32[3,16,16,128]{3,2,1,0:T(8,128)S(1)}, f32[3,16,16,128]{3,2,1,0:T(8,128)S(1)}) custom-call(s32[8,4,16]{2,1,0:T(4,128)} %bitcast.7, bf16[16,128,512]{2,1,0:T(8,128)(2,1)} %dens_ref.1), custom_call_target="tpu_custom_call" | custom-call | flops 1073741824 | bytes 2097152 | tf_op jit(solution)/shard_map/slab/pallas_call | solution.py:115
  3.5 0.5 %collective-permute-start = (f32[3,16,16,128]{3,2,1,0:T(8,128)S(1)}, f32[3,16,16,128]{3,2,1,0:T(8,128)S(1)}, u32[]{:S(2)}, u32[]{:S(2)}) collective-permute-start(f32[3,16,16,128]{3,2,1,0:T(8,128)S(1)} %get-tuple-element.15), channel_id=1, source_target_pairs={{0,1},{1,0},{2,3},{3,2},{4,5},{5,4},{6,7},{7,6},{8,9},{9,8},{10,11... | collective-permute-start | bytes 1179656 | tf_op jit(solution)/shard_map/ppermute | solution.py:165
  4.7 0.1 mul.37
  4.8 0.6 %collective-permute-done.refs_0_ = f32[3,16,16,128]{3,2,1,0:T(8,128)S(1)} collective-permute-done((f32[3,16,16,128]{3,2,1,0:T(8,128)S(1)}, f32[3,16,16,128]{3,2,1,0:T(8,128)S(1)}, u32[]{:S(2)}, u32[]{:S(2)}) %collective-permute-start) | collective-permute-done | bytes 393248 | tf_op jit(solution)/shard_map/ppermute | solution.py:165
  5.4 0.0 copy-done
  5.4 0.1 merge.2
  5.5 3.9 %collective-permute-start.1 = (f32[3,4,16,128]{3,2,1,0:T(8,128)S(1)}, f32[3,4,16,128]{3,2,1,0:T(8,128)S(1)}, u32[]{:S(2)}, u32[]{:S(2)}) collective-permute-start(f32[3,4,16,128]{3,2,1,0:T(8,128)S(1)} %get-tuple-element.17), channel_id=1, source_target_pairs={{0,6},{1,7},{2,4},{3,5},{4,2},{5,3},{6,0},{7,1},{8,14},{9,15},{10,... | collective-permute-start | bytes 294920 | tf_op jit(solution)/shard_map/ppermute | solution.py:165
  9.4 0.5 %collective-permute-start.2 = (f32[3,4,16,128]{3,2,1,0:T(8,128)S(1)}, f32[3,4,16,128]{3,2,1,0:T(8,128)S(1)}, u32[]{:S(2)}, u32[]{:S(2)}) collective-permute-start(f32[3,4,16,128]{3,2,1,0:T(8,128)S(1)} %get-tuple-element.18), channel_id=1, source_target_pairs={{0,4},{1,5},{2,6},{3,7},{4,0},{5,1},{6,2},{7,3},{8,12},{9,13},{10,... | collective-permute-start | bytes 294920 | tf_op jit(solution)/shard_map/ppermute | solution.py:165
  9.9 0.1 collective-permute-start.3
  10.0 0.0 copy-done.2
  10.0 0.1 broadcast_multiply_fusion
  10.1 2.5 %collective-permute-done.1.refs_0_ = f32[3,4,16,128]{3,2,1,0:T(8,128)S(1)} collective-permute-done((f32[3,4,16,128]{3,2,1,0:T(8,128)S(1)}, f32[3,4,16,128]{3,2,1,0:T(8,128)S(1)}, u32[]{:S(2)}, u32[]{:S(2)}) %collective-permute-start.1) | collective-permute-done | bytes 98336 | tf_op jit(solution)/shard_map/ppermute | solution.py:165
  12.6 2.0 %collective-permute-done.2.refs_1_ = f32[3,4,16,128]{3,2,1,0:T(8,128)S(1)} collective-permute-done((f32[3,4,16,128]{3,2,1,0:T(8,128)S(1)}, f32[3,4,16,128]{3,2,1,0:T(8,128)S(1)}, u32[]{:S(2)}, u32[]{:S(2)}) %collective-permute-start.2) | collective-permute-done | bytes 98336 | tf_op jit(solution)/shard_map/ppermute | solution.py:165
  14.6 0.3 %collective-permute-done.3.refs_2_ = f32[3,4,16,128]{3,2,1,0:T(8,128)S(1)} collective-permute-done((f32[3,4,16,128]{3,2,1,0:T(8,128)S(1)}, f32[3,4,16,128]{3,2,1,0:T(8,128)S(1)}, u32[]{:S(2)}, u32[]{:S(2)}) %collective-permute-start.3) | collective-permute-done | bytes 98336 | tf_op jit(solution)/shard_map/ppermute | solution.py:165
  14.9 0.1 merge.3
  15.0 2.6 %collective-permute-start.4 = (f32[3,1,16,128]{3,2,1,0:T(8,128)S(1)}, f32[3,1,16,128]{3,2,1,0:T(8,128)S(1)}, u32[]{:S(2)}, u32[]{:S(2)}) collective-permute-start(f32[3,1,16,128]{3,2,1,0:T(8,128)S(1)} %get-tuple-element.21), channel_id=1, source_target_pairs={{0,16},{1,17},{2,18},{3,19},{4,20},{5,21},{6,22},{7,23},{8,24},{9,... | collective-permute-start | bytes 73736 | tf_op jit(solution)/shard_map/ppermute | solution.py:165
  17.6 1.2 %collective-permute-start.5 = (f32[3,1,16,128]{3,2,1,0:T(8,128)S(1)}, f32[3,1,16,128]{3,2,1,0:T(8,128)S(1)}, u32[]{:S(2)}, u32[]{:S(2)}) collective-permute-start(f32[3,1,16,128]{3,2,1,0:T(8,128)S(1)} %get-tuple-element.22), channel_id=1, source_target_pairs={{0,24},{1,25},{2,26},{3,27},{4,28},{5,29},{6,30},{7,31},{8,16},{9,... | collective-permute-start | bytes 73736 | tf_op jit(solution)/shard_map/ppermute | solution.py:165
  18.9 0.3 %collective-permute-start.6 = (f32[3,1,16,128]{3,2,1,0:T(8,128)S(1)}, f32[3,1,16,128]{3,2,1,0:T(8,128)S(1)}, u32[]{:S(2)}, u32[]{:S(2)}) collective-permute-start(f32[3,1,16,128]{3,2,1,0:T(8,128)S(1)} %get-tuple-element.23), channel_id=1, source_target_pairs={{0,8},{1,9},{2,10},{3,11},{4,12},{5,13},{6,14},{7,15},{8,0},{9,1},... | collective-permute-start | bytes 73736 | tf_op jit(solution)/shard_map/ppermute | solution.py:165
  19.2 0.0 copy-done.1
  19.2 0.1 stack_broadcast_in_dim.2
  19.3 1.4 %collective-permute-done.4.refs_0_ = f32[3,1,16,128]{3,2,1,0:T(8,128)S(1)} collective-permute-done((f32[3,1,16,128]{3,2,1,0:T(8,128)S(1)}, f32[3,1,16,128]{3,2,1,0:T(8,128)S(1)}, u32[]{:S(2)}, u32[]{:S(2)}) %collective-permute-start.4) | collective-permute-done | bytes 24608 | tf_op jit(solution)/shard_map/ppermute | solution.py:165
  20.7 1.7 %collective-permute-done.5.refs_1_ = f32[3,1,16,128]{3,2,1,0:T(8,128)S(1)} collective-permute-done((f32[3,1,16,128]{3,2,1,0:T(8,128)S(1)}, f32[3,1,16,128]{3,2,1,0:T(8,128)S(1)}, u32[]{:S(2)}, u32[]{:S(2)}) %collective-permute-start.5) | collective-permute-done | bytes 24608 | tf_op jit(solution)/shard_map/ppermute | solution.py:165
  22.4 0.3 %collective-permute-done.6.refs_2_ = f32[3,1,16,128]{3,2,1,0:T(8,128)S(1)} collective-permute-done((f32[3,1,16,128]{3,2,1,0:T(8,128)S(1)}, f32[3,1,16,128]{3,2,1,0:T(8,128)S(1)}, u32[]{:S(2)}, u32[]{:S(2)}) %collective-permute-start.6) | collective-permute-done | bytes 24608 | tf_op jit(solution)/shard_map/ppermute | solution.py:165
  22.7 0.1 broadcast_in_dim.5.glow_ref
  22.8 0.7 %finish.1 = f32[4,4,512]{2,1,0:T(4,128)} custom-call(s32[1,32]{1,0:T(1,128)S(1)} %bitcast.6, f32[2,3,16,128]{3,2,1,0:T(8,128)S(1)} %broadcast_in_dim.5.glow_ref, f32[3,1,16,128]{3,2,1,0:T(8,128)S(1)} %collective-permute-done.4.refs_0_, f32[3,1,16,128]{3,2,1,0:T(8,128)S(1)} %collective-permute-done.5.refs_1_, ...), custom_call_target="tpu_custom_call" | custom-call | tf_op jit(solution)/shard_map/finish/pallas_call | solution.py:269
  (3 shorter events, 0.1 us)
Async XLA Ops:
  0.0 5.4 %copy-start = (s32[32]{0:T(128)S(1)}, s32[32]{0:T(128)}, u32[]{:S(2)}) copy-start(s32[32]{0:T(128)} %param.9) | copy-start | bytes 388
  0.0 10.0 %copy-start.2 = (f32[3]{0:T(128)S(1)}, f32[3]{0:T(128)}, u32[]{:S(2)}) copy-start(f32[3]{0:T(128)} %param.11) | copy-start | bytes 40
  0.0 19.2 %copy-start.1 = (f32[3]{0:T(128)S(1)}, f32[3]{0:T(128)}, u32[]{:S(2)}) copy-start(f32[3]{0:T(128)} %param.10) | copy-start | bytes 40
  3.5 1.9 %collective-permute-start = (f32[3,16,16,128]{3,2,1,0:T(8,128)S(1)}, f32[3,16,16,128]{3,2,1,0:T(8,128)S(1)}, u32[]{:S(2)}, u32[]{:S(2)}) collective-permute-start(f32[3,16,16,128]{3,2,1,0:T(8,128)S(1)} %get-tuple-element.15), channel_id=1, source_target_pairs={{0,1},{1,0},{2,3},{3,2},{4,5},{5,4},{6,7},{7,6},{8,9},{9,8},{10,11... | collective-permute-start | bytes 1179656 | tf_op jit(solution)/shard_map/ppermute | solution.py:165
  5.5 7.1 %collective-permute-start.1 = (f32[3,4,16,128]{3,2,1,0:T(8,128)S(1)}, f32[3,4,16,128]{3,2,1,0:T(8,128)S(1)}, u32[]{:S(2)}, u32[]{:S(2)}) collective-permute-start(f32[3,4,16,128]{3,2,1,0:T(8,128)S(1)} %get-tuple-element.17), channel_id=1, source_target_pairs={{0,6},{1,7},{2,4},{3,5},{4,2},{5,3},{6,0},{7,1},{8,14},{9,15},{10,... | collective-permute-start | bytes 294920 | tf_op jit(solution)/shard_map/ppermute | solution.py:165
  9.4 5.2 %collective-permute-start.2 = (f32[3,4,16,128]{3,2,1,0:T(8,128)S(1)}, f32[3,4,16,128]{3,2,1,0:T(8,128)S(1)}, u32[]{:S(2)}, u32[]{:S(2)}) collective-permute-start(f32[3,4,16,128]{3,2,1,0:T(8,128)S(1)} %get-tuple-element.18), channel_id=1, source_target_pairs={{0,4},{1,5},{2,6},{3,7},{4,0},{5,1},{6,2},{7,3},{8,12},{9,13},{10,... | collective-permute-start | bytes 294920 | tf_op jit(solution)/shard_map/ppermute | solution.py:165
  9.9 4.9 %collective-permute-start.3 = (f32[3,4,16,128]{3,2,1,0:T(8,128)S(1)}, f32[3,4,16,128]{3,2,1,0:T(8,128)S(1)}, u32[]{:S(2)}, u32[]{:S(2)}) collective-permute-start(f32[3,4,16,128]{3,2,1,0:T(8,128)S(1)} %get-tuple-element.19), channel_id=1, source_target_pairs={{0,2},{1,3},{2,0},{3,1},{4,6},{5,7},{6,4},{7,5},{8,10},{9,11},{10,... | collective-permute-start | bytes 294920 | tf_op jit(solution)/shard_map/ppermute | solution.py:165
  15.0 5.7 %collective-permute-start.4 = (f32[3,1,16,128]{3,2,1,0:T(8,128)S(1)}, f32[3,1,16,128]{3,2,1,0:T(8,128)S(1)}, u32[]{:S(2)}, u32[]{:S(2)}) collective-permute-start(f32[3,1,16,128]{3,2,1,0:T(8,128)S(1)} %get-tuple-element.21), channel_id=1, source_target_pairs={{0,16},{1,17},{2,18},{3,19},{4,20},{5,21},{6,22},{7,23},{8,24},{9,... | collective-permute-start | bytes 73736 | tf_op jit(solution)/shard_map/ppermute | solution.py:165
  17.6 4.7 %collective-permute-start.5 = (f32[3,1,16,128]{3,2,1,0:T(8,128)S(1)}, f32[3,1,16,128]{3,2,1,0:T(8,128)S(1)}, u32[]{:S(2)}, u32[]{:S(2)}) collective-permute-start(f32[3,1,16,128]{3,2,1,0:T(8,128)S(1)} %get-tuple-element.22), channel_id=1, source_target_pairs={{0,24},{1,25},{2,26},{3,27},{4,28},{5,29},{6,30},{7,31},{8,16},{9,... | collective-permute-start | bytes 73736 | tf_op jit(solution)/shard_map/ppermute | solution.py:165
  18.9 3.8 %collective-permute-start.6 = (f32[3,1,16,128]{3,2,1,0:T(8,128)S(1)}, f32[3,1,16,128]{3,2,1,0:T(8,128)S(1)}, u32[]{:S(2)}, u32[]{:S(2)}) collective-permute-start(f32[3,1,16,128]{3,2,1,0:T(8,128)S(1)} %get-tuple-element.23), channel_id=1, source_target_pairs={{0,8},{1,9},{2,10},{3,11},{4,12},{5,13},{6,14},{7,15},{8,0},{9,1},... | collective-permute-start | bytes 73736 | tf_op jit(solution)/shard_map/ppermute | solution.py:165

commit v7 on v6

--- a/solution.py
+++ b/solution.py
@@ -206,6 +206,16 @@
     return jnp.where(depth < 0.125, depth * series, 1.0 - jnp.exp(-depth))
 
 
+def glow_kernel(share_rows, offset_ref, ambient_ref, diffuse_ref, glow_ref):
+    shape = glow_ref.shape[2:]
+    row = lax.broadcasted_iota(jnp.int32, shape, 0) % share_rows + lax.axis_index("depth") * share_rows
+    row = (row + offset_ref[0:1, 0:1]).astype(jnp.float32)
+    source = 0.6 + 0.4 * jnp.cos(2.0 * math.pi * row / 64.0)
+    for channel in range(3):
+        glow_ref[0, channel] = jnp.broadcast_to(ambient_ref[0:1, channel : channel + 1], shape)
+        glow_ref[1, channel] = diffuse_ref[0:1, channel : channel + 1] * source
+
+
 def finish_kernel(kappa, low, count, ring, order_ref, glow_ref, *refs):
     held, image = refs[:count], refs[count]
     places = places_of(order_ref, low, count, ring)
@@ -261,11 +271,15 @@
         )(first, *held)
         low, ring = through, next_ring
         held = sent_and_held(pieces, low, ring)
-    row_pos = band_offset[0] + my_slab * share_rows + jnp.arange(share_rows, dtype=jnp.int32)
-    source = 0.6 + 0.4 * jnp.cos(2.0 * math.pi * row_pos.astype(jnp.float32) / 64.0)
-    source = jnp.tile(source, cells // LANES)
-    glow = jnp.stack([jnp.broadcast_to(ambient[:, None], (3, source.shape[0])), diffuse[:, None] * source[None]])
-    glow = jnp.broadcast_to(glow[..., None], (*glow.shape, LANES))
+    glow = pl.pallas_call(
+        functools.partial(glow_kernel, share_rows),
+        out_shape=pltpu.VMEM((2, 3, share_rows * cells // LANES, LANES), jnp.float32),
+        in_specs=[vmem] * 3,
+        out_specs=vmem,
+        compiler_params=pltpu.CompilerParams(vmem_limit_bytes=4 * 2**20),
+        cost_estimate=pl.CostEstimate(flops=10**5, bytes_accessed=10**5, transcendentals=2048),
+        name="glow",
+    )(band_offset[None], ambient[None], diffuse[None])
     return pl.pallas_call(
         functools.partial(finish_kernel, kappa, low, len(held), ring),
         out_shape=jax.ShapeDtypeStruct((4, share_rows, cells), jnp.float32),

time: 23.7 us -> 23.6 us (level)
  transfers between devices with their start and end apart: 7 -> 7, of which waited for: 7 -> 7; matrix products, arithmetic and copies ran while one was open for 1% -> 0% of each run, Pallas kernels for 0% -> 1%
where the time goes in v7:
time: 23.6 us; the launch traced here: 23.4 us
  starting transfers between devices  9.24 us (39%)
  waiting for transfers between devices  8.85 us (38%)
  Pallas kernels  4.62 us (20%)
  between operations  0.7 us (3%)
    ppermute x7, starting transfers between devices, sent_and_held(): held.append(lax.ppermute(pieces[hop], 'depth', pairs))  9.24 us
    ppermute x7, waiting for transfers between devices, sent_and_held(): held.append(lax.ppermute(pieces[hop], 'depth', pairs))  8.85 us
    pallas_call x1, Pallas kernels, composite_slab(): pl.pallas_call(functools.partial(slab_kernel, -kappa * log2e, -extinct *...  3.49 us
    pallas_call x1, Pallas kernels, on_device(): pl.pallas_call(functools.partial(finish_kernel, kappa, low, len(held), ri...  0.73 us
  transfers between devices with their start and end apart: 7, of which 7 were waited for; matrix products, arithmetic and copies ran while one was open for 0% of the time, Pallas kernels for 1%

profile of v7, /device:TPU:0, one launch (start us, length us, event | category | flops | bytes accessed | tf_op | source)
XLA Modules:
  0.0 23.4 jit_solution(5903711328446474262)
XLA Ops:
  0.0 0.0 copy-start
  0.0 0.0 copy-start.1
  0.0 0.0 copy-start.2
  0.0 3.5 %slab.1 = (f32[3,16,16,128]{3,2,1,0:T(8,128)S(1)}, f32[3,16,16,128]{3,2,1,0:T(8,128)S(1)}) custom-call(s32[8,4,16]{2,1,0:T(4,128)} %bitcast.11, bf16[16,128,512]{2,1,0:T(8,128)(2,1)} %dens_ref.1), custom_call_target="tpu_custom_call" | custom-call | flops 1073741824 | bytes 2097152 | tf_op jit(solution)/shard_map/slab/pallas_call | solution.py:115
  3.5 0.5 %collective-permute-start = (f32[3,16,16,128]{3,2,1,0:T(8,128)S(1)}, f32[3,16,16,128]{3,2,1,0:T(8,128)S(1)}, u32[]{:S(2)}, u32[]{:S(2)}) collective-permute-start(f32[3,16,16,128]{3,2,1,0:T(8,128)S(1)} %get-tuple-element.15), channel_id=1, source_target_pairs={{0,1},{1,0},{2,3},{3,2},{4,5},{5,4},{6,7},{7,6},{8,9},{9,8},{10,11... | collective-permute-start | bytes 1179656 | tf_op jit(solution)/shard_map/ppermute | solution.py:165
  4.0 1.3 %collective-permute-done.refs_0_ = f32[3,16,16,128]{3,2,1,0:T(8,128)S(1)} collective-permute-done((f32[3,16,16,128]{3,2,1,0:T(8,128)S(1)}, f32[3,16,16,128]{3,2,1,0:T(8,128)S(1)}, u32[]{:S(2)}, u32[]{:S(2)}) %collective-permute-start) | collective-permute-done | bytes 393248 | tf_op jit(solution)/shard_map/ppermute | solution.py:165
  5.4 0.0 copy-done
  5.4 0.1 merge.2
  5.5 3.9 %collective-permute-start.1 = (f32[3,4,16,128]{3,2,1,0:T(8,128)S(1)}, f32[3,4,16,128]{3,2,1,0:T(8,128)S(1)}, u32[]{:S(2)}, u32[]{:S(2)}) collective-permute-start(f32[3,4,16,128]{3,2,1,0:T(8,128)S(1)} %get-tuple-element.17), channel_id=1, source_target_pairs={{0,6},{1,7},{2,4},{3,5},{4,2},{5,3},{6,0},{7,1},{8,14},{9,15},{10,... | collective-permute-start | bytes 294920 | tf_op jit(solution)/shard_map/ppermute | solution.py:165
  9.4 0.5 %collective-permute-start.2 = (f32[3,4,16,128]{3,2,1,0:T(8,128)S(1)}, f32[3,4,16,128]{3,2,1,0:T(8,128)S(1)}, u32[]{:S(2)}, u32[]{:S(2)}) collective-permute-start(f32[3,4,16,128]{3,2,1,0:T(8,128)S(1)} %get-tuple-element.18), channel_id=1, source_target_pairs={{0,4},{1,5},{2,6},{3,7},{4,0},{5,1},{6,2},{7,3},{8,12},{9,13},{10,... | collective-permute-start | bytes 294920 | tf_op jit(solution)/shard_map/ppermute | solution.py:165
  9.9 0.1 collective-permute-start.3
  10.0 2.6 %collective-permute-done.1.refs_0_ = f32[3,4,16,128]{3,2,1,0:T(8,128)S(1)} collective-permute-done((f32[3,4,16,128]{3,2,1,0:T(8,128)S(1)}, f32[3,4,16,128]{3,2,1,0:T(8,128)S(1)}, u32[]{:S(2)}, u32[]{:S(2)}) %collective-permute-start.1) | collective-permute-done | bytes 98336 | tf_op jit(solution)/shard_map/ppermute | solution.py:165
  12.6 2.0 %collective-permute-done.2.refs_1_ = f32[3,4,16,128]{3,2,1,0:T(8,128)S(1)} collective-permute-done((f32[3,4,16,128]{3,2,1,0:T(8,128)S(1)}, f32[3,4,16,128]{3,2,1,0:T(8,128)S(1)}, u32[]{:S(2)}, u32[]{:S(2)}) %collective-permute-start.2) | collective-permute-done | bytes 98336 | tf_op jit(solution)/shard_map/ppermute | solution.py:165
  14.6 0.3 %collective-permute-done.3.refs_2_ = f32[3,4,16,128]{3,2,1,0:T(8,128)S(1)} collective-permute-done((f32[3,4,16,128]{3,2,1,0:T(8,128)S(1)}, f32[3,4,16,128]{3,2,1,0:T(8,128)S(1)}, u32[]{:S(2)}, u32[]{:S(2)}) %collective-permute-start.3) | collective-permute-done | bytes 98336 | tf_op jit(solution)/shard_map/ppermute | solution.py:165
  14.9 0.1 merge.3
  15.0 2.6 %collective-permute-start.4 = (f32[3,1,16,128]{3,2,1,0:T(8,128)S(1)}, f32[3,1,16,128]{3,2,1,0:T(8,128)S(1)}, u32[]{:S(2)}, u32[]{:S(2)}) collective-permute-start(f32[3,1,16,128]{3,2,1,0:T(8,128)S(1)} %get-tuple-element.21), channel_id=1, source_target_pairs={{0,16},{1,17},{2,18},{3,19},{4,20},{5,21},{6,22},{7,23},{8,24},{9,... | collective-permute-start | bytes 73736 | tf_op jit(solution)/shard_map/ppermute | solution.py:165
  17.6 1.2 %collective-permute-start.5 = (f32[3,1,16,128]{3,2,1,0:T(8,128)S(1)}, f32[3,1,16,128]{3,2,1,0:T(8,128)S(1)}, u32[]{:S(2)}, u32[]{:S(2)}) collective-permute-start(f32[3,1,16,128]{3,2,1,0:T(8,128)S(1)} %get-tuple-element.22), channel_id=1, source_target_pairs={{0,24},{1,25},{2,26},{3,27},{4,28},{5,29},{6,30},{7,31},{8,16},{9,... | collective-permute-start | bytes 73736 | tf_op jit(solution)/shard_map/ppermute | solution.py:165
  18.9 0.3 %collective-permute-start.6 = (f32[3,1,16,128]{3,2,1,0:T(8,128)S(1)}, f32[3,1,16,128]{3,2,1,0:T(8,128)S(1)}, u32[]{:S(2)}, u32[]{:S(2)}) collective-permute-start(f32[3,1,16,128]{3,2,1,0:T(8,128)S(1)} %get-tuple-element.23), channel_id=1, source_target_pairs={{0,8},{1,9},{2,10},{3,11},{4,12},{5,13},{6,14},{7,15},{8,0},{9,1},... | collective-permute-start | bytes 73736 | tf_op jit(solution)/shard_map/ppermute | solution.py:165
  19.9 0.0 copy-done.1
  19.9 0.0 copy-done.2
  19.9 0.1 glow.1.glow_ref
  20.0 0.7 %collective-permute-done.4.refs_0_ = f32[3,1,16,128]{3,2,1,0:T(8,128)S(1)} collective-permute-done((f32[3,1,16,128]{3,2,1,0:T(8,128)S(1)}, f32[3,1,16,128]{3,2,1,0:T(8,128)S(1)}, u32[]{:S(2)}, u32[]{:S(2)}) %collective-permute-start.4) | collective-permute-done | bytes 24608 | tf_op jit(solution)/shard_map/ppermute | solution.py:165
  20.7 1.7 %collective-permute-done.5.refs_1_ = f32[3,1,16,128]{3,2,1,0:T(8,128)S(1)} collective-permute-done((f32[3,1,16,128]{3,2,1,0:T(8,128)S(1)}, f32[3,1,16,128]{3,2,1,0:T(8,128)S(1)}, u32[]{:S(2)}, u32[]{:S(2)}) %collective-permute-start.5) | collective-permute-done | bytes 24608 | tf_op jit(solution)/shard_map/ppermute | solution.py:165
  22.4 0.3 %collective-permute-done.6.refs_2_ = f32[3,1,16,128]{3,2,1,0:T(8,128)S(1)} collective-permute-done((f32[3,1,16,128]{3,2,1,0:T(8,128)S(1)}, f32[3,1,16,128]{3,2,1,0:T(8,128)S(1)}, u32[]{:S(2)}, u32[]{:S(2)}) %collective-permute-start.6) | collective-permute-done | bytes 24608 | tf_op jit(solution)/shard_map/ppermute | solution.py:165
  22.7 0.7 %finish.1 = f32[4,4,512]{2,1,0:T(4,128)} custom-call(s32[1,32]{1,0:T(1,128)S(1)} %bitcast.8, f32[2,3,16,128]{3,2,1,0:T(8,128)S(1)} %glow.1.glow_ref, f32[3,1,16,128]{3,2,1,0:T(8,128)S(1)} %collective-permute-done.4.refs_0_, f32[3,1,16,128]{3,2,1,0:T(8,128)S(1)} %collective-permute-done.5.refs_1_, f32[3,1,16,128]{3,2,1,0:T(8,128)S(1)} %collective-permute-done.6.refs_2_, ...), custom_call_target="tpu_custom_call" | custom-call | tf_op jit(solution)/shard_map/finish/pallas_call | solution.py:283
Async XLA Ops:
  0.0 5.4 %copy-start = (s32[32]{0:T(128)S(1)}, s32[32]{0:T(128)}, u32[]{:S(2)}) copy-start(s32[32]{0:T(128)} %param.9) | copy-start | bytes 388
  0.0 19.9 %copy-start.1 = (f32[3]{0:T(128)S(1)}, f32[3]{0:T(128)}, u32[]{:S(2)}) copy-start(f32[3]{0:T(128)} %param.10) | copy-start | bytes 40
  0.0 19.9 %copy-start.2 = (f32[3]{0:T(128)S(1)}, f32[3]{0:T(128)}, u32[]{:S(2)}) copy-start(f32[3]{0:T(128)} %param.11) | copy-start | bytes 40
  3.5 1.9 %collective-permute-start = (f32[3,16,16,128]{3,2,1,0:T(8,128)S(1)}, f32[3,16,16,128]{3,2,1,0:T(8,128)S(1)}, u32[]{:S(2)}, u32[]{:S(2)}) collective-permute-start(f32[3,16,16,128]{3,2,1,0:T(8,128)S(1)} %get-tuple-element.15), channel_id=1, source_target_pairs={{0,1},{1,0},{2,3},{3,2},{4,5},{5,4},{6,7},{7,6},{8,9},{9,8},{10,11... | collective-permute-start | bytes 1179656 | tf_op jit(solution)/shard_map/ppermute | solution.py:165
  5.5 7.1 %collective-permute-start.1 = (f32[3,4,16,128]{3,2,1,0:T(8,128)S(1)}, f32[3,4,16,128]{3,2,1,0:T(8,128)S(1)}, u32[]{:S(2)}, u32[]{:S(2)}) collective-permute-start(f32[3,4,16,128]{3,2,1,0:T(8,128)S(1)} %get-tuple-element.17), channel_id=1, source_target_pairs={{0,6},{1,7},{2,4},{3,5},{4,2},{5,3},{6,0},{7,1},{8,14},{9,15},{10,... | collective-permute-start | bytes 294920 | tf_op jit(solution)/shard_map/ppermute | solution.py:165
  9.4 5.2 %collective-permute-start.2 = (f32[3,4,16,128]{3,2,1,0:T(8,128)S(1)}, f32[3,4,16,128]{3,2,1,0:T(8,128)S(1)}, u32[]{:S(2)}, u32[]{:S(2)}) collective-permute-start(f32[3,4,16,128]{3,2,1,0:T(8,128)S(1)} %get-tuple-element.18), channel_id=1, source_target_pairs={{0,4},{1,5},{2,6},{3,7},{4,0},{5,1},{6,2},{7,3},{8,12},{9,13},{10,... | collective-permute-start | bytes 294920 | tf_op jit(solution)/shard_map/ppermute | solution.py:165
  9.9 4.9 %collective-permute-start.3 = (f32[3,4,16,128]{3,2,1,0:T(8,128)S(1)}, f32[3,4,16,128]{3,2,1,0:T(8,128)S(1)}, u32[]{:S(2)}, u32[]{:S(2)}) collective-permute-start(f32[3,4,16,128]{3,2,1,0:T(8,128)S(1)} %get-tuple-element.19), channel_id=1, source_target_pairs={{0,2},{1,3},{2,0},{3,1},{4,6},{5,7},{6,4},{7,5},{8,10},{9,11},{10,... | collective-permute-start | bytes 294920 | tf_op jit(solution)/shard_map/ppermute | solution.py:165
  15.0 5.7 %collective-permute-start.4 = (f32[3,1,16,128]{3,2,1,0:T(8,128)S(1)}, f32[3,1,16,128]{3,2,1,0:T(8,128)S(1)}, u32[]{:S(2)}, u32[]{:S(2)}) collective-permute-start(f32[3,1,16,128]{3,2,1,0:T(8,128)S(1)} %get-tuple-element.21), channel_id=1, source_target_pairs={{0,16},{1,17},{2,18},{3,19},{4,20},{5,21},{6,22},{7,23},{8,24},{9,... | collective-permute-start | bytes 73736 | tf_op jit(solution)/shard_map/ppermute | solution.py:165
  17.6 4.7 %collective-permute-start.5 = (f32[3,1,16,128]{3,2,1,0:T(8,128)S(1)}, f32[3,1,16,128]{3,2,1,0:T(8,128)S(1)}, u32[]{:S(2)}, u32[]{:S(2)}) collective-permute-start(f32[3,1,16,128]{3,2,1,0:T(8,128)S(1)} %get-tuple-element.22), channel_id=1, source_target_pairs={{0,24},{1,25},{2,26},{3,27},{4,28},{5,29},{6,30},{7,31},{8,16},{9,... | collective-permute-start | bytes 73736 | tf_op jit(solution)/shard_map/ppermute | solution.py:165
  18.9 3.8 %collective-permute-start.6 = (f32[3,1,16,128]{3,2,1,0:T(8,128)S(1)}, f32[3,1,16,128]{3,2,1,0:T(8,128)S(1)}, u32[]{:S(2)}, u32[]{:S(2)}) collective-permute-start(f32[3,1,16,128]{3,2,1,0:T(8,128)S(1)} %get-tuple-element.23), channel_id=1, source_target_pairs={{0,8},{1,9},{2,10},{3,11},{4,12},{5,13},{6,14},{7,15},{8,0},{9,1},... | collective-permute-start | bytes 73736 | tf_op jit(solution)/shard_map/ppermute | solution.py:165

commit v8 on v7

--- a/solution.py
+++ b/solution.py
@@ -47,7 +47,11 @@
     upper[...] = (
         lax.broadcasted_iota(jnp.int32, (cells, cells), 0) < lax.broadcasted_iota(jnp.int32, (cells, cells), 1)
     ).astype(jnp.float32).astype(jnp.bfloat16)
-    odd = lax.axis_index("depth") & 1 == 1
+    me = lax.axis_index("depth")
+    odd = me & 1 == 1
+    fan = give_ref.shape[0]
+    mine = me >> 1 & (fan - 1)
+    laps = group * (shares // 2) // fan
     flag_copy.wait()
 
     def work(step, carry):
@@ -95,19 +99,20 @@
                     for side in range(2):
                         first = (2 * pair + side) * share_rows
                         halves.append(jnp.concatenate([o[channel][first : first + share_rows] for o in outs], axis=0))
-                    to = (step * group + g) * (shares // 2) + pair
-                    keep_ref[channel, to] = jnp.where(odd, halves[1], halves[0])
-                    give_ref[channel, to] = jnp.where(odd, halves[0], halves[1])
+                    local = g * (shares // 2) + pair
+                    hop, row = mine ^ local % fan, step * laps + local // fan
+                    keep_ref[hop, channel, row] = jnp.where(odd, halves[1], halves[0])
+                    give_ref[hop, channel, row] = jnp.where(odd, halves[0], halves[1])
         return carry
 
     lax.fori_loop(0, rows // tall, work, 0)
 
 
-def composite_slab(clip_flags, density, nearer, kappa, extinct, depth_n):
+def composite_slab(clip_flags, density, nearer, kappa, extinct, depth_n, fan):
     slices, rows, cells = density.shape
     share_rows = rows // depth_n
     blocks_r, blocks_x = clip_flags.shape[1:]
-    half = (3, depth_n // 2, share_rows * cells // LANES, LANES)
+    half = (fan, 3, depth_n // 2 // fan, share_rows * cells // LANES, LANES)
     log2e = math.log2(math.e)
     has_nearer = nearer is not None
     tall = math.gcd(blocks_r, 2) * rows // blocks_r
@@ -199,6 +204,16 @@
                 out[hop][channel, row] = merged[channel]
 
 
+def pair_kernel(kappa, first, order_ref, keep_ref, recv_ref, *out):
+    places = places_of(order_ref, 0, 2, False)
+    for at, piece in enumerate(out):
+        for row in range(piece.shape[1]):
+            held = [[recv_ref[at, channel, row] for channel in range(3)], [keep_ref[first + at, channel, row] for channel in range(3)]]
+            merged = over(kappa, places, held)
+            for channel in range(3):
+                piece[channel, row] = merged[channel]
+
+
 def opacity(depth):
     series = 1.0 - depth * (1.0 / 6.0)
     for term in (5.0, 4.0, 3.0, 2.0):
@@ -249,24 +264,43 @@
         totals = jnp.sum(totals, axis=3).reshape(slices, rows)
         nearer = prefix(totals, "xs", lambda early, late: early + late, jnp.zeros_like(totals))
         nearer = nearer[:, :, None]
-    held = sent_and_held(composite_slab(clip_flags, density, nearer, kappa, extinct, depth_n), 0, False)
     first = order[None]
     vmem = pl.BlockSpec(memory_space=pltpu.VMEM)
-    low, ring = 0, False
+    small = pltpu.CompilerParams(vmem_limit_bytes=4 * 2**20)
+    fan = 4
+    keep, give = composite_slab(clip_flags, density, nearer, kappa, extinct, depth_n, fan)
+    pairs = [(source, source ^ 1) for source in range(depth_n)]
+    far = lax.ppermute(give[fan - 1 :], "depth", pairs)
+    near = lax.ppermute(give[: fan - 1], "depth", pairs)
+
+    def paired(start, recv):
+        return pl.pallas_call(
+            functools.partial(pair_kernel, kappa, start),
+            out_shape=[pltpu.VMEM(keep.shape[1:], jnp.float32)] * recv.shape[0],
+            in_specs=[vmem] * 3,
+            out_specs=[vmem] * recv.shape[0],
+            compiler_params=small,
+            name="pair",
+        )(first, keep, recv)
+
+    farthest = paired(fan - 1, far)
+    pieces = [*paired(0, near), *farthest]
+    low, ring = 1, False
+    held = sent_and_held(pieces, low, ring)
     while True:
         count = len(held)
         through = low + count.bit_length() - 1
         if through == levels:
             break
         fan = 4 if through + 1 < levels else 2
-        next_ring = low > 0 and fan == 4
+        next_ring = fan == 4
         shape = (3, held[0].shape[1] // fan, *held[0].shape[2:])
         pieces = pl.pallas_call(
             functools.partial(merge_kernel, kappa, low, count, ring, next_ring),
             out_shape=[pltpu.VMEM(shape, jnp.float32)] * fan,
             in_specs=[vmem] * (1 + count),
             out_specs=[vmem] * fan,
-            compiler_params=pltpu.CompilerParams(vmem_limit_bytes=4 * 2**20),
+            compiler_params=small,
             name="merge",
         )(first, *held)
         low, ring = through, next_ring
@@ -276,7 +310,7 @@
         out_shape=pltpu.VMEM((2, 3, share_rows * cells // LANES, LANES), jnp.float32),
         in_specs=[vmem] * 3,
         out_specs=vmem,
-        compiler_params=pltpu.CompilerParams(vmem_limit_bytes=4 * 2**20),
+        compiler_params=small,
         cost_estimate=pl.CostEstimate(flops=10**5, bytes_accessed=10**5, transcendentals=2048),
         name="glow",
     )(band_offset[None], ambient[None], diffuse[None])
@@ -284,7 +318,7 @@
         functools.partial(finish_kernel, kappa, low, len(held), ring),
         out_shape=jax.ShapeDtypeStruct((4, share_rows, cells), jnp.float32),
         in_specs=[vmem] * (2 + len(held)),
-        compiler_params=pltpu.CompilerParams(vmem_limit_bytes=4 * 2**20),
+        compiler_params=small,
         name="finish",
     )(first, glow, *held)
 

time: 23.6 us -> 23.6 us (level)
  waiting for transfers between devices: 8.85 us -> 8.57 us
    ppermute x7 -> x6, waiting for transfers between devices: 8.85 us -> 7.33 us  [sent_and_held(): held.append(lax.ppermute(pieces[hop], 'depth', pairs))]
    ppermute x0 -> x2, waiting for transfers between devices: none -> 1.25 us  [the longest x1 1.24 us: on_device(): far = lax.ppermute(give[fan - 1:], 'depth', pairs)]
    ppermute x0 -> x2, starting transfers between devices: none -> 0.64 us  [the longest x1 0.52 us: on_device(): near = lax.ppermute(give[:fan - 1], 'depth', pairs)]
    ppermute x7 -> x6, starting transfers between devices: 9.24 us -> 8.76 us  [sent_and_held(): held.append(lax.ppermute(pieces[hop], 'depth', pairs))]
  transfers between devices with their start and end apart: 7 -> 8, of which waited for: 7 -> 7; matrix products, arithmetic and copies ran while one was open for 0% -> 0% of each run, Pallas kernels for 1% -> 2%
where the time goes in v8:
time: 23.6 us; the launch traced here: 23.4 us
  starting transfers between devices  9.4 us (40%)
  waiting for transfers between devices  8.57 us (36%)
  Pallas kernels  4.68 us (20%)
  between operations  0.73 us (3%)
    ppermute x6, starting transfers between devices, sent_and_held(): held.append(lax.ppermute(pieces[hop], 'depth', pairs))  8.76 us
    ppermute x6, waiting for transfers between devices, sent_and_held(): held.append(lax.ppermute(pieces[hop], 'depth', pairs))  7.33 us
    pallas_call x1, Pallas kernels, composite_slab(): pl.pallas_call(functools.partial(slab_kernel, -kappa * log2e, -extinct *...  3.46 us
    ppermute x1, waiting for transfers between devices, on_device(): far = lax.ppermute(give[fan - 1:], 'depth', pairs)  1.24 us
    pallas_call x1, Pallas kernels, on_device(): pl.pallas_call(functools.partial(finish_kernel, kappa, low, len(held), ri...  0.73 us
    ppermute x1, starting transfers between devices, on_device(): near = lax.ppermute(give[:fan - 1], 'depth', pairs)  0.52 us
  transfers between devices with their start and end apart: 8, of which 7 were waited for; matrix products, arithmetic and copies ran while one was open for 0% of the time, Pallas kernels for 2%

profile of v8, /device:TPU:0, one launch (start us, length us, event | category | flops | bytes accessed | tf_op | source)
XLA Modules:
  0.0 23.4 jit_solution(11650633443106949470)
XLA Ops:
  0.0 0.0 copy-start
  0.0 3.5 %slab.1 = (f32[4,3,4,16,128]{4,3,2,1,0:T(8,128)S(1)}, f32[4,3,4,16,128]{4,3,2,1,0:T(8,128)S(1)}) custom-call(s32[8,4,16]{2,1,0:T(4,128)} %bitcast.12, bf16[16,128,512]{2,1,0:T(8,128)(2,1)} %dens_ref.1), custom_call_target="tpu_custom_call" | custom-call | flops 1073741824 | bytes 2097152 | tf_op jit(solution)/shard_map/slab/pallas_call | solution.py:120
  3.5 0.0 copy-start.1
  3.5 0.0 copy-start.2
  3.5 0.5 %collective-permute-start.2 = (f32[3,3,4,16,128]{4,3,2,1,0:T(8,128)S(1)}, f32[3,3,4,16,128]{4,3,2,1,0:T(8,128)S(1)}, u32[]{:S(2)}, u32[]{:S(2)}) collective-permute-start(f32[3,3,4,16,128]{4,3,2,1,0:T(8,128)S(1)} %slice.7), channel_id=1, source_target_pairs={{0,1},{1,0},{2,3},{3,2},{4,5},{5,4},{6,7},{7,6},{8,9},{9,8},{10,11... | collective-permute-start | bytes 884744 | tf_op jit(solution)/shard_map/ppermute | solution.py:274
  4.1 0.1 collective-permute-start
  4.2 1.2 %collective-permute-done.recv_ref = f32[1,3,4,16,128]{4,3,2,1,0:T(8,128)S(1)} collective-permute-done((f32[1,3,4,16,128]{4,3,2,1,0:T(8,128)S(1)}, f32[1,3,4,16,128]{4,3,2,1,0:T(8,128)S(1)}, u32[]{:S(2)}, u32[]{:S(2)}) %collective-permute-start) | collective-permute-done | bytes 98336 | tf_op jit(solution)/shard_map/ppermute | solution.py:273
  5.4 0.0 copy-done
  5.4 0.1 pair.2
  5.5 3.9 %collective-permute-start.1 = (f32[3,4,16,128]{3,2,1,0:T(8,128)S(1)}, f32[3,4,16,128]{3,2,1,0:T(8,128)S(1)}, u32[]{:S(2)}, u32[]{:S(2)}) collective-permute-start(f32[3,4,16,128]{3,2,1,0:T(8,128)S(1)} %pair.2), channel_id=1, source_target_pairs={{0,6},{1,7},{2,4},{3,5},{4,2},{5,3},{6,0},{7,1},{8,14},{9,15},{10,... | collective-permute-start | bytes 294920 | tf_op jit(solution)/shard_map/ppermute | solution.py:170
  9.4 0.0 collective-permute-done.2.recv_ref
  9.4 0.1 pair.3
  9.5 0.6 %collective-permute-start.3 = (f32[3,4,16,128]{3,2,1,0:T(8,128)S(1)}, f32[3,4,16,128]{3,2,1,0:T(8,128)S(1)}, u32[]{:S(2)}, u32[]{:S(2)}) collective-permute-start(f32[3,4,16,128]{3,2,1,0:T(8,128)S(1)} %get-tuple-element.16), channel_id=1, source_target_pairs={{0,4},{1,5},{2,6},{3,7},{4,0},{5,1},{6,2},{7,3},{8,12},{9,13},{10,... | collective-permute-start | bytes 294920 | tf_op jit(solution)/shard_map/ppermute | solution.py:170
  10.1 0.1 collective-permute-start.4
  10.2 2.4 %collective-permute-done.1.refs_0_ = f32[3,4,16,128]{3,2,1,0:T(8,128)S(1)} collective-permute-done((f32[3,4,16,128]{3,2,1,0:T(8,128)S(1)}, f32[3,4,16,128]{3,2,1,0:T(8,128)S(1)}, u32[]{:S(2)}, u32[]{:S(2)}) %collective-permute-start.1) | collective-permute-done | bytes 98336 | tf_op jit(solution)/shard_map/ppermute | solution.py:170
  12.6 2.0 %collective-permute-done.3.refs_1_ = f32[3,4,16,128]{3,2,1,0:T(8,128)S(1)} collective-permute-done((f32[3,4,16,128]{3,2,1,0:T(8,128)S(1)}, f32[3,4,16,128]{3,2,1,0:T(8,128)S(1)}, u32[]{:S(2)}, u32[]{:S(2)}) %collective-permute-start.3) | collective-permute-done | bytes 98336 | tf_op jit(solution)/shard_map/ppermute | solution.py:170
  14.6 0.2 %collective-permute-done.4.refs_2_ = f32[3,4,16,128]{3,2,1,0:T(8,128)S(1)} collective-permute-done((f32[3,4,16,128]{3,2,1,0:T(8,128)S(1)}, f32[3,4,16,128]{3,2,1,0:T(8,128)S(1)}, u32[]{:S(2)}, u32[]{:S(2)}) %collective-permute-start.4) | collective-permute-done | bytes 98336 | tf_op jit(solution)/shard_map/ppermute | solution.py:170
  14.9 0.1 merge.1
  15.0 2.6 %collective-permute-start.5 = (f32[3,1,16,128]{3,2,1,0:T(8,128)S(1)}, f32[3,1,16,128]{3,2,1,0:T(8,128)S(1)}, u32[]{:S(2)}, u32[]{:S(2)}) collective-permute-start(f32[3,1,16,128]{3,2,1,0:T(8,128)S(1)} %get-tuple-element.19), channel_id=1, source_target_pairs={{0,16},{1,17},{2,18},{3,19},{4,20},{5,21},{6,22},{7,23},{8,24},{9,... | collective-permute-start | bytes 73736 | tf_op jit(solution)/shard_map/ppermute | solution.py:170
  17.6 1.2 %collective-permute-start.6 = (f32[3,1,16,128]{3,2,1,0:T(8,128)S(1)}, f32[3,1,16,128]{3,2,1,0:T(8,128)S(1)}, u32[]{:S(2)}, u32[]{:S(2)}) collective-permute-start(f32[3,1,16,128]{3,2,1,0:T(8,128)S(1)} %get-tuple-element.20), channel_id=1, source_target_pairs={{0,24},{1,25},{2,26},{3,27},{4,28},{5,29},{6,30},{7,31},{8,16},{9,... | collective-permute-start | bytes 73736 | tf_op jit(solution)/shard_map/ppermute | solution.py:170
  18.9 0.3 %collective-permute-start.7 = (f32[3,1,16,128]{3,2,1,0:T(8,128)S(1)}, f32[3,1,16,128]{3,2,1,0:T(8,128)S(1)}, u32[]{:S(2)}, u32[]{:S(2)}) collective-permute-start(f32[3,1,16,128]{3,2,1,0:T(8,128)S(1)} %get-tuple-element.21), channel_id=1, source_target_pairs={{0,8},{1,9},{2,10},{3,11},{4,12},{5,13},{6,14},{7,15},{8,0},{9,1},... | collective-permute-start | bytes 73736 | tf_op jit(solution)/shard_map/ppermute | solution.py:170
  19.9 0.0 copy-done.1
  19.9 0.0 copy-done.2
  19.9 0.1 glow.1.glow_ref
  20.0 0.7 %collective-permute-done.5.refs_0_ = f32[3,1,16,128]{3,2,1,0:T(8,128)S(1)} collective-permute-done((f32[3,1,16,128]{3,2,1,0:T(8,128)S(1)}, f32[3,1,16,128]{3,2,1,0:T(8,128)S(1)}, u32[]{:S(2)}, u32[]{:S(2)}) %collective-permute-start.5) | collective-permute-done | bytes 24608 | tf_op jit(solution)/shard_map/ppermute | solution.py:170
  20.7 1.7 %collective-permute-done.6.refs_1_ = f32[3,1,16,128]{3,2,1,0:T(8,128)S(1)} collective-permute-done((f32[3,1,16,128]{3,2,1,0:T(8,128)S(1)}, f32[3,1,16,128]{3,2,1,0:T(8,128)S(1)}, u32[]{:S(2)}, u32[]{:S(2)}) %collective-permute-start.6) | collective-permute-done | bytes 24608 | tf_op jit(solution)/shard_map/ppermute | solution.py:170
  22.4 0.3 %collective-permute-done.7.refs_2_ = f32[3,1,16,128]{3,2,1,0:T(8,128)S(1)} collective-permute-done((f32[3,1,16,128]{3,2,1,0:T(8,128)S(1)}, f32[3,1,16,128]{3,2,1,0:T(8,128)S(1)}, u32[]{:S(2)}, u32[]{:S(2)}) %collective-permute-start.7) | collective-permute-done | bytes 24608 | tf_op jit(solution)/shard_map/ppermute | solution.py:170
  22.7 0.7 %finish.1 = f32[4,4,512]{2,1,0:T(4,128)} custom-call(s32[1,32]{1,0:T(1,128)S(1)} %bitcast.9, f32[2,3,16,128]{3,2,1,0:T(8,128)S(1)} %glow.1.glow_ref, f32[3,1,16,128]{3,2,1,0:T(8,128)S(1)} %collective-permute-done.5.refs_0_, f32[3,1,16,128]{3,2,1,0:T(8,128)S(1)} %collective-permute-done.6.refs_1_, f32[3,1,16,128]{3,2,1,0:T(8,128)S(1)} %collective-permute-done.7.refs_2_, ...), custom_call_target="tpu_custom_call" | custom-call | tf_op jit(solution)/shard_map/finish/pallas_call | solution.py:317
  (2 shorter events, 0.0 us)
Async XLA Ops:
  0.0 5.4 %copy-start = (s32[32]{0:T(128)S(1)}, s32[32]{0:T(128)}, u32[]{:S(2)}) copy-start(s32[32]{0:T(128)} %param.9) | copy-start | bytes 388
  3.5 16.4 %copy-start.1 = (f32[3]{0:T(128)S(1)}, f32[3]{0:T(128)}, u32[]{:S(2)}) copy-start(f32[3]{0:T(128)} %param.10) | copy-start | bytes 40
  3.5 16.4 %copy-start.2 = (f32[3]{0:T(128)S(1)}, f32[3]{0:T(128)}, u32[]{:S(2)}) copy-start(f32[3]{0:T(128)} %param.11) | copy-start | bytes 40
  3.5 5.9 %collective-permute-start.2 = (f32[3,3,4,16,128]{4,3,2,1,0:T(8,128)S(1)}, f32[3,3,4,16,128]{4,3,2,1,0:T(8,128)S(1)}, u32[]{:S(2)}, u32[]{:S(2)}) collective-permute-start(f32[3,3,4,16,128]{4,3,2,1,0:T(8,128)S(1)} %slice.7), channel_id=1, source_target_pairs={{0,1},{1,0},{2,3},{3,2},{4,5},{5,4},{6,7},{7,6},{8,9},{9,8},{10,11... | collective-permute-start | bytes 884744 | tf_op jit(solution)/shard_map/ppermute | solution.py:274
  4.1 1.4 %collective-permute-start = (f32[1,3,4,16,128]{4,3,2,1,0:T(8,128)S(1)}, f32[1,3,4,16,128]{4,3,2,1,0:T(8,128)S(1)}, u32[]{:S(2)}, u32[]{:S(2)}) collective-permute-start(f32[1,3,4,16,128]{4,3,2,1,0:T(8,128)S(1)} %slice.6), channel_id=1, source_target_pairs={{0,1},{1,0},{2,3},{3,2},{4,5},{5,4},{6,7},{7,6},{8,9},{9,8},{10,11... | collective-permute-start | bytes 294920 | tf_op jit(solution)/shard_map/ppermute | solution.py:273
  5.5 7.1 %collective-permute-start.1 = (f32[3,4,16,128]{3,2,1,0:T(8,128)S(1)}, f32[3,4,16,128]{3,2,1,0:T(8,128)S(1)}, u32[]{:S(2)}, u32[]{:S(2)}) collective-permute-start(f32[3,4,16,128]{3,2,1,0:T(8,128)S(1)} %pair.2), channel_id=1, source_target_pairs={{0,6},{1,7},{2,4},{3,5},{4,2},{5,3},{6,0},{7,1},{8,14},{9,15},{10,... | collective-permute-start | bytes 294920 | tf_op jit(solution)/shard_map/ppermute | solution.py:170
  9.5 5.1 %collective-permute-start.3 = (f32[3,4,16,128]{3,2,1,0:T(8,128)S(1)}, f32[3,4,16,128]{3,2,1,0:T(8,128)S(1)}, u32[]{:S(2)}, u32[]{:S(2)}) collective-permute-start(f32[3,4,16,128]{3,2,1,0:T(8,128)S(1)} %get-tuple-element.16), channel_id=1, source_target_pairs={{0,4},{1,5},{2,6},{3,7},{4,0},{5,1},{6,2},{7,3},{8,12},{9,13},{10,... | collective-permute-start | bytes 294920 | tf_op jit(solution)/shard_map/ppermute | solution.py:170
  10.1 4.8 %collective-permute-start.4 = (f32[3,4,16,128]{3,2,1,0:T(8,128)S(1)}, f32[3,4,16,128]{3,2,1,0:T(8,128)S(1)}, u32[]{:S(2)}, u32[]{:S(2)}) collective-permute-start(f32[3,4,16,128]{3,2,1,0:T(8,128)S(1)} %get-tuple-element.17), channel_id=1, source_target_pairs={{0,2},{1,3},{2,0},{3,1},{4,6},{5,7},{6,4},{7,5},{8,10},{9,11},{10,... | collective-permute-start | bytes 294920 | tf_op jit(solution)/shard_map/ppermute | solution.py:170
  15.0 5.7 %collective-permute-start.5 = (f32[3,1,16,128]{3,2,1,0:T(8,128)S(1)}, f32[3,1,16,128]{3,2,1,0:T(8,128)S(1)}, u32[]{:S(2)}, u32[]{:S(2)}) collective-permute-start(f32[3,1,16,128]{3,2,1,0:T(8,128)S(1)} %get-tuple-element.19), channel_id=1, source_target_pairs={{0,16},{1,17},{2,18},{3,19},{4,20},{5,21},{6,22},{7,23},{8,24},{9,... | collective-permute-start | bytes 73736 | tf_op jit(solution)/shard_map/ppermute | solution.py:170
  17.6 4.7 %collective-permute-start.6 = (f32[3,1,16,128]{3,2,1,0:T(8,128)S(1)}, f32[3,1,16,128]{3,2,1,0:T(8,128)S(1)}, u32[]{:S(2)}, u32[]{:S(2)}) collective-permute-start(f32[3,1,16,128]{3,2,1,0:T(8,128)S(1)} %get-tuple-element.20), channel_id=1, source_target_pairs={{0,24},{1,25},{2,26},{3,27},{4,28},{5,29},{6,30},{7,31},{8,16},{9,... | collective-permute-start | bytes 73736 | tf_op jit(solution)/shard_map/ppermute | solution.py:170
  18.9 3.8 %collective-permute-start.7 = (f32[3,1,16,128]{3,2,1,0:T(8,128)S(1)}, f32[3,1,16,128]{3,2,1,0:T(8,128)S(1)}, u32[]{:S(2)}, u32[]{:S(2)}) collective-permute-start(f32[3,1,16,128]{3,2,1,0:T(8,128)S(1)} %get-tuple-element.21), channel_id=1, source_target_pairs={{0,8},{1,9},{2,10},{3,11},{4,12},{5,13},{6,14},{7,15},{8,0},{9,1},... | collective-permute-start | bytes 73736 | tf_op jit(solution)/shard_map/ppermute | solution.py:170

commit v9 on v7

--- a/solution.py
+++ b/solution.py
@@ -141,7 +141,10 @@
 
 
 def step_of(position, hop, count, ring):
-    if ring:
+    if ring == 1:
+        turn = (position ^ position >> 1) + hop & 3
+        return turn ^ turn >> 1
+    if ring == 2:
         turn = ((position & 1) << 1 | position >> 1) + hop & 3
         return (turn & 1) << 1 | turn >> 1
     return position ^ hop
@@ -150,7 +153,7 @@
 def sending_order(count, ring):
     if count < 4:
         return (1,)
-    return (1, 3, 2) if ring else (3, 2, 1)
+    return (2, 1, 3) if ring == 1 else (1, 3, 2)
 
 
 def sent_and_held(pieces, low, ring):
@@ -249,17 +252,17 @@
         totals = jnp.sum(totals, axis=3).reshape(slices, rows)
         nearer = prefix(totals, "xs", lambda early, late: early + late, jnp.zeros_like(totals))
         nearer = nearer[:, :, None]
-    held = sent_and_held(composite_slab(clip_flags, density, nearer, kappa, extinct, depth_n), 0, False)
+    held = sent_and_held(composite_slab(clip_flags, density, nearer, kappa, extinct, depth_n), 0, 0)
     first = order[None]
     vmem = pl.BlockSpec(memory_space=pltpu.VMEM)
-    low, ring = 0, False
+    low, ring = 0, 0
     while True:
         count = len(held)
         through = low + count.bit_length() - 1
         if through == levels:
             break
         fan = 4 if through + 1 < levels else 2
-        next_ring = low > 0 and fan == 4
+        next_ring = 0 if fan < 4 else 1 if low == 0 else 2
         shape = (3, held[0].shape[1] // fan, *held[0].shape[2:])
         pieces = pl.pallas_call(
             functools.partial(merge_kernel, kappa, low, count, ring, next_ring),

time: 23.6 us -> 23.6 us (level)
  waiting for transfers between devices: 8.85 us -> 7.47 us
  starting transfers between devices: 9.24 us -> 10.6 us
    ppermute x7, starting transfers between devices: 9.24 us -> 10.6 us  [sent_and_held(): held.append(lax.ppermute(pieces[hop], 'depth', pairs))]
    ppermute x7, waiting for transfers between devices: 8.85 us -> 7.47 us  [sent_and_held(): held.append(lax.ppermute(pieces[hop], 'depth', pairs))]
where the time goes in v9:
time: 23.6 us; the launch traced here: 23.4 us
  starting transfers between devices  10.6 us (45%)
  waiting for transfers between devices  7.47 us (32%)
  Pallas kernels  4.62 us (20%)
  between operations  0.7 us (3%)
    ppermute x7, starting transfers between devices, sent_and_held(): held.append(lax.ppermute(pieces[hop], 'depth', pairs))  10.6 us
    ppermute x7, waiting for transfers between devices, sent_and_held(): held.append(lax.ppermute(pieces[hop], 'depth', pairs))  7.47 us
    pallas_call x1, Pallas kernels, composite_slab(): pl.pallas_call(functools.partial(slab_kernel, -kappa * log2e, -extinct *...  3.49 us
    pallas_call x1, Pallas kernels, on_device(): pl.pallas_call(functools.partial(finish_kernel, kappa, low, len(held), ri...  0.73 us
  transfers between devices with their start and end apart: 7, of which 7 were waited for; matrix products, arithmetic and copies ran while one was open for 0% of the time, Pallas kernels for 1%

profile of v9, /device:TPU:0, one launch (start us, length us, event | category | flops | bytes accessed | tf_op | source)
XLA Modules:
  0.0 23.4 jit_solution(9657580302067119858)
XLA Ops:
  0.0 0.0 copy-start
  0.0 0.0 copy-start.1
  0.0 0.0 copy-start.2
  0.0 3.5 %slab.1 = (f32[3,16,16,128]{3,2,1,0:T(8,128)S(1)}, f32[3,16,16,128]{3,2,1,0:T(8,128)S(1)}) custom-call(s32[8,4,16]{2,1,0:T(4,128)} %bitcast.11, bf16[16,128,512]{2,1,0:T(8,128)(2,1)} %dens_ref.1), custom_call_target="tpu_custom_call" | custom-call | flops 1073741824 | bytes 2097152 | tf_op jit(solution)/shard_map/slab/pallas_call | solution.py:115
  3.5 0.5 %collective-permute-start = (f32[3,16,16,128]{3,2,1,0:T(8,128)S(1)}, f32[3,16,16,128]{3,2,1,0:T(8,128)S(1)}, u32[]{:S(2)}, u32[]{:S(2)}) collective-permute-start(f32[3,16,16,128]{3,2,1,0:T(8,128)S(1)} %get-tuple-element.15), channel_id=1, source_target_pairs={{0,1},{1,0},{2,3},{3,2},{4,5},{5,4},{6,7},{7,6},{8,9},{9,8},{10,11... | collective-permute-start | bytes 1179656 | tf_op jit(solution)/shard_map/ppermute | solution.py:168
  4.0 1.3 %collective-permute-done.refs_0_ = f32[3,16,16,128]{3,2,1,0:T(8,128)S(1)} collective-permute-done((f32[3,16,16,128]{3,2,1,0:T(8,128)S(1)}, f32[3,16,16,128]{3,2,1,0:T(8,128)S(1)}, u32[]{:S(2)}, u32[]{:S(2)}) %collective-permute-start) | collective-permute-done | bytes 393248 | tf_op jit(solution)/shard_map/ppermute | solution.py:168
  5.4 0.0 copy-done
  5.4 0.1 merge.2
  5.5 3.9 %collective-permute-start.1 = (f32[3,4,16,128]{3,2,1,0:T(8,128)S(1)}, f32[3,4,16,128]{3,2,1,0:T(8,128)S(1)}, u32[]{:S(2)}, u32[]{:S(2)}) collective-permute-start(f32[3,4,16,128]{3,2,1,0:T(8,128)S(1)} %get-tuple-element.17), channel_id=1, source_target_pairs={{0,6},{1,7},{2,4},{3,5},{4,2},{5,3},{6,0},{7,1},{8,14},{9,15},{10,... | collective-permute-start | bytes 294920 | tf_op jit(solution)/shard_map/ppermute | solution.py:168
  9.4 0.5 %collective-permute-start.2 = (f32[3,4,16,128]{3,2,1,0:T(8,128)S(1)}, f32[3,4,16,128]{3,2,1,0:T(8,128)S(1)}, u32[]{:S(2)}, u32[]{:S(2)}) collective-permute-start(f32[3,4,16,128]{3,2,1,0:T(8,128)S(1)} %get-tuple-element.18), channel_id=1, source_target_pairs={{0,2},{1,3},{2,6},{3,7},{4,0},{5,1},{6,4},{7,5},{8,10},{9,11},{10,... | collective-permute-start | bytes 294920 | tf_op jit(solution)/shard_map/ppermute | solution.py:168
  9.9 1.5 %collective-permute-start.3 = (f32[3,4,16,128]{3,2,1,0:T(8,128)S(1)}, f32[3,4,16,128]{3,2,1,0:T(8,128)S(1)}, u32[]{:S(2)}, u32[]{:S(2)}) collective-permute-start(f32[3,4,16,128]{3,2,1,0:T(8,128)S(1)} %get-tuple-element.19), channel_id=1, source_target_pairs={{0,4},{1,5},{2,0},{3,1},{4,6},{5,7},{6,2},{7,3},{8,12},{9,13},{10,... | collective-permute-start | bytes 294920 | tf_op jit(solution)/shard_map/ppermute | solution.py:168
  11.4 1.6 %collective-permute-done.1.refs_0_ = f32[3,4,16,128]{3,2,1,0:T(8,128)S(1)} collective-permute-done((f32[3,4,16,128]{3,2,1,0:T(8,128)S(1)}, f32[3,4,16,128]{3,2,1,0:T(8,128)S(1)}, u32[]{:S(2)}, u32[]{:S(2)}) %collective-permute-start.1) | collective-permute-done | bytes 98336 | tf_op jit(solution)/shard_map/ppermute | solution.py:168
  13.0 1.6 %collective-permute-done.2.refs_1_ = f32[3,4,16,128]{3,2,1,0:T(8,128)S(1)} collective-permute-done((f32[3,4,16,128]{3,2,1,0:T(8,128)S(1)}, f32[3,4,16,128]{3,2,1,0:T(8,128)S(1)}, u32[]{:S(2)}, u32[]{:S(2)}) %collective-permute-start.2) | collective-permute-done | bytes 98336 | tf_op jit(solution)/shard_map/ppermute | solution.py:168
  14.6 0.3 %collective-permute-done.3.refs_2_ = f32[3,4,16,128]{3,2,1,0:T(8,128)S(1)} collective-permute-done((f32[3,4,16,128]{3,2,1,0:T(8,128)S(1)}, f32[3,4,16,128]{3,2,1,0:T(8,128)S(1)}, u32[]{:S(2)}, u32[]{:S(2)}) %collective-permute-start.3) | collective-permute-done | bytes 98336 | tf_op jit(solution)/shard_map/ppermute | solution.py:168
  14.9 0.1 merge.3
  15.0 2.6 %collective-permute-start.4 = (f32[3,1,16,128]{3,2,1,0:T(8,128)S(1)}, f32[3,1,16,128]{3,2,1,0:T(8,128)S(1)}, u32[]{:S(2)}, u32[]{:S(2)}) collective-permute-start(f32[3,1,16,128]{3,2,1,0:T(8,128)S(1)} %get-tuple-element.21), channel_id=1, source_target_pairs={{0,16},{1,17},{2,18},{3,19},{4,20},{5,21},{6,22},{7,23},{8,24},{9,... | collective-permute-start | bytes 73736 | tf_op jit(solution)/shard_map/ppermute | solution.py:168
  17.6 1.2 %collective-permute-start.5 = (f32[3,1,16,128]{3,2,1,0:T(8,128)S(1)}, f32[3,1,16,128]{3,2,1,0:T(8,128)S(1)}, u32[]{:S(2)}, u32[]{:S(2)}) collective-permute-start(f32[3,1,16,128]{3,2,1,0:T(8,128)S(1)} %get-tuple-element.22), channel_id=1, source_target_pairs={{0,24},{1,25},{2,26},{3,27},{4,28},{5,29},{6,30},{7,31},{8,16},{9,... | collective-permute-start | bytes 73736 | tf_op jit(solution)/shard_map/ppermute | solution.py:168
  18.9 0.3 %collective-permute-start.6 = (f32[3,1,16,128]{3,2,1,0:T(8,128)S(1)}, f32[3,1,16,128]{3,2,1,0:T(8,128)S(1)}, u32[]{:S(2)}, u32[]{:S(2)}) collective-permute-start(f32[3,1,16,128]{3,2,1,0:T(8,128)S(1)} %get-tuple-element.23), channel_id=1, source_target_pairs={{0,8},{1,9},{2,10},{3,11},{4,12},{5,13},{6,14},{7,15},{8,0},{9,1},... | collective-permute-start | bytes 73736 | tf_op jit(solution)/shard_map/ppermute | solution.py:168
  19.9 0.0 copy-done.1
  19.9 0.0 copy-done.2
  19.9 0.1 glow.1.glow_ref
  20.0 0.8 %collective-permute-done.4.refs_0_ = f32[3,1,16,128]{3,2,1,0:T(8,128)S(1)} collective-permute-done((f32[3,1,16,128]{3,2,1,0:T(8,128)S(1)}, f32[3,1,16,128]{3,2,1,0:T(8,128)S(1)}, u32[]{:S(2)}, u32[]{:S(2)}) %collective-permute-start.4) | collective-permute-done | bytes 24608 | tf_op jit(solution)/shard_map/ppermute | solution.py:168
  20.8 1.6 %collective-permute-done.5.refs_1_ = f32[3,1,16,128]{3,2,1,0:T(8,128)S(1)} collective-permute-done((f32[3,1,16,128]{3,2,1,0:T(8,128)S(1)}, f32[3,1,16,128]{3,2,1,0:T(8,128)S(1)}, u32[]{:S(2)}, u32[]{:S(2)}) %collective-permute-start.5) | collective-permute-done | bytes 24608 | tf_op jit(solution)/shard_map/ppermute | solution.py:168
  22.4 0.3 %collective-permute-done.6.refs_2_ = f32[3,1,16,128]{3,2,1,0:T(8,128)S(1)} collective-permute-done((f32[3,1,16,128]{3,2,1,0:T(8,128)S(1)}, f32[3,1,16,128]{3,2,1,0:T(8,128)S(1)}, u32[]{:S(2)}, u32[]{:S(2)}) %collective-permute-start.6) | collective-permute-done | bytes 24608 | tf_op jit(solution)/shard_map/ppermute | solution.py:168
  22.7 0.7 %finish.1 = f32[4,4,512]{2,1,0:T(4,128)} custom-call(s32[1,32]{1,0:T(1,128)S(1)} %bitcast.8, f32[2,3,16,128]{3,2,1,0:T(8,128)S(1)} %glow.1.glow_ref, f32[3,1,16,128]{3,2,1,0:T(8,128)S(1)} %collective-permute-done.4.refs_0_, f32[3,1,16,128]{3,2,1,0:T(8,128)S(1)} %collective-permute-done.5.refs_1_, f32[3,1,16,128]{3,2,1,0:T(8,128)S(1)} %collective-permute-done.6.refs_2_, ...), custom_call_target="tpu_custom_call" | custom-call | tf_op jit(solution)/shard_map/finish/pallas_call | solution.py:286
Async XLA Ops:
  0.0 5.4 %copy-start = (s32[32]{0:T(128)S(1)}, s32[32]{0:T(128)}, u32[]{:S(2)}) copy-start(s32[32]{0:T(128)} %param.9) | copy-start | bytes 388
  0.0 19.9 %copy-start.1 = (f32[3]{0:T(128)S(1)}, f32[3]{0:T(128)}, u32[]{:S(2)}) copy-start(f32[3]{0:T(128)} %param.10) | copy-start | bytes 40
  0.0 19.9 %copy-start.2 = (f32[3]{0:T(128)S(1)}, f32[3]{0:T(128)}, u32[]{:S(2)}) copy-start(f32[3]{0:T(128)} %param.11) | copy-start | bytes 40
  3.5 1.9 %collective-permute-start = (f32[3,16,16,128]{3,2,1,0:T(8,128)S(1)}, f32[3,16,16,128]{3,2,1,0:T(8,128)S(1)}, u32[]{:S(2)}, u32[]{:S(2)}) collective-permute-start(f32[3,16,16,128]{3,2,1,0:T(8,128)S(1)} %get-tuple-element.15), channel_id=1, source_target_pairs={{0,1},{1,0},{2,3},{3,2},{4,5},{5,4},{6,7},{7,6},{8,9},{9,8},{10,11... | collective-permute-start | bytes 1179656 | tf_op jit(solution)/shard_map/ppermute | solution.py:168
  5.5 7.5 %collective-permute-start.1 = (f32[3,4,16,128]{3,2,1,0:T(8,128)S(1)}, f32[3,4,16,128]{3,2,1,0:T(8,128)S(1)}, u32[]{:S(2)}, u32[]{:S(2)}) collective-permute-start(f32[3,4,16,128]{3,2,1,0:T(8,128)S(1)} %get-tuple-element.17), channel_id=1, source_target_pairs={{0,6},{1,7},{2,4},{3,5},{4,2},{5,3},{6,0},{7,1},{8,14},{9,15},{10,... | collective-permute-start | bytes 294920 | tf_op jit(solution)/shard_map/ppermute | solution.py:168
  9.4 5.2 %collective-permute-start.2 = (f32[3,4,16,128]{3,2,1,0:T(8,128)S(1)}, f32[3,4,16,128]{3,2,1,0:T(8,128)S(1)}, u32[]{:S(2)}, u32[]{:S(2)}) collective-permute-start(f32[3,4,16,128]{3,2,1,0:T(8,128)S(1)} %get-tuple-element.18), channel_id=1, source_target_pairs={{0,2},{1,3},{2,6},{3,7},{4,0},{5,1},{6,4},{7,5},{8,10},{9,11},{10,... | collective-permute-start | bytes 294920 | tf_op jit(solution)/shard_map/ppermute | solution.py:168
  9.9 4.9 %collective-permute-start.3 = (f32[3,4,16,128]{3,2,1,0:T(8,128)S(1)}, f32[3,4,16,128]{3,2,1,0:T(8,128)S(1)}, u32[]{:S(2)}, u32[]{:S(2)}) collective-permute-start(f32[3,4,16,128]{3,2,1,0:T(8,128)S(1)} %get-tuple-element.19), channel_id=1, source_target_pairs={{0,4},{1,5},{2,0},{3,1},{4,6},{5,7},{6,2},{7,3},{8,12},{9,13},{10,... | collective-permute-start | bytes 294920 | tf_op jit(solution)/shard_map/ppermute | solution.py:168
  15.0 5.8 %collective-permute-start.4 = (f32[3,1,16,128]{3,2,1,0:T(8,128)S(1)}, f32[3,1,16,128]{3,2,1,0:T(8,128)S(1)}, u32[]{:S(2)}, u32[]{:S(2)}) collective-permute-start(f32[3,1,16,128]{3,2,1,0:T(8,128)S(1)} %get-tuple-element.21), channel_id=1, source_target_pairs={{0,16},{1,17},{2,18},{3,19},{4,20},{5,21},{6,22},{7,23},{8,24},{9,... | collective-permute-start | bytes 73736 | tf_op jit(solution)/shard_map/ppermute | solution.py:168
  17.6 4.7 %collective-permute-start.5 = (f32[3,1,16,128]{3,2,1,0:T(8,128)S(1)}, f32[3,1,16,128]{3,2,1,0:T(8,128)S(1)}, u32[]{:S(2)}, u32[]{:S(2)}) collective-permute-start(f32[3,1,16,128]{3,2,1,0:T(8,128)S(1)} %get-tuple-element.22), channel_id=1, source_target_pairs={{0,24},{1,25},{2,26},{3,27},{4,28},{5,29},{6,30},{7,31},{8,16},{9,... | collective-permute-start | bytes 73736 | tf_op jit(solution)/shard_map/ppermute | solution.py:168
  18.9 3.8 %collective-permute-start.6 = (f32[3,1,16,128]{3,2,1,0:T(8,128)S(1)}, f32[3,1,16,128]{3,2,1,0:T(8,128)S(1)}, u32[]{:S(2)}, u32[]{:S(2)}) collective-permute-start(f32[3,1,16,128]{3,2,1,0:T(8,128)S(1)} %get-tuple-element.23), channel_id=1, source_target_pairs={{0,8},{1,9},{2,10},{3,11},{4,12},{5,13},{6,14},{7,15},{8,0},{9,1},... | collective-permute-start | bytes 73736 | tf_op jit(solution)/shard_map/ppermute | solution.py:168

commit v10 on v7

--- a/solution.py
+++ b/solution.py
@@ -36,14 +36,14 @@
     tall = group * band
     shares = band // share_rows
 
-    def copy(step):
-        at = pl.ds(pl.multiple_of(step * tall, tall), tall)
-        return pltpu.make_async_copy(dens_ref.at[:, at, :], dens.at[:, at, :], sems.at[step])
+    def copy(part):
+        at = pl.ds(0, tall) if part == 0 else pl.ds(tall, rows - tall)
+        return pltpu.make_async_copy(dens_ref.at[:, at, :], dens.at[:, at, :], sems.at[part])
 
     flag_copy = pltpu.make_async_copy(flags_hbm, flags, flag_sem)
     flag_copy.start()
-    for step in range(rows // tall):
-        copy(step).start()
+    copy(0).start()
+    copy(1).start()
     upper[...] = (
         lax.broadcasted_iota(jnp.int32, (cells, cells), 0) < lax.broadcasted_iota(jnp.int32, (cells, cells), 1)
     ).astype(jnp.float32).astype(jnp.bfloat16)
@@ -51,7 +51,14 @@
     flag_copy.wait()
 
     def work(step, carry):
-        copy(step).wait()
+        @pl.when(step == 0)
+        def _():
+            copy(0).wait()
+
+        @pl.when(step == 1)
+        def _():
+            copy(1).wait()
+
         for g in range(group):
             block = step * group + g
             at = pl.ds(pl.multiple_of(block * band, band), band)
@@ -123,7 +130,7 @@
             pltpu.VMEM((slices, tall, cells), jnp.float32),
             pltpu.VMEM((cells, cells), jnp.bfloat16),
             pltpu.SMEM((blocks_r, blocks_x, slices), jnp.int32),
-            pltpu.SemaphoreType.DMA((rows // tall,)),
+            pltpu.SemaphoreType.DMA((2,)),
             pltpu.SemaphoreType.DMA,
         ],
         compiler_params=pltpu.CompilerParams(vmem_limit_bytes=24 * 2**20),

time: 23.6 us -> 23.5 us (level)
  no operation moved by 1% of the time
where the time goes in v10:
time: 23.5 us; the launch traced here: 23.4 us
  starting transfers between devices  9.26 us (39%)
  waiting for transfers between devices  8.84 us (38%)
  Pallas kernels  4.56 us (19%)
  between operations  0.7 us (3%)
    ppermute x7, starting transfers between devices, sent_and_held(): held.append(lax.ppermute(pieces[hop], 'depth', pairs))  9.26 us
    ppermute x7, waiting for transfers between devices, sent_and_held(): held.append(lax.ppermute(pieces[hop], 'depth', pairs))  8.84 us
    pallas_call x1, Pallas kernels, composite_slab(): pl.pallas_call(functools.partial(slab_kernel, -kappa * log2e, -extinct *...  3.43 us
    pallas_call x1, Pallas kernels, on_device(): pl.pallas_call(functools.partial(finish_kernel, kappa, low, len(held), ri...  0.73 us
  transfers between devices with their start and end apart: 7, of which 7 were waited for; matrix products, arithmetic and copies ran while one was open for 0% of the time, Pallas kernels for 1%

profile of v10, /device:TPU:0, one launch (start us, length us, event | category | flops | bytes accessed | tf_op | source)
XLA Modules:
  0.0 23.4 jit_solution(7356880511835610594)
XLA Ops:
  0.0 0.0 copy-start
  0.0 0.0 copy-start.1
  0.0 0.0 copy-start.2
  0.0 3.4 %slab.1 = (f32[3,16,16,128]{3,2,1,0:T(8,128)S(1)}, f32[3,16,16,128]{3,2,1,0:T(8,128)S(1)}) custom-call(s32[8,4,16]{2,1,0:T(4,128)} %bitcast.11, bf16[16,128,512]{2,1,0:T(8,128)(2,1)} %dens_ref.1), custom_call_target="tpu_custom_call" | custom-call | flops 1073741824 | bytes 2097152 | tf_op jit(solution)/shard_map/slab/pallas_call | solution.py:122
  3.4 0.5 %collective-permute-start = (f32[3,16,16,128]{3,2,1,0:T(8,128)S(1)}, f32[3,16,16,128]{3,2,1,0:T(8,128)S(1)}, u32[]{:S(2)}, u32[]{:S(2)}) collective-permute-start(f32[3,16,16,128]{3,2,1,0:T(8,128)S(1)} %get-tuple-element.15), channel_id=1, source_target_pairs={{0,1},{1,0},{2,3},{3,2},{4,5},{5,4},{6,7},{7,6},{8,9},{9,8},{10,11... | collective-permute-start | bytes 1179656 | tf_op jit(solution)/shard_map/ppermute | solution.py:172
  4.0 1.3 %collective-permute-done.refs_0_ = f32[3,16,16,128]{3,2,1,0:T(8,128)S(1)} collective-permute-done((f32[3,16,16,128]{3,2,1,0:T(8,128)S(1)}, f32[3,16,16,128]{3,2,1,0:T(8,128)S(1)}, u32[]{:S(2)}, u32[]{:S(2)}) %collective-permute-start) | collective-permute-done | bytes 393248 | tf_op jit(solution)/shard_map/ppermute | solution.py:172
  5.3 0.0 copy-done
  5.3 0.1 merge.2
  5.5 3.9 %collective-permute-start.1 = (f32[3,4,16,128]{3,2,1,0:T(8,128)S(1)}, f32[3,4,16,128]{3,2,1,0:T(8,128)S(1)}, u32[]{:S(2)}, u32[]{:S(2)}) collective-permute-start(f32[3,4,16,128]{3,2,1,0:T(8,128)S(1)} %get-tuple-element.17), channel_id=1, source_target_pairs={{0,6},{1,7},{2,4},{3,5},{4,2},{5,3},{6,0},{7,1},{8,14},{9,15},{10,... | collective-permute-start | bytes 294920 | tf_op jit(solution)/shard_map/ppermute | solution.py:172
  9.3 0.5 %collective-permute-start.2 = (f32[3,4,16,128]{3,2,1,0:T(8,128)S(1)}, f32[3,4,16,128]{3,2,1,0:T(8,128)S(1)}, u32[]{:S(2)}, u32[]{:S(2)}) collective-permute-start(f32[3,4,16,128]{3,2,1,0:T(8,128)S(1)} %get-tuple-element.18), channel_id=1, source_target_pairs={{0,4},{1,5},{2,6},{3,7},{4,0},{5,1},{6,2},{7,3},{8,12},{9,13},{10,... | collective-permute-start | bytes 294920 | tf_op jit(solution)/shard_map/ppermute | solution.py:172
  9.8 0.1 collective-permute-start.3
  10.0 2.6 %collective-permute-done.1.refs_0_ = f32[3,4,16,128]{3,2,1,0:T(8,128)S(1)} collective-permute-done((f32[3,4,16,128]{3,2,1,0:T(8,128)S(1)}, f32[3,4,16,128]{3,2,1,0:T(8,128)S(1)}, u32[]{:S(2)}, u32[]{:S(2)}) %collective-permute-start.1) | collective-permute-done | bytes 98336 | tf_op jit(solution)/shard_map/ppermute | solution.py:172
  12.5 2.0 %collective-permute-done.2.refs_1_ = f32[3,4,16,128]{3,2,1,0:T(8,128)S(1)} collective-permute-done((f32[3,4,16,128]{3,2,1,0:T(8,128)S(1)}, f32[3,4,16,128]{3,2,1,0:T(8,128)S(1)}, u32[]{:S(2)}, u32[]{:S(2)}) %collective-permute-start.2) | collective-permute-done | bytes 98336 | tf_op jit(solution)/shard_map/ppermute | solution.py:172
  14.5 0.3 %collective-permute-done.3.refs_2_ = f32[3,4,16,128]{3,2,1,0:T(8,128)S(1)} collective-permute-done((f32[3,4,16,128]{3,2,1,0:T(8,128)S(1)}, f32[3,4,16,128]{3,2,1,0:T(8,128)S(1)}, u32[]{:S(2)}, u32[]{:S(2)}) %collective-permute-start.3) | collective-permute-done | bytes 98336 | tf_op jit(solution)/shard_map/ppermute | solution.py:172
  14.8 0.1 merge.3
  14.9 2.6 %collective-permute-start.4 = (f32[3,1,16,128]{3,2,1,0:T(8,128)S(1)}, f32[3,1,16,128]{3,2,1,0:T(8,128)S(1)}, u32[]{:S(2)}, u32[]{:S(2)}) collective-permute-start(f32[3,1,16,128]{3,2,1,0:T(8,128)S(1)} %get-tuple-element.21), channel_id=1, source_target_pairs={{0,16},{1,17},{2,18},{3,19},{4,20},{5,21},{6,22},{7,23},{8,24},{9,... | collective-permute-start | bytes 73736 | tf_op jit(solution)/shard_map/ppermute | solution.py:172
  17.6 1.2 %collective-permute-start.5 = (f32[3,1,16,128]{3,2,1,0:T(8,128)S(1)}, f32[3,1,16,128]{3,2,1,0:T(8,128)S(1)}, u32[]{:S(2)}, u32[]{:S(2)}) collective-permute-start(f32[3,1,16,128]{3,2,1,0:T(8,128)S(1)} %get-tuple-element.22), channel_id=1, source_target_pairs={{0,24},{1,25},{2,26},{3,27},{4,28},{5,29},{6,30},{7,31},{8,16},{9,... | collective-permute-start | bytes 73736 | tf_op jit(solution)/shard_map/ppermute | solution.py:172
  18.8 0.3 %collective-permute-start.6 = (f32[3,1,16,128]{3,2,1,0:T(8,128)S(1)}, f32[3,1,16,128]{3,2,1,0:T(8,128)S(1)}, u32[]{:S(2)}, u32[]{:S(2)}) collective-permute-start(f32[3,1,16,128]{3,2,1,0:T(8,128)S(1)} %get-tuple-element.23), channel_id=1, source_target_pairs={{0,8},{1,9},{2,10},{3,11},{4,12},{5,13},{6,14},{7,15},{8,0},{9,1},... | collective-permute-start | bytes 73736 | tf_op jit(solution)/shard_map/ppermute | solution.py:172
  19.8 0.0 copy-done.1
  19.8 0.0 copy-done.2
  19.8 0.1 glow.1.glow_ref
  20.0 0.7 %collective-permute-done.4.refs_0_ = f32[3,1,16,128]{3,2,1,0:T(8,128)S(1)} collective-permute-done((f32[3,1,16,128]{3,2,1,0:T(8,128)S(1)}, f32[3,1,16,128]{3,2,1,0:T(8,128)S(1)}, u32[]{:S(2)}, u32[]{:S(2)}) %collective-permute-start.4) | collective-permute-done | bytes 24608 | tf_op jit(solution)/shard_map/ppermute | solution.py:172
  20.6 1.7 %collective-permute-done.5.refs_1_ = f32[3,1,16,128]{3,2,1,0:T(8,128)S(1)} collective-permute-done((f32[3,1,16,128]{3,2,1,0:T(8,128)S(1)}, f32[3,1,16,128]{3,2,1,0:T(8,128)S(1)}, u32[]{:S(2)}, u32[]{:S(2)}) %collective-permute-start.5) | collective-permute-done | bytes 24608 | tf_op jit(solution)/shard_map/ppermute | solution.py:172
  22.3 0.3 %collective-permute-done.6.refs_2_ = f32[3,1,16,128]{3,2,1,0:T(8,128)S(1)} collective-permute-done((f32[3,1,16,128]{3,2,1,0:T(8,128)S(1)}, f32[3,1,16,128]{3,2,1,0:T(8,128)S(1)}, u32[]{:S(2)}, u32[]{:S(2)}) %collective-permute-start.6) | collective-permute-done | bytes 24608 | tf_op jit(solution)/shard_map/ppermute | solution.py:172
  22.6 0.7 %finish.1 = f32[4,4,512]{2,1,0:T(4,128)} custom-call(s32[1,32]{1,0:T(1,128)S(1)} %bitcast.8, f32[2,3,16,128]{3,2,1,0:T(8,128)S(1)} %glow.1.glow_ref, f32[3,1,16,128]{3,2,1,0:T(8,128)S(1)} %collective-permute-done.4.refs_0_, f32[3,1,16,128]{3,2,1,0:T(8,128)S(1)} %collective-permute-done.5.refs_1_, f32[3,1,16,128]{3,2,1,0:T(8,128)S(1)} %collective-permute-done.6.refs_2_, ...), custom_call_target="tpu_custom_call" | custom-call | tf_op jit(solution)/shard_map/finish/pallas_call | solution.py:290
Async XLA Ops:
  0.0 5.3 %copy-start = (s32[32]{0:T(128)S(1)}, s32[32]{0:T(128)}, u32[]{:S(2)}) copy-start(s32[32]{0:T(128)} %param.9) | copy-start | bytes 388
  0.0 19.8 %copy-start.1 = (f32[3]{0:T(128)S(1)}, f32[3]{0:T(128)}, u32[]{:S(2)}) copy-start(f32[3]{0:T(128)} %param.10) | copy-start | bytes 40
  0.0 19.8 %copy-start.2 = (f32[3]{0:T(128)S(1)}, f32[3]{0:T(128)}, u32[]{:S(2)}) copy-start(f32[3]{0:T(128)} %param.11) | copy-start | bytes 40
  3.4 1.9 %collective-permute-start = (f32[3,16,16,128]{3,2,1,0:T(8,128)S(1)}, f32[3,16,16,128]{3,2,1,0:T(8,128)S(1)}, u32[]{:S(2)}, u32[]{:S(2)}) collective-permute-start(f32[3,16,16,128]{3,2,1,0:T(8,128)S(1)} %get-tuple-element.15), channel_id=1, source_target_pairs={{0,1},{1,0},{2,3},{3,2},{4,5},{5,4},{6,7},{7,6},{8,9},{9,8},{10,11... | collective-permute-start | bytes 1179656 | tf_op jit(solution)/shard_map/ppermute | solution.py:172
  5.5 7.1 %collective-permute-start.1 = (f32[3,4,16,128]{3,2,1,0:T(8,128)S(1)}, f32[3,4,16,128]{3,2,1,0:T(8,128)S(1)}, u32[]{:S(2)}, u32[]{:S(2)}) collective-permute-start(f32[3,4,16,128]{3,2,1,0:T(8,128)S(1)} %get-tuple-element.17), channel_id=1, source_target_pairs={{0,6},{1,7},{2,4},{3,5},{4,2},{5,3},{6,0},{7,1},{8,14},{9,15},{10,... | collective-permute-start | bytes 294920 | tf_op jit(solution)/shard_map/ppermute | solution.py:172
  9.3 5.2 %collective-permute-start.2 = (f32[3,4,16,128]{3,2,1,0:T(8,128)S(1)}, f32[3,4,16,128]{3,2,1,0:T(8,128)S(1)}, u32[]{:S(2)}, u32[]{:S(2)}) collective-permute-start(f32[3,4,16,128]{3,2,1,0:T(8,128)S(1)} %get-tuple-element.18), channel_id=1, source_target_pairs={{0,4},{1,5},{2,6},{3,7},{4,0},{5,1},{6,2},{7,3},{8,12},{9,13},{10,... | collective-permute-start | bytes 294920 | tf_op jit(solution)/shard_map/ppermute | solution.py:172
  9.8 4.9 %collective-permute-start.3 = (f32[3,4,16,128]{3,2,1,0:T(8,128)S(1)}, f32[3,4,16,128]{3,2,1,0:T(8,128)S(1)}, u32[]{:S(2)}, u32[]{:S(2)}) collective-permute-start(f32[3,4,16,128]{3,2,1,0:T(8,128)S(1)} %get-tuple-element.19), channel_id=1, source_target_pairs={{0,2},{1,3},{2,0},{3,1},{4,6},{5,7},{6,4},{7,5},{8,10},{9,11},{10,... | collective-permute-start | bytes 294920 | tf_op jit(solution)/shard_map/ppermute | solution.py:172
  14.9 5.7 %collective-permute-start.4 = (f32[3,1,16,128]{3,2,1,0:T(8,128)S(1)}, f32[3,1,16,128]{3,2,1,0:T(8,128)S(1)}, u32[]{:S(2)}, u32[]{:S(2)}) collective-permute-start(f32[3,1,16,128]{3,2,1,0:T(8,128)S(1)} %get-tuple-element.21), channel_id=1, source_target_pairs={{0,16},{1,17},{2,18},{3,19},{4,20},{5,21},{6,22},{7,23},{8,24},{9,... | collective-permute-start | bytes 73736 | tf_op jit(solution)/shard_map/ppermute | solution.py:172
  17.6 4.7 %collective-permute-start.5 = (f32[3,1,16,128]{3,2,1,0:T(8,128)S(1)}, f32[3,1,16,128]{3,2,1,0:T(8,128)S(1)}, u32[]{:S(2)}, u32[]{:S(2)}) collective-permute-start(f32[3,1,16,128]{3,2,1,0:T(8,128)S(1)} %get-tuple-element.22), channel_id=1, source_target_pairs={{0,24},{1,25},{2,26},{3,27},{4,28},{5,29},{6,30},{7,31},{8,16},{9,... | collective-permute-start | bytes 73736 | tf_op jit(solution)/shard_map/ppermute | solution.py:172
  18.8 3.8 %collective-permute-start.6 = (f32[3,1,16,128]{3,2,1,0:T(8,128)S(1)}, f32[3,1,16,128]{3,2,1,0:T(8,128)S(1)}, u32[]{:S(2)}, u32[]{:S(2)}) collective-permute-start(f32[3,1,16,128]{3,2,1,0:T(8,128)S(1)} %get-tuple-element.23), channel_id=1, source_target_pairs={{0,8},{1,9},{2,10},{3,11},{4,12},{5,13},{6,14},{7,15},{8,0},{9,1},... | collective-permute-start | bytes 73736 | tf_op jit(solution)/shard_map/ppermute | solution.py:172

commit v11 on v10

--- a/solution.py
+++ b/solution.py
@@ -147,10 +147,12 @@
     )
 
 
-def step_of(position, hop, count, ring):
+def step_of(position, hop, count, ring, odd):
     if ring:
         turn = ((position & 1) << 1 | position >> 1) + hop & 3
         return (turn & 1) << 1 | turn >> 1
+    if count == 4 and hop in (1, 2):
+        return position ^ hop ^ 3 * odd
     return position ^ hop
 
 
@@ -168,7 +170,7 @@
         pairs = []
         for source in range(depth_n):
             position = source >> low & (count - 1)
-            pairs.append((source, source + ((step_of(position, hop, count, ring) - position) << low)))
+            pairs.append((source, source + ((step_of(position, hop, count, ring, source & 1) - position) << low)))
         held.append(lax.ppermute(pieces[hop], "depth", pairs))
     return [*held, pieces[0]]
 
@@ -190,7 +192,8 @@
 def places_of(order_ref, low, count, ring):
     mine = lax.axis_index("depth") >> low & (count - 1)
     flips = order_ref[0:1, 0:1] >> low & (count - 1)
-    return [flips ^ step_of(mine, -hop if ring else hop, count, ring) for hop in (*sending_order(count, ring), 0)]
+    odd = lax.axis_index("depth") & 1
+    return [flips ^ step_of(mine, -hop if ring else hop, count, ring, odd) for hop in (*sending_order(count, ring), 0)]
 
 
 def merge_kernel(kappa, low, count, ring, next_ring, order_ref, *refs):
@@ -200,7 +203,7 @@
     mine = lax.axis_index("depth") >> (low + count.bit_length() - 1) & (fan - 1)
     for hop in range(fan):
         for row in range(out[hop].shape[1]):
-            at = row * fan + step_of(mine, hop, fan, next_ring)
+            at = row * fan + step_of(mine, hop, fan, next_ring, lax.axis_index("depth") & 1)
             merged = over(kappa, places, [[piece[channel, at] for channel in range(3)] for piece in held])
             for channel in range(3):
                 out[hop][channel, row] = merged[channel]

time: 23.5 us -> 23.5 us (level)
  no operation moved by 1% of the time
where the time goes in v11:
time: 23.5 us; the launch traced here: 23.4 us
  starting transfers between devices  9.31 us (40%)
  waiting for transfers between devices  8.78 us (37%)
  Pallas kernels  4.56 us (19%)
  between operations  0.7 us (3%)
    ppermute x7, starting transfers between devices, sent_and_held(): held.append(lax.ppermute(pieces[hop], 'depth', pairs))  9.31 us
    ppermute x7, waiting for transfers between devices, sent_and_held(): held.append(lax.ppermute(pieces[hop], 'depth', pairs))  8.78 us
    pallas_call x1, Pallas kernels, composite_slab(): pl.pallas_call(functools.partial(slab_kernel, -kappa * log2e, -extinct *...  3.43 us
    pallas_call x1, Pallas kernels, on_device(): pl.pallas_call(functools.partial(finish_kernel, kappa, low, len(held), ri...  0.73 us
  transfers between devices with their start and end apart: 7, of which 7 were waited for; matrix products, arithmetic and copies ran while one was open for 0% of the time, Pallas kernels for 1%

profile of v11, /device:TPU:0, one launch (start us, length us, event | category | flops | bytes accessed | tf_op | source)
XLA Modules:
  0.0 23.4 jit_solution(14258081781034692189)
XLA Ops:
  0.0 0.0 copy-start
  0.0 0.0 copy-start.1
  0.0 0.0 copy-start.2
  0.0 3.4 %slab.1 = (f32[3,16,16,128]{3,2,1,0:T(8,128)S(1)}, f32[3,16,16,128]{3,2,1,0:T(8,128)S(1)}) custom-call(s32[8,4,16]{2,1,0:T(4,128)} %bitcast.11, bf16[16,128,512]{2,1,0:T(8,128)(2,1)} %dens_ref.1), custom_call_target="tpu_custom_call" | custom-call | flops 1073741824 | bytes 2097152 | tf_op jit(solution)/shard_map/slab/pallas_call | solution.py:122
  3.4 0.5 %collective-permute-start = (f32[3,16,16,128]{3,2,1,0:T(8,128)S(1)}, f32[3,16,16,128]{3,2,1,0:T(8,128)S(1)}, u32[]{:S(2)}, u32[]{:S(2)}) collective-permute-start(f32[3,16,16,128]{3,2,1,0:T(8,128)S(1)} %get-tuple-element.15), channel_id=1, source_target_pairs={{0,1},{1,0},{2,3},{3,2},{4,5},{5,4},{6,7},{7,6},{8,9},{9,8},{10,11... | collective-permute-start | bytes 1179656 | tf_op jit(solution)/shard_map/ppermute | solution.py:174
  4.0 1.3 %collective-permute-done.refs_0_ = f32[3,16,16,128]{3,2,1,0:T(8,128)S(1)} collective-permute-done((f32[3,16,16,128]{3,2,1,0:T(8,128)S(1)}, f32[3,16,16,128]{3,2,1,0:T(8,128)S(1)}, u32[]{:S(2)}, u32[]{:S(2)}) %collective-permute-start) | collective-permute-done | bytes 393248 | tf_op jit(solution)/shard_map/ppermute | solution.py:174
  5.3 0.0 copy-done
  5.3 0.1 merge.2
  5.5 3.9 %collective-permute-start.1 = (f32[3,4,16,128]{3,2,1,0:T(8,128)S(1)}, f32[3,4,16,128]{3,2,1,0:T(8,128)S(1)}, u32[]{:S(2)}, u32[]{:S(2)}) collective-permute-start(f32[3,4,16,128]{3,2,1,0:T(8,128)S(1)} %get-tuple-element.17), channel_id=1, source_target_pairs={{0,6},{1,7},{2,4},{3,5},{4,2},{5,3},{6,0},{7,1},{8,14},{9,15},{10,... | collective-permute-start | bytes 294920 | tf_op jit(solution)/shard_map/ppermute | solution.py:174
  9.3 0.5 %collective-permute-start.2 = (f32[3,4,16,128]{3,2,1,0:T(8,128)S(1)}, f32[3,4,16,128]{3,2,1,0:T(8,128)S(1)}, u32[]{:S(2)}, u32[]{:S(2)}) collective-permute-start(f32[3,4,16,128]{3,2,1,0:T(8,128)S(1)} %get-tuple-element.18), channel_id=1, source_target_pairs={{0,4},{1,3},{2,6},{3,1},{4,0},{5,7},{6,2},{7,5},{8,12},{9,11},{10,... | collective-permute-start | bytes 294920 | tf_op jit(solution)/shard_map/ppermute | solution.py:174
  9.8 0.1 collective-permute-start.3
  10.0 2.9 %collective-permute-done.1.refs_0_ = f32[3,4,16,128]{3,2,1,0:T(8,128)S(1)} collective-permute-done((f32[3,4,16,128]{3,2,1,0:T(8,128)S(1)}, f32[3,4,16,128]{3,2,1,0:T(8,128)S(1)}, u32[]{:S(2)}, u32[]{:S(2)}) %collective-permute-start.1) | collective-permute-done | bytes 98336 | tf_op jit(solution)/shard_map/ppermute | solution.py:174
  12.9 1.7 %collective-permute-done.2.refs_1_ = f32[3,4,16,128]{3,2,1,0:T(8,128)S(1)} collective-permute-done((f32[3,4,16,128]{3,2,1,0:T(8,128)S(1)}, f32[3,4,16,128]{3,2,1,0:T(8,128)S(1)}, u32[]{:S(2)}, u32[]{:S(2)}) %collective-permute-start.2) | collective-permute-done | bytes 98336 | tf_op jit(solution)/shard_map/ppermute | solution.py:174
  14.6 0.2 collective-permute-done.3.refs_2_
  14.8 0.1 merge.3
  14.9 2.7 %collective-permute-start.4 = (f32[3,1,16,128]{3,2,1,0:T(8,128)S(1)}, f32[3,1,16,128]{3,2,1,0:T(8,128)S(1)}, u32[]{:S(2)}, u32[]{:S(2)}) collective-permute-start(f32[3,1,16,128]{3,2,1,0:T(8,128)S(1)} %get-tuple-element.21), channel_id=1, source_target_pairs={{0,16},{1,17},{2,18},{3,19},{4,20},{5,21},{6,22},{7,23},{8,24},{9,... | collective-permute-start | bytes 73736 | tf_op jit(solution)/shard_map/ppermute | solution.py:174
  17.6 1.2 %collective-permute-start.5 = (f32[3,1,16,128]{3,2,1,0:T(8,128)S(1)}, f32[3,1,16,128]{3,2,1,0:T(8,128)S(1)}, u32[]{:S(2)}, u32[]{:S(2)}) collective-permute-start(f32[3,1,16,128]{3,2,1,0:T(8,128)S(1)} %get-tuple-element.22), channel_id=1, source_target_pairs={{0,24},{1,25},{2,26},{3,27},{4,28},{5,29},{6,30},{7,31},{8,16},{9,... | collective-permute-start | bytes 73736 | tf_op jit(solution)/shard_map/ppermute | solution.py:174
  18.8 0.4 %collective-permute-start.6 = (f32[3,1,16,128]{3,2,1,0:T(8,128)S(1)}, f32[3,1,16,128]{3,2,1,0:T(8,128)S(1)}, u32[]{:S(2)}, u32[]{:S(2)}) collective-permute-start(f32[3,1,16,128]{3,2,1,0:T(8,128)S(1)} %get-tuple-element.23), channel_id=1, source_target_pairs={{0,8},{1,9},{2,10},{3,11},{4,12},{5,13},{6,14},{7,15},{8,0},{9,1},... | collective-permute-start | bytes 73736 | tf_op jit(solution)/shard_map/ppermute | solution.py:174
  19.9 0.0 copy-done.1
  19.9 0.0 copy-done.2
  19.9 0.1 glow.1.glow_ref
  20.0 0.6 %collective-permute-done.4.refs_0_ = f32[3,1,16,128]{3,2,1,0:T(8,128)S(1)} collective-permute-done((f32[3,1,16,128]{3,2,1,0:T(8,128)S(1)}, f32[3,1,16,128]{3,2,1,0:T(8,128)S(1)}, u32[]{:S(2)}, u32[]{:S(2)}) %collective-permute-start.4) | collective-permute-done | bytes 24608 | tf_op jit(solution)/shard_map/ppermute | solution.py:174
  20.6 1.7 %collective-permute-done.5.refs_1_ = f32[3,1,16,128]{3,2,1,0:T(8,128)S(1)} collective-permute-done((f32[3,1,16,128]{3,2,1,0:T(8,128)S(1)}, f32[3,1,16,128]{3,2,1,0:T(8,128)S(1)}, u32[]{:S(2)}, u32[]{:S(2)}) %collective-permute-start.5) | collective-permute-done | bytes 24608 | tf_op jit(solution)/shard_map/ppermute | solution.py:174
  22.4 0.3 %collective-permute-done.6.refs_2_ = f32[3,1,16,128]{3,2,1,0:T(8,128)S(1)} collective-permute-done((f32[3,1,16,128]{3,2,1,0:T(8,128)S(1)}, f32[3,1,16,128]{3,2,1,0:T(8,128)S(1)}, u32[]{:S(2)}, u32[]{:S(2)}) %collective-permute-start.6) | collective-permute-done | bytes 24608 | tf_op jit(solution)/shard_map/ppermute | solution.py:174
  22.6 0.7 %finish.1 = f32[4,4,512]{2,1,0:T(4,128)} custom-call(s32[1,32]{1,0:T(1,128)S(1)} %bitcast.8, f32[2,3,16,128]{3,2,1,0:T(8,128)S(1)} %glow.1.glow_ref, f32[3,1,16,128]{3,2,1,0:T(8,128)S(1)} %collective-permute-done.4.refs_0_, f32[3,1,16,128]{3,2,1,0:T(8,128)S(1)} %collective-permute-done.5.refs_1_, f32[3,1,16,128]{3,2,1,0:T(8,128)S(1)} %collective-permute-done.6.refs_2_, ...), custom_call_target="tpu_custom_call" | custom-call | tf_op jit(solution)/shard_map/finish/pallas_call | solution.py:293
Async XLA Ops:
  0.0 5.3 %copy-start = (s32[32]{0:T(128)S(1)}, s32[32]{0:T(128)}, u32[]{:S(2)}) copy-start(s32[32]{0:T(128)} %param.9) | copy-start | bytes 388
  0.0 19.9 %copy-start.1 = (f32[3]{0:T(128)S(1)}, f32[3]{0:T(128)}, u32[]{:S(2)}) copy-start(f32[3]{0:T(128)} %param.10) | copy-start | bytes 40
  0.0 19.9 %copy-start.2 = (f32[3]{0:T(128)S(1)}, f32[3]{0:T(128)}, u32[]{:S(2)}) copy-start(f32[3]{0:T(128)} %param.11) | copy-start | bytes 40
  3.4 1.9 %collective-permute-start = (f32[3,16,16,128]{3,2,1,0:T(8,128)S(1)}, f32[3,16,16,128]{3,2,1,0:T(8,128)S(1)}, u32[]{:S(2)}, u32[]{:S(2)}) collective-permute-start(f32[3,16,16,128]{3,2,1,0:T(8,128)S(1)} %get-tuple-element.15), channel_id=1, source_target_pairs={{0,1},{1,0},{2,3},{3,2},{4,5},{5,4},{6,7},{7,6},{8,9},{9,8},{10,11... | collective-permute-start | bytes 1179656 | tf_op jit(solution)/shard_map/ppermute | solution.py:174
  5.5 7.5 %collective-permute-start.1 = (f32[3,4,16,128]{3,2,1,0:T(8,128)S(1)}, f32[3,4,16,128]{3,2,1,0:T(8,128)S(1)}, u32[]{:S(2)}, u32[]{:S(2)}) collective-permute-start(f32[3,4,16,128]{3,2,1,0:T(8,128)S(1)} %get-tuple-element.17), channel_id=1, source_target_pairs={{0,6},{1,7},{2,4},{3,5},{4,2},{5,3},{6,0},{7,1},{8,14},{9,15},{10,... | collective-permute-start | bytes 294920 | tf_op jit(solution)/shard_map/ppermute | solution.py:174
  9.3 5.3 %collective-permute-start.2 = (f32[3,4,16,128]{3,2,1,0:T(8,128)S(1)}, f32[3,4,16,128]{3,2,1,0:T(8,128)S(1)}, u32[]{:S(2)}, u32[]{:S(2)}) collective-permute-start(f32[3,4,16,128]{3,2,1,0:T(8,128)S(1)} %get-tuple-element.18), channel_id=1, source_target_pairs={{0,4},{1,3},{2,6},{3,1},{4,0},{5,7},{6,2},{7,5},{8,12},{9,11},{10,... | collective-permute-start | bytes 294920 | tf_op jit(solution)/shard_map/ppermute | solution.py:174
  9.8 4.9 %collective-permute-start.3 = (f32[3,4,16,128]{3,2,1,0:T(8,128)S(1)}, f32[3,4,16,128]{3,2,1,0:T(8,128)S(1)}, u32[]{:S(2)}, u32[]{:S(2)}) collective-permute-start(f32[3,4,16,128]{3,2,1,0:T(8,128)S(1)} %get-tuple-element.19), channel_id=1, source_target_pairs={{0,2},{1,5},{2,0},{3,7},{4,6},{5,1},{6,4},{7,3},{8,10},{9,13},{10,... | collective-permute-start | bytes 294920 | tf_op jit(solution)/shard_map/ppermute | solution.py:174
  14.9 5.7 %collective-permute-start.4 = (f32[3,1,16,128]{3,2,1,0:T(8,128)S(1)}, f32[3,1,16,128]{3,2,1,0:T(8,128)S(1)}, u32[]{:S(2)}, u32[]{:S(2)}) collective-permute-start(f32[3,1,16,128]{3,2,1,0:T(8,128)S(1)} %get-tuple-element.21), channel_id=1, source_target_pairs={{0,16},{1,17},{2,18},{3,19},{4,20},{5,21},{6,22},{7,23},{8,24},{9,... | collective-permute-start | bytes 73736 | tf_op jit(solution)/shard_map/ppermute | solution.py:174
  17.6 4.7 %collective-permute-start.5 = (f32[3,1,16,128]{3,2,1,0:T(8,128)S(1)}, f32[3,1,16,128]{3,2,1,0:T(8,128)S(1)}, u32[]{:S(2)}, u32[]{:S(2)}) collective-permute-start(f32[3,1,16,128]{3,2,1,0:T(8,128)S(1)} %get-tuple-element.22), channel_id=1, source_target_pairs={{0,24},{1,25},{2,26},{3,27},{4,28},{5,29},{6,30},{7,31},{8,16},{9,... | collective-permute-start | bytes 73736 | tf_op jit(solution)/shard_map/ppermute | solution.py:174
  18.8 3.8 %collective-permute-start.6 = (f32[3,1,16,128]{3,2,1,0:T(8,128)S(1)}, f32[3,1,16,128]{3,2,1,0:T(8,128)S(1)}, u32[]{:S(2)}, u32[]{:S(2)}) collective-permute-start(f32[3,1,16,128]{3,2,1,0:T(8,128)S(1)} %get-tuple-element.23), channel_id=1, source_target_pairs={{0,8},{1,9},{2,10},{3,11},{4,12},{5,13},{6,14},{7,15},{8,0},{9,1},... | collective-permute-start | bytes 73736 | tf_op jit(solution)/shard_map/ppermute | solution.py:174
